TPU v7x, 32 devices: a whole 2x2x4 slice. The times are simulated.
32 devices in a mesh: dp: 8 (over z, x), fsdp: 4 (over y, core).
Axes of the slice: x: 2, y: 2, z: 4, core: 2. Of those that a mesh axis runs over, the one named last changes fastest.
Arguments:
- inputs: float32 [32768, 768], P(('dp', 'fsdp')), may hold values from -6 to 6
- img_lens: int32 [32, 12], P(('dp', 'fsdp')), may hold values from 1 to 128, 1024 in all within a row
- valid_rows: int32 [32], P(('dp', 'fsdp')), may hold values from 896 to 1024
- w_qkv: float32 [1769472], P(('dp', 'fsdp')), may hold values from -0.21875 to 0.21875
- w_proj: float32 [589824], P(('dp', 'fsdp')), may hold values from -0.625 to 0.625
- w_fc1: float32 [2359296], P(('dp', 'fsdp')), may hold values from -0.21875 to 0.21875
- b_fc1: float32 [3072], P(('dp', 'fsdp')), may hold values from -1.2 to 1.2
- w_fc2: float32 [2359296], P(('dp', 'fsdp')), may hold values from -0.109375 to 0.109375
- vectors: float32 [7680], P(('dp', 'fsdp')), may hold values from -1.2 to 1.6, as said below
- cotangent: float32 [32768, 768], P(('dp', 'fsdp')), may hold values from -6 to 6
Outputs:
- output: float32 [32768, 768], P(('dp', 'fsdp'))
- d_input: float32 [32768, 768], P(('dp', 'fsdp'))
- g_qkv: float32 [1769472], P(('dp', 'fsdp'))
- g_proj: float32 [589824], P(('dp', 'fsdp'))
- g_fc1: float32 [2359296], P(('dp', 'fsdp'))
- g_bfc1: float32 [3072], P(('dp', 'fsdp'))
- g_fc2: float32 [2359296], P(('dp', 'fsdp'))
- g_vectors: float32 [7680], P(('dp', 'fsdp'))
Inputs may be any that keep to these rules, and one draw needn't show every extreme that they name: `img_lens`: each set's 12 lengths sum to 1024, and the largest is exactly 128. `vectors`: norm gains lie near 1, layer scales between 0.5 and 1.5, biases near 0.
All inputs are finite; a program needn't handle non-finite values.
Results may differ from a plain program's by a relative error of at most 0.012.
Values may be sent and summed in bfloat16 or wider, within the bound.
No kernel may reach another device: no remote copies, remote signals or barrier semaphores. Data moves between devices by JAX's collectives and lax.ppermute only.
A program may use at most 320 MiB of HBM per device.

v0:
```python
import functools

import jax
import jax.numpy as jnp
from jax import lax
from jax.experimental import pallas as pl
from jax.experimental.pallas import tpu as pltpu
from jax.sharding import Mesh
from jax.sharding import PartitionSpec as P

HEADS = 12
HD = 64
ROWS = 1024
D = HEADS * HD
FF = 4 * D
PAIRS = HEADS // 2
BLK = 128
WIN = 3 * BLK
NBLK = ROWS // BLK
TILE = 256
EPS = 1e-06
ALL = ("a", "b", "f", "c")
bf16 = jnp.bfloat16
f32 = jnp.float32
VMEM_LIMIT = 60 * 1024 * 1024
ANY = pl.BlockSpec(memory_space=pl.ANY)


def cost(us):
    return pl.CostEstimate(flops=us * 1_100_000_000, bytes_accessed=us * 3_000_000, transcendentals=0)


def dot_nn(left, right):
    return lax.dot_general(left, right, (((1,), (0,)), ((), ())), preferred_element_type=f32)


def dot_nt(left, right):
    return lax.dot_general(left, right, (((1,), (1,)), ((), ())), preferred_element_type=f32)


def dot_tn(left, right):
    return lax.dot_general(left, right, (((0,), (0,)), ((), ())), preferred_element_type=f32)


def eye():
    rows = lax.broadcasted_iota(jnp.int32, (BLK, BLK), 0)
    cols = lax.broadcasted_iota(jnp.int32, (BLK, BLK), 1)
    return (rows == cols).astype(f32).astype(bf16)


def flip(one, block):
    return dot_nt(one, block).astype(bf16)


def norm_parts(values):
    center = values - jnp.mean(values, axis=-1, keepdims=True)
    scale = lax.rsqrt(jnp.mean(center * center, axis=-1, keepdims=True) + EPS)
    return center * scale, scale


def norm_back(grad, normed, scale, gain):
    inner = grad * gain
    first = jnp.mean(inner, axis=-1, keepdims=True)
    second = jnp.mean(inner * normed, axis=-1, keepdims=True)
    return scale * (inner - first - normed * second)


def col_sum(values):
    return jnp.sum(values, axis=0, keepdims=True)


def gelu_parts(u):
    mag = jnp.abs(u) * 0.7071067811865476
    t = 1.0 / (1.0 + 0.3275911 * mag)
    e = jnp.exp(-(mag * mag))
    poly = t * (0.254829592 + t * (-0.284496736 + t * (1.421413741 + t * (-1.453152027 + t * 1.061405429))))
    tail = poly * e
    half = 0.5 * jnp.where(u >= 0, 2.0 - tail, tail)
    return u * half, half + 0.3989422804014327 * u * e


def params(**kw):
    return pltpu.CompilerParams(vmem_limit_bytes=VMEM_LIMIT, **kw)


def whole(shape):
    return pl.BlockSpec(shape, lambda *_: (0,) * len(shape))


def qkv_kernel(*refs):
    parts, refs = refs[:-15], refs[-15:]
    x_ref, turn_ref, vec_ref, _, q_ref, k_ref, v_ref, kt_ref, vt_ref, ht_ref, w_out, w_ref, sems, out_sem, _ = refs
    size = D // len(parts)

    def copies():
        return [
            pltpu.make_async_copy(p.at[:, : 3 * D], w_ref.at[pl.ds(n * size, size)], sems.at[n]) for n, p in enumerate(parts)
        ]

    def keep():
        return pltpu.make_async_copy(w_ref, w_out, out_sem)

    @pl.when(pl.program_id(0) == 0)
    def _():
        for copy in copies():
            copy.start()
        for copy in copies():
            copy.wait()
        keep().start()

    normed, _ = norm_parts(x_ref[...])
    low = dot_nn((normed * vec_ref[0:1] + vec_ref[1:2]).astype(bf16), turn_ref[...]).astype(bf16)
    one = eye()
    q_ref[...] = ((dot_nn(low, w_ref[:, :D]) + vec_ref[2:3]).astype(bf16).astype(f32) * 0.125).astype(bf16)
    k = dot_nn(low, w_ref[:, D : 2 * D]).astype(bf16)
    v = (dot_nn(low, w_ref[:, 2 * D :]) + vec_ref[3:4]).astype(bf16)
    k_ref[...] = k
    v_ref[...] = v
    for p in range(PAIRS):
        s = slice(p * BLK, (p + 1) * BLK)
        kt_ref[s] = flip(one, k[:, s])
        vt_ref[s] = flip(one, v[:, s])
        ht_ref[s] = flip(one, low[:, s])

    @pl.when(pl.program_id(0) == ROWS // TILE - 1)
    def _():
        keep().wait()


def qkv_call(parts, x, turn, vec, token):
    tok = pl.BlockSpec((TILE, D), lambda i: (i, 0))
    feat = pl.BlockSpec((D, TILE), lambda i: (0, i))
    return pl.pallas_call(
        qkv_kernel,
        grid=(ROWS // TILE,),
        in_specs=[ANY] * len(parts) + [tok, whole((D, D)), whole((16, D)), ANY],
        out_specs=[tok, tok, tok, feat, feat, feat, ANY],
        out_shape=[jax.ShapeDtypeStruct((ROWS, D), bf16)] * 3
        + [jax.ShapeDtypeStruct((D, ROWS), bf16)] * 3
        + [jax.ShapeDtypeStruct((D, 3 * D), bf16)],
        scratch_shapes=[
            pltpu.VMEM((D, 3 * D), bf16),
            pltpu.SemaphoreType.DMA((len(parts),)),
            pltpu.SemaphoreType.DMA,
            pltpu.VMEM((8, BLK), f32),
        ],
        compiler_params=params(),
        cost_estimate=cost(14),
        name="norm_qkv",
    )(*parts, x, turn, vec, token)


def fill_segments(lens_ref, valid_ref, segc, segr):
    row_c = lax.broadcasted_iota(jnp.int32, (ROWS, BLK), 0)
    row_r = lax.broadcasted_iota(jnp.int32, (8, ROWS), 1)
    sum_c = jnp.zeros((ROWS, BLK), jnp.int32)
    sum_r = jnp.zeros((8, ROWS), jnp.int32)
    end = jnp.int32(0)
    for j in range(lens_ref.shape[1]):
        end = end + lens_ref[0, j]
        sum_c = sum_c + (row_c >= end).astype(jnp.int32)
        sum_r = sum_r + (row_r >= end).astype(jnp.int32)
    valid = valid_ref[0]
    segc[...] = jnp.where(row_c < valid, sum_c, -1)
    segr[...] = jnp.where(row_r < valid, sum_r, -1)


def block_start(i):
    return pl.multiple_of(jnp.clip(i - 1, 0, NBLK - 3) * BLK, BLK)


def block_bias(segc, segr, i, start):
    keys = segc[pl.ds(start, WIN), :]
    rows = segr[0:1, pl.ds(pl.multiple_of(i * BLK, BLK), BLK)]
    bias = jnp.where(keys == rows, 0.0, -1000000000.0).astype(f32)
    return jnp.concatenate([bias, bias], axis=1)


def lane_masks():
    low = lax.broadcasted_iota(jnp.int32, (1, BLK), 1) < HD
    return low.astype(f32).astype(bf16), (1.0 - low.astype(f32)).astype(bf16)


def stack_pair(block, masks):
    return jnp.concatenate([block * masks[0], block * masks[1]], axis=0)


def attn_kernel(lens_ref, valid_ref, q_ref, k_ref, vt_ref, o_ref, lse_ref, segc, segr):
    i = pl.program_id(0)

    @pl.when(i == 0)
    def _():
        fill_segments(lens_ref, valid_ref, segc, segr)

    start = block_start(i)
    bias = block_bias(segc, segr, i, start)
    masks = lane_masks()
    one = eye()
    for p in range(PAIRS):
        s = slice(p * BLK, (p + 1) * BLK)
        queries = stack_pair(q_ref[:, s], masks)
        scores = dot_nt(k_ref[pl.ds(start, WIN), s], queries) + bias
        peak = jnp.max(scores, axis=0, keepdims=True)
        expo = jnp.exp(scores - peak)
        total = col_sum(expo)
        mixed = dot_nn(vt_ref[s, pl.ds(start, WIN)], expo.astype(bf16)) / total
        flat = jnp.concatenate([mixed[:HD, :BLK], mixed[HD:, BLK:]], axis=0).astype(bf16)
        o_ref[:, s] = flip(one, flat)
        lse_ref[0, p : p + 1] = peak + jnp.log(total)


def attn_call(lens, valid, q, k, vt):
    return pl.pallas_call(
        attn_kernel,
        grid=(NBLK,),
        in_specs=[
            pl.BlockSpec(memory_space=pltpu.SMEM),
            pl.BlockSpec(memory_space=pltpu.SMEM),
            pl.BlockSpec((BLK, D), lambda i: (i, 0)),
            whole((ROWS, D)),
            whole((D, ROWS)),
        ],
        out_specs=[
            pl.BlockSpec((BLK, D), lambda i: (i, 0)),
            pl.BlockSpec((1, 8, 2 * BLK), lambda i: (i, 0, 0)),
        ],
        out_shape=[
            jax.ShapeDtypeStruct((ROWS, D), bf16),
            jax.ShapeDtypeStruct((NBLK, 8, 2 * BLK), f32),
        ],
        scratch_shapes=[pltpu.VMEM((ROWS, BLK), jnp.int32), pltpu.VMEM((8, ROWS), jnp.int32)],
        compiler_params=params(),
        cost_estimate=cost(20),
        name="attend",
    )(lens, valid, q, k, vt)


def proj_kernel(o_ref, w_ref, x_ref, ct_ref, turn_ref, vec_ref, x1_ref, a_ref, h_ref, ht_ref, ot_ref, dz_ref):
    weight = w_ref[...].astype(f32).reshape(D, D).astype(bf16)
    branch = dot_nn(o_ref[...], weight) + vec_ref[4:5]
    inner = x_ref[...] + vec_ref[5:6] * branch
    x1_ref[...] = inner
    a_ref[...] = branch.astype(bf16)
    normed, _ = norm_parts(inner)
    low = (normed * vec_ref[6:7] + vec_ref[7:8]).astype(bf16)
    h_ref[...] = low
    one = eye()
    turned = dot_nn(low, turn_ref[...]).astype(bf16)
    turned_o = dot_nn(o_ref[...], turn_ref[...]).astype(bf16)
    for p in range(PAIRS):
        s = slice(p * BLK, (p + 1) * BLK)
        ht_ref[s] = flip(one, turned[:, s])
        ot_ref[s] = flip(one, turned_o[:, s])
    dz_ref[...] = (vec_ref[9:10] * ct_ref[...]).astype(bf16)


def proj_call(o, mlp, x, ct, turn, vec):
    n, _, _ = mlp.shape
    r = D // n
    tok = pl.BlockSpec((TILE, D), lambda i: (i, 0))
    feat = pl.BlockSpec((D, TILE), lambda i: (0, i))
    return pl.pallas_call(
        proj_kernel,
        grid=(ROWS // TILE,),
        in_specs=[tok, pl.BlockSpec((n, r, D), lambda i: (0, 8, 0)), tok, tok, whole((D, D)), whole((16, D))],
        out_specs=[tok, tok, tok, feat, feat, tok],
        out_shape=[
            jax.ShapeDtypeStruct((ROWS, D), f32),
            jax.ShapeDtypeStruct((ROWS, D), bf16),
            jax.ShapeDtypeStruct((ROWS, D), bf16),
            jax.ShapeDtypeStruct((D, ROWS), bf16),
            jax.ShapeDtypeStruct((D, ROWS), bf16),
            jax.ShapeDtypeStruct((ROWS, D), bf16),
        ],
        compiler_params=params(),
        cost_estimate=cost(11),
        name="proj_norm",
    )(o, mlp, x, ct, turn, vec)


STEPS = FF // D


def up_kernel(me_ref, h_ref, dz_ref, w_ref, b_ref, m_ref, gp_ref, *refs):
    weight = w_ref[...].astype(f32).reshape(D, D).astype(bf16)
    for t in range(ROWS // TILE):
        r = slice(t * TILE, (t + 1) * TILE)
        m, gp = gelu_parts(dot_nn(h_ref[r], weight) + b_ref[...])
        m_ref[r] = m.astype(bf16)
        gp_ref[r] = gp.astype(bf16)
    if len(refs) == 1:
        refs[0][...] = dot_tn(m_ref[...], dz_ref[...]).astype(bf16)
        return
    keep_ref, away_ref, dw_ref = refs
    dw_ref[...] = dot_tn(m_ref[...], dz_ref[...])
    count, _, size, _ = keep_ref.shape
    for k in range(count):
        for c, ref in enumerate((keep_ref, away_ref)):
            row = ((k ^ me_ref[1]) * 2 + (c ^ me_ref[2])) * size
            ref[k, 0] = dw_ref[pl.ds(pl.multiple_of(row, 8), size), :].astype(bf16)


def up_call(me, h, dz, mlp, b, direct):
    n = mlp.shape[0]
    r = D // n
    part = pl.BlockSpec((ROWS, D), lambda j, me: (0, j ^ me[0]))
    if direct:
        grads = (n // (2 * STEPS), STEPS, 4 * r, D)
        spec = pl.BlockSpec((grads[0], 1, 4 * r, D), lambda j, me: (0, j, 0, 0))
        grad_specs, grad_shapes = [spec] * 2, [jax.ShapeDtypeStruct(grads, bf16)] * 2
    else:
        grad_specs = [pl.BlockSpec((D, D), lambda j, me: (j ^ me[0], 0))]
        grad_shapes = [jax.ShapeDtypeStruct((FF, D), bf16)]
    return pl.pallas_call(
        up_kernel,
        grid_spec=pltpu.PrefetchScalarGridSpec(
            num_scalar_prefetch=1,
            grid=(STEPS,),
            in_specs=[
                whole((ROWS, D)),
                whole((ROWS, D)),
                pl.BlockSpec((n, r, D), lambda j, me: (0, 4 + (j ^ me[0]), 0)),
                pl.BlockSpec((1, D), lambda j, me: (0, j ^ me[0])),
            ],
            out_specs=[part, part] + grad_specs,
            scratch_shapes=[pltpu.VMEM((D, D), f32)] if direct else [],
        ),
        out_shape=[jax.ShapeDtypeStruct((ROWS, FF), bf16)] * 2 + grad_shapes,
        compiler_params=params(),
        cost_estimate=cost(25),
        name="mlp_up",
    )(me, h, dz, mlp, b)


def down_kernel(m_ref, gp_ref, dz_ref, ht_ref, w1_ref, w2_ref, x1_ref, ct_ref, a_ref, ot_ref, wp_ref, vec_ref, *refs):
    out_ref, dx_ref, do_ref, keep_ref, away_ref, db1_ref, sums_ref, _, z_acc, dh_acc = refs[-10:]
    j = pl.program_id(0)

    @pl.when(j < STEPS)
    def _():
        w1 = w1_ref[...].astype(f32).reshape(D, D).astype(bf16)
        w2 = w2_ref[...].reshape(D, D)
        z = dot_nn(m_ref[...], w2)
        du = (dot_nt(dz_ref[...], w2) * gp_ref[...].astype(f32)).astype(bf16)
        db1_ref[...] = col_sum(du.astype(f32))
        keep_ref[...] = dot_nn(ht_ref[: D // 2], du).astype(bf16)
        away_ref[...] = dot_nn(ht_ref[D // 2 :], du).astype(bf16)
        dh = dot_nt(du, w1)

        @pl.when(j == 0)
        def _():
            z_acc[...] = z
            dh_acc[...] = dh

        @pl.when(j > 0)
        def _():
            z_acc[...] += z
            dh_acc[...] += dh

    @pl.when(j == STEPS)
    def _():
        wp = wp_ref[...].astype(f32).reshape(D, D).astype(bf16)
        sums = [jnp.zeros((1, D), f32) for _ in range(6)]
        dwp = jnp.zeros((D, D), f32)
        for t in range(ROWS // TILE):
            r = slice(t * TILE, (t + 1) * TILE)
            inner, ct, branch = x1_ref[r], ct_ref[r], z_acc[r] + vec_ref[8:9]
            out_ref[r] = inner + vec_ref[9:10] * branch
            normed, scale = norm_parts(inner)
            dh_t = dh_acc[r]
            dx = ct + norm_back(dh_t, normed, scale, vec_ref[6:7])
            dx_ref[r] = dx
            da = (vec_ref[5:6] * dx).astype(bf16)
            do_ref[r] = dot_nt(da, wp).astype(bf16)
            dwp = dwp + dot_nn(ot_ref[:, r], da)
            adds = (da.astype(f32), dx * a_ref[r].astype(f32), dh_t * normed, dh_t, dz_ref[r].astype(f32), ct * branch)
            sums = [s + col_sum(v) for s, v in zip(sums, adds)]
        keep_ref[...] = dwp[: D // 2].astype(bf16)
        away_ref[...] = dwp[D // 2 :].astype(bf16)
        sums_ref[...] = jnp.concatenate(sums + [jnp.zeros((2, D), f32)], axis=0)


def down_call(m, gp, dz, ht, mlp, x1, ct, a, ot, vec, passed, tokens):
    n = mlp.shape[0]
    r = D // n

    def last(j):
        return jnp.minimum(j, STEPS - 1)

    part = pl.BlockSpec((ROWS, D), lambda j: (0, last(j)))
    grad = pl.BlockSpec((D // 2, D), lambda j: (0, j))
    return pl.pallas_call(
        down_kernel,
        grid=(STEPS + 1,),
        in_specs=[
            part,
            part,
            whole((ROWS, D)),
            whole((D, ROWS)),
            pl.BlockSpec((n, r, D), lambda j: (0, 4 + last(j), 0)),
            pl.BlockSpec((n // 4, 4 * r, D), lambda j: (last(j), 0, 0)),
            whole((ROWS, D)),
            whole((ROWS, D)),
            whole((ROWS, D)),
            whole((D, ROWS)),
            pl.BlockSpec((n, r, D), lambda j: (0, 8, 0)),
            whole((16, D)),
            ANY,
        ]
        + [ANY] * len(tokens),
        out_specs=[
            whole((ROWS, D)),
            whole((ROWS, D)),
            whole((ROWS, D)),
            grad,
            grad,
            pl.BlockSpec((1, D), lambda j: (0, last(j))),
            whole((8, D)),
            ANY,
        ],
        out_shape=[
            jax.ShapeDtypeStruct((ROWS, D), f32),
            jax.ShapeDtypeStruct((ROWS, D), f32),
            jax.ShapeDtypeStruct((ROWS, D), bf16),
            jax.ShapeDtypeStruct((D // 2, FF + D), bf16),
            jax.ShapeDtypeStruct((D // 2, FF + D), bf16),
            jax.ShapeDtypeStruct((1, FF), f32),
            jax.ShapeDtypeStruct((8, D), f32),
            jax.ShapeDtypeStruct(passed.shape, passed.dtype),
        ],
        scratch_shapes=[pltpu.VMEM((ROWS, D), f32), pltpu.VMEM((ROWS, D), f32)],
        input_output_aliases={12: 7},
        compiler_params=params(),
        cost_estimate=cost(40),
        name="mlp_down",
    )(m, gp, dz, ht, mlp, mlp, x1, ct, a, ot, mlp, vec, passed, *tokens)


GROUPS = 1
WIDE = D // GROUPS


def back_kernel(group, passed, lens_ref, valid_ref, q_ref, k_ref, v_ref, do_ref, kt_ref, lse_ref, ht_ref, *refs):
    dq_ref, dk_ref, dv_ref, keep_ref, away_ref, sums_ref = refs[-10 - passed :][:6]
    segc, segr, dk_acc, dv_acc = refs[-4:]
    i = pl.program_id(0)

    @pl.when(i == 0)
    def _():
        fill_segments(lens_ref, valid_ref, segc, segr)
        dk_acc[...] = jnp.zeros_like(dk_acc)
        dv_acc[...] = jnp.zeros_like(dv_acc)

    start = block_start(i)
    here = pl.multiple_of(i * BLK, BLK)
    bias = block_bias(segc, segr, i, start)
    masks = lane_masks()
    one = eye()
    window = pl.ds(start, WIN)
    for p in range(PAIRS // GROUPS):
        s = slice(p * BLK, (p + 1) * BLK)
        n = group * (PAIRS // GROUPS) + p
        queries = stack_pair(q_ref[:, s], masks)
        grads = stack_pair(do_ref[:, s], masks)
        probs = jnp.exp(dot_nt(k_ref[window, s], queries) + bias - lse_ref[0, n : n + 1])
        dprobs = dot_nt(v_ref[window, s], grads)
        dv_acc[window, s] += dot_nn(probs.astype(bf16), grads)
        center = col_sum(probs * dprobs)
        dscores = (probs * (dprobs - center)).astype(bf16)
        dk_acc[window, s] += dot_nn(dscores, queries)
        dq = dot_nn(kt_ref[s, window], dscores)
        dq = (jnp.concatenate([dq[:HD, :BLK], dq[HD:, BLK:]], axis=0) * 0.125).astype(bf16)
        dq_ref[pl.ds(here, BLK), s] = flip(one, dq)

    @pl.when(i == NBLK - 1)
    def _():
        dk_ref[...] = dk_acc[...].astype(bf16)
        dv_ref[...] = dv_acc[...].astype(bf16)
        for c, ref in enumerate((dq_ref, dk_ref, dv_ref)):
            s = slice(c * WIDE, (c + 1) * WIDE)
            away_ref[:, s] = dot_nn(ht_ref[D // 2 :], ref[...]).astype(bf16)
            keep_ref[:, s] = dot_nn(ht_ref[: D // 2], ref[...]).astype(bf16)
        dbq = col_sum(dq_ref[...].astype(f32))
        dbv = col_sum(dv_ref[...].astype(f32))
        sums_ref[...] = jnp.concatenate([dbq, dbv, jnp.zeros((6, WIDE), f32)], axis=0)


def back_call(group, lens, valid, q, k, v, do, kt, lse, ht, before=(), passed=(), tokens=()):
    tok = pl.BlockSpec((BLK, WIDE), lambda i: (i, group))
    full = pl.BlockSpec((ROWS, WIDE), lambda i: (0, group))
    extra = list(before) + list(passed) + list(tokens)
    aliases = {9 + n: n for n in range(len(before))}
    aliases.update({9 + len(before) + n: 6 + n for n in range(len(passed))})
    out = pl.pallas_call(
        functools.partial(back_kernel, group, len(passed)),
        grid=(NBLK,),
        in_specs=[
            pl.BlockSpec(memory_space=pltpu.SMEM),
            pl.BlockSpec(memory_space=pltpu.SMEM),
            tok,
            full,
            full,
            tok,
            pl.BlockSpec((WIDE, ROWS), lambda i: (group, 0)),
            pl.BlockSpec((1, 8, 2 * BLK), lambda i: (i, 0, 0)),
            whole((D, ROWS)),
        ]
        + [ANY] * len(extra),
        out_specs=[full] * 3 + [whole((D // 2, 3 * WIDE))] * 2 + [whole((8, WIDE))] + [ANY] * len(passed),
        out_shape=[jax.ShapeDtypeStruct((ROWS, D), bf16)] * 3
        + [jax.ShapeDtypeStruct((D // 2, 3 * WIDE), bf16)] * 2
        + [jax.ShapeDtypeStruct((8, WIDE), f32)]
        + [jax.ShapeDtypeStruct(p.shape, p.dtype) for p in passed],
        scratch_shapes=[
            pltpu.VMEM((ROWS, BLK), jnp.int32),
            pltpu.VMEM((8, ROWS), jnp.int32),
            pltpu.VMEM((ROWS, WIDE), f32),
            pltpu.VMEM((ROWS, WIDE), f32),
        ],
        input_output_aliases=aliases,
        compiler_params=params(),
        cost_estimate=cost(22),
        name="attend_back",
    )(lens, valid, q, k, v, do, kt, lse, ht, *extra)
    return out[:6], out[6:]


def input_kernel(passed, dq_ref, dk_ref, dv_ref, w_ref, turn_ref, x_ref, dx1_ref, vec_ref, *refs):
    dx_ref, sums_ref = refs[len(refs) - 2 - passed :][:2]
    i = pl.program_id(0)
    dh = dot_nt(dq_ref[...], w_ref[:, :D]) + dot_nt(dk_ref[...], w_ref[:, D : 2 * D]) + dot_nt(dv_ref[...], w_ref[:, 2 * D :])
    dh = dot_nt(dh.astype(bf16), turn_ref[...])
    normed, scale = norm_parts(x_ref[...])
    dx_ref[...] = dx1_ref[...] + norm_back(dh, normed, scale, vec_ref[0:1])
    sums = jnp.concatenate([col_sum(dh * normed), col_sum(dh), jnp.zeros((6, D), f32)], axis=0)

    @pl.when(i == 0)
    def _():
        sums_ref[...] = sums

    @pl.when(i > 0)
    def _():
        sums_ref[...] += sums


def input_call(dq, dk, dv, w, turn, x, dx1, vec, passed=(), tokens=()):
    tok = pl.BlockSpec((TILE, D), lambda i: (i, 0))
    extra = list(passed) + list(tokens)
    out = pl.pallas_call(
        functools.partial(input_kernel, len(passed)),
        grid=(ROWS // TILE,),
        in_specs=[tok, tok, tok, whole((D, 3 * D)), whole((D, D)), tok, tok, whole((16, D))] + [ANY] * len(extra),
        out_specs=[tok, whole((8, D))] + [ANY] * len(passed),
        out_shape=[jax.ShapeDtypeStruct((ROWS, D), f32), jax.ShapeDtypeStruct((8, D), f32)]
        + [jax.ShapeDtypeStruct(p.shape, p.dtype) for p in passed],
        input_output_aliases={8 + n: 2 + n for n in range(len(passed))},
        compiler_params=params(),
        cost_estimate=cost(13),
        name="input_back",
    )(dq, dk, dv, w, turn, x, dx1, vec, *extra)
    return out[:2], out[2:]


def swap_cores(x):
    return lax.ppermute(x, "c", [(0, 1), (1, 0)])


def from_peer(x, axes, k):
    return lax.ppermute(x, axes, [(i, i ^ k) for i in range(lax.axis_size(axes))])


def gate_kernel(*refs):
    del refs


def gate(array, tokens):
    return pl.pallas_call(
        gate_kernel,
        in_specs=[ANY] * (1 + len(tokens)),
        out_specs=ANY,
        out_shape=jax.ShapeDtypeStruct(array.shape, array.dtype),
        input_output_aliases={0: 0},
        name="gate",
    )(array, *tokens)


def own_order(rows):
    place = jnp.arange(D, dtype=jnp.int32)
    k, rest = place % rows, place // rows
    na, nb, nf = lax.axis_size("a"), lax.axis_size("b"), lax.axis_size("f")
    a, rest = rest % na ^ lax.axis_index("a"), rest // na
    f, rest = rest % nf ^ lax.axis_index("f"), rest // nf
    b, c = rest % nb ^ lax.axis_index("b"), rest // nb ^ lax.axis_index("c")
    return (((a * nb + b) * nf + f) * 2 + c) * rows + k


def gather_own(shard):
    stack = jnp.concatenate([shard] + [from_peer(shard, "a", k) for k in range(1, lax.axis_size("a"))], axis=0)
    parts = [stack] + [from_peer(stack, ("b", "f"), k) for k in range(1, lax.axis_size(("b", "f")))]
    if stack.shape[0] % 16:
        parts = [jnp.concatenate(parts, axis=0)]
    return parts + [swap_cores(p) for p in parts]


def add(terms):
    total = 0.0
    for array, low, high in terms:
        total = total + array[low:high].astype(f32)
    return total


def plain(arrays):
    return [(g, 0, g.shape[0]) for g in arrays]


def exchange(terms, axes):
    count = lax.axis_size(axes)
    size = (terms[0][2] - terms[0][1]) // count

    def block(k):
        return [(t, low + k * size, low + (k + 1) * size) for t, low, _ in terms]

    return block(0), [from_peer(add(block(k)).astype(bf16), axes, k) for k in range(1, count)]


def hold(terms, array):
    return [(array,) + terms[0][1:]] + terms[1:]


def scatter_own(keep, away):
    terms = plain([keep, swap_cores(away)])
    for axes in (("b", "f"), "a"):
        terms, got = exchange(terms, axes)
        terms = terms + plain(got)
    return add(terms)


def join_owners(mlp, rows):
    group = 1 if rows % 8 == 0 else 8
    if group == 1:
        return mlp
    count = mlp.shape[0] // group
    tall = mlp[:, : 4 * rows].reshape(count, group * 4 * rows, D)
    wide = mlp[:, 4 * rows : 8 * rows].reshape(count, group, 4, rows, D)
    wide = jnp.swapaxes(wide, 1, 2).reshape(count, group * 4 * rows, D)
    proj = mlp[:, 8 * rows :].reshape(count, group * rows, D)
    return jnp.concatenate([tall, wide, proj], axis=1)


def shards(inputs, img_lens, valid_rows, w_qkv, w_proj, w_fc1, b_fc1, w_fc2, vectors, cotangent):
    devices = lax.axis_size(ALL)
    rows = D // devices
    slots = rows * BLK
    small = jnp.concatenate([vectors, b_fc1])
    small = jnp.pad(small, (0, slots - small.shape[0])).reshape(rows, BLK)
    head = jnp.concatenate([w_qkv.reshape(rows, 3 * D), small], axis=1).astype(bf16)
    fc1_shard = jnp.swapaxes(w_fc1.reshape(rows, 4, D), 0, 1).reshape(4 * rows, D)
    mlp = jnp.concatenate([w_fc2.reshape(4 * rows, D), fc1_shard, w_proj.reshape(rows, D)], axis=0).astype(bf16)
    mlp = join_owners(lax.all_gather(mlp, ALL, axis=0), rows)

    order = own_order(rows)
    turn = (jnp.arange(D, dtype=jnp.int32)[:, None] == order[None, :]).astype(bf16)
    parts = gather_own(head)
    small = jnp.concatenate([p[:, 3 * D :] for p in parts], axis=0)
    small = jnp.dot(turn, small, preferred_element_type=f32).reshape(devices, slots)
    nvec = vectors.shape[0]
    vec = jnp.pad(small[:, :nvec].reshape(10, D), ((0, 6), (0, 0)))
    b1 = small[:, nvec : nvec + b_fc1.shape[0]].reshape(1, FF)

    q, k, v, kt, vt, h1t, wqkv = qkv_call(parts, inputs, turn, vec, order)
    o, lse = attn_call(img_lens, valid_rows, q, k, vt)
    x1, a, h2, h2t, ot, dz = proj_call(o, mlp, inputs, cotangent, turn, vec)
    na, nb, nf = lax.axis_size("a"), lax.axis_size("b"), lax.axis_size("f")
    direct = na == STEPS and rows % 8 == 0
    zero = jnp.zeros((), jnp.int32)
    me = jnp.stack(
        [lax.axis_index("a") if direct else zero, lax.axis_index(("b", "f")), lax.axis_index("c")]
    ).astype(jnp.int32)
    m, gp, *dw2 = up_call(me, h2, dz, mlp, b1, direct)
    if direct:
        keep2, away2 = [g.reshape(FF // 2, D) for g in dw2]
    else:
        dw2 = jnp.take(dw2[0].reshape(devices, 4 * rows, D), order[::rows] // rows, axis=0).reshape(FF, D)
        keep2, away2 = dw2[: FF // 2], dw2[FF // 2 :]

    bf = ("b", "f")
    core2 = swap_cores(away2)
    up2, up2_got = exchange(plain([keep2, core2]), bf)
    result, dx1, do, keep, away, db1, sums2, keep2 = down_call(
        m, gp, dz, h2t, mlp, x1, cotangent, a, ot, vec, passed=keep2, tokens=[core2]
    )
    core = swap_cores(gate(away, up2_got))
    up2, up2_last = exchange(hold(up2, keep2) + plain(up2_got), "a")
    mid, mid_got = exchange(plain([keep, core]), bf)

    (dq, dk, dv, keep1, away1, sums_a), (keep, keep2) = back_call(
        0, img_lens, valid_rows, q, k, v, do, kt, lse, h1t, passed=[keep, keep2], tokens=[core]
    )
    core1 = swap_cores(gate(away1, mid_got + up2_last))
    g_fc2 = add(hold(up2, keep2) + plain(up2_last))
    mid, mid_last = exchange(hold(mid, keep) + plain(mid_got), "a")
    second, second_got = exchange(plain([keep1, core1]), bf)

    (d_input, sums0), (keep, keep1) = input_call(
        dq, dk, dv, wqkv, turn, inputs, dx1, vec, passed=[keep, keep1], tokens=[core1]
    )
    sums0 = gate(sums0, second_got + mid_last)
    second, second_last = exchange(hold(second, keep1) + plain(second_got), "a")
    gvec = jnp.concatenate([sums0[:2], sums_a[:2], sums2[:6]], axis=0).reshape(devices, nvec)
    gsmall = jnp.concatenate([gvec, db1.reshape(devices, b_fc1.shape[0])], axis=1)
    gsmall = jnp.pad(gsmall, ((0, 0), (0, -gsmall.shape[1] % BLK))).astype(bf16)
    pick = (order[::rows] // rows)[:, None] == jnp.arange(devices, dtype=jnp.int32)[None, :]
    gsmall = jnp.dot(pick.astype(bf16), gsmall, preferred_element_type=f32).astype(bf16)
    gsmall = scatter_own(gsmall[: devices // 2], gsmall[devices // 2 :]).reshape(-1)

    g_mid = add(hold(mid, keep) + plain(mid_last))
    g_fc1, g_proj = g_mid[:, :FF], g_mid[:, FF:]
    g_qkv = add(second + plain(second_last))
    return (
        result,
        d_input,
        g_qkv.reshape(-1),
        g_proj.reshape(-1),
        g_fc1.reshape(-1),
        gsmall[nvec : nvec + b_fc1.shape[0]],
        g_fc2.reshape(-1),
        gsmall[:nvec],
    )


def solution(mesh):
    dp, fsdp = mesh.shape["dp"], mesh.shape["fsdp"]
    fine = Mesh(mesh.devices.reshape(dp // 2, 2, fsdp // 2, 2), ALL)
    rows, flat = P(ALL, None), P(ALL)
    return jax.shard_map(
        shards,
        mesh=fine,
        in_specs=(rows, rows, flat, flat, flat, flat, flat, flat, flat, rows),
        out_specs=(rows, rows, flat, flat, flat, flat, flat, flat),
        check_vma=False,
    )
```

profile of v0, /device:TPU:0, one launch (start us, length us, event | category | flops | bytes accessed | tf_op | source)
XLA Modules:
  0.0 325.7 jit_solution(16186048127049702443)
XLA Ops:
  7.2 1.0 convert.56
  8.3 1.0 convert.55
  9.3 1.0 convert.54
  10.5 0.7 pad_maximum_fusion.1
  11.5 5.1 %collective-permute-start.2 = (bf16[24,2432]{1,0:T(8,128)(2,1)S(1)}, bf16[24,2432]{1,0:T(8,128)(2,1)S(1)}, u32[]{:S(2)}, u32[]{:S(2)}) collective-permute-start(bf16[24,2432]{1,0:T(8,128)(2,1)S(1)} %pad_maximum_fusion.2), channel_id=1, source_target_pairs={{0,24},{8,16},{16,8},{24,0},{1,25},{9,17},{17,9},{25,1},{2,26},{10... | collective-permute-start | bytes 350216 | tf_op jit(solution)/shard_map/ppermute | solution.py:569
  18.6 2.2 collective-permute-done.2
  20.8 5.8 %collective-permute-done.1 = bf16[24,2432]{1,0:T(8,128)(2,1)S(1)} collective-permute-done((bf16[24,2432]{1,0:T(8,128)(2,1)S(1)}, bf16[24,2432]{1,0:T(8,128)(2,1)S(1)}, u32[]{:S(2)}, u32[]{:S(2)}) %collective-permute-start.1) | collective-permute-done | bytes 116768 | tf_op jit(solution)/shard_map/ppermute | solution.py:569
  26.7 2.5 collective-permute-start.5
  30.2 1.5 fusion.1.refs_9_.turn_ref
  31.7 9.6 %collective-permute-done.5.refs_3_ = bf16[96,2432]{1,0:T(8,128)(2,1)S(1)} collective-permute-done((bf16[96,2432]{1,0:T(8,128)(2,1)S(1)}, bf16[96,2432]{1,0:T(8,128)(2,1)S(1)}, u32[]{:S(2)}, u32[]{:S(2)}) %collective-permute-start.5) | collective-permute-done | bytes 466976 | tf_op jit(solution)/shard_map/ppermute | solution.py:569
  41.3 8.1 %collective-permute-done.4.refs_2_ = bf16[96,2432]{1,0:T(8,128)(2,1)S(1)} collective-permute-done((bf16[96,2432]{1,0:T(8,128)(2,1)S(1)}, bf16[96,2432]{1,0:T(8,128)(2,1)S(1)}, u32[]{:S(2)}, u32[]{:S(2)}) %collective-permute-start.4) | collective-permute-done | bytes 466976 | tf_op jit(solution)/shard_map/ppermute | solution.py:569
  50.0 1.9 collective-permute-done.7.refs_5_
  51.9 0.8 copy-done.40
  52.8 0.8 copy-done.38
  55.7 13.6 %norm_qkv.1 = (bf16[1024,768]{1,0:T(8,128)(2,1)}, bf16[1024,768]{1,0:T(8,128)(2,1)}, bf16[1024,768]{1,0:T(8,128)(2,1)}, bf16[768,1024]{1,0:T(8,128)(2,1)}, bf16[...) custom-call(bf16[96,2432]{1,0:T(8,128)(2,1)} %copy-done.28, ...), custom_call_target="tpu_custom_call" | custom-call | flops 15399999488 | bytes 42000000 | tf_op jit(solution)/shard_map/norm_qkv/pallas_call | solution.py:133
  69.3 18.8 %attend.1 = (bf16[1024,768]{1,0:T(8,128)(2,1)}, f32[8,8,256]{2,1,0:T(8,128)}) custom-call(s32[1,12]{1,0:T(1,128)} %lens_ref.3, s32[1]{0:T(128)S(6)} %copy.44.valid_ref, bf16[1024,768]{1,0:T(8,128)(2,1)} %get-tuple-element.47.q_ref, bf16[1024,768]{1,0:T(8,128)(2,1)} %get-tuple-element.48.k_ref, bf16[768,1024]{1,0:T(8,128)(2,1)} %get-tuple-element.49.vt_ref), custom_call_target="tpu_custom_call" | custom-call | flops 22000001024 | bytes 60000000 | tf_op jit(solution)/shard_map/attend/pallas_call | solution.py:213
  88.1 20.8 %all-gather.2.cloned.1.call-done.w_ref.w1_ref.w2_ref.wp_ref = bf16[32,216,768]{2,1,0:T(8,128)(2,1)} async-done(((bf16[1,216,768]{2,1,0:T(8,128)(2,1)}), bf16[32,216,768]{2,1,0:T(8,128)(2,1)}) %all-gather.2.cloned.1.call-update) | async-done | bytes 10616848 | tf_op jit(solution)/shard_map/all_gather | solution.py:659
  108.9 11.4 %proj_norm.1 = (f32[1024,768]{1,0:T(8,128)}, bf16[1024,768]{1,0:T(8,128)(2,1)}, bf16[1024,768]{1,0:T(8,128)(2,1)}, bf16[768,1024]{1,0:T(8,128)(2,1)}, bf16[768,1...) custom-call(bf16[1024,768]{1,0:T(8,128)(2,1)} %get-tuple-element.50.o_ref, ...), custom_call_target="tpu_custom_call" | custom-call | flops 12099999744 | bytes 33000000 | tf_op jit(solution)/shard_map/proj_norm/pallas_call | solution.py:262
  120.3 24.9 %mlp_up.1 = (bf16[1024,3072]{1,0:T(8,128)(2,1)}, bf16[1024,3072]{1,0:T(8,128)(2,1)}, bf16[4,4,96,768]{3,2,1,0:T(8,128)(2,1)}, bf16[4,4,96,768]{3,2,1,0:T(8,128)(2,1)}) custom-call(s32[3]{0:T(128)} %pad_add_fusion.me_ref, bf16[1024,768]{1,0:T(8,128)(2,1)} %get-tuple-element.51.h_ref, bf16[1024,768]{1,0:T(8,128)(2,1)} %get-tuple-element.52.dz_ref, ...), custom_call_target="tpu_custom_call" | custom-call | flops 27499999232 | bytes 75000000 | tf_op jit(solution)/shard_map/mlp_up/pallas_call | solution.py:314
  145.4 1.5 fusion.71
  147.0 3.0 collective-permute-done.10.refs_1_
  149.9 1.8 fusion.2
  151.7 1.4 collective-permute-start.13
  153.1 1.6 collective-permute-start.12
  155.2 39.9 %mlp_down.1 = (f32[1024,768]{1,0:T(8,128)}, f32[1024,768]{1,0:T(8,128)}, bf16[1024,768]{1,0:T(8,128)(2,1)}, bf16[384,3840]{1,0:T(8,128)(2,1)}, bf16[384,3840]{1,...) custom-call(bf16[1024,3072]{1,0:T(8,128)(2,1)} %get-tuple-element.53, ...), custom_call_target="tpu_custom_call", output_to_operand_aliasing={{7}: (12, {})} | custom-call | flops 44000002048 | bytes 120000000 | tf_op jit(solution)/shard_map/mlp_down/pallas_call | solution.py:392
  195.1 0.8 copy-done.9
  196.0 0.8 copy-done.10
  196.8 2.1 add_convert_fusion.9
  198.9 2.1 collective-permute-start.20
  201.0 0.8 collective-permute-start.19
  201.8 1.5 collective-permute-start.18
  203.4 2.1 add_convert_fusion
  205.6 1.4 collective-permute-start.17
  207.1 1.6 collective-permute-start.16
  209.1 38.9 %attend_back.1 = (bf16[1024,768]{1,0:T(8,128)(2,1)}, bf16[1024,768]{1,0:T(8,128)(2,1)}, bf16[1024,768]{1,0:T(8,128)(2,1)}, bf16[384,2304]{1,0:T(8,128)(2,1)}, bf...) custom-call(s32[1,12]{1,0:T(1,128)} %lens_ref.3, ...), custom_call_target="tpu_custom_call", output_to_operand_aliasing={{6}: (9, {}), {7}: (10, {})} | custom-call | flops 24199999488 | bytes 66000000 | tf_op jit(solution)/shard_map/attend_back/pallas_call | solution.py:494
  249.6 0.9 slice.474
  251.3 1.5 convert_add_fusion.4
  252.7 0.7 reshape.247
  253.5 0.9 slice.814
  254.4 2.5 add_convert_fusion.8
  256.8 5.7 %collective-permute-start.28 = (bf16[24,3840]{1,0:T(8,128)(2,1)S(1)}, bf16[24,3840]{1,0:T(8,128)(2,1)S(1)}, u32[]{:S(2)}, u32[]{:S(2)}) collective-permute-start(bf16[24,3840]{1,0:T(8,128)(2,1)S(1)} %get-tuple-element.86), channel_id=1, source_target_pairs={{0,8},{8,0},{16,24},{24,16},{1,9},{9,1},{17,25},{25,17},{2,10},{10... | collective-permute-start | bytes 552968 | tf_op jit(solution)/shard_map/ppermute | solution.py:569
  262.5 2.0 collective-permute-start.30
  264.5 1.6 add_convert_fusion.5
  266.7 1.5 collective-permute-start.24
  268.3 1.4 collective-permute-start.23
  269.6 13.1 %input_back.1 = (f32[1024,768]{1,0:T(8,128)}, f32[8,768]{1,0:T(8,128)}, bf16[384,3840]{1,0:T(8,128)(2,1)}, bf16[384,2304]{1,0:T(8,128)(2,1)}) custom-call(bf16[1024,768]{1,0:T(8,128)(2,1)} %get-tuple-element.70.dq_ref, bf16[1024,768]{1,0:T(8,128)(2,1)} %get-tuple-element.71.dk_ref, ...), custom_call_target="tpu_custom_call", output_to_operand_aliasing={{2}: (8, {}), {3}: (9, {})} | custom-call | flops 14300000256 | bytes 39000000 | tf_op jit(solution)/shard_map/input_back/pallas_call | solution.py:549
  282.8 4.9 %collective-permute-done.22.refs_1_ = bf16[96,2304]{1,0:T(8,128)(2,1)S(1)} collective-permute-done((bf16[96,2304]{1,0:T(8,128)(2,1)}, bf16[96,2304]{1,0:T(8,128)(2,1)S(1)}, u32[]{:S(2)}, u32[]{:S(2)}) %collective-permute-start.22) | collective-permute-done | bytes 442400 | tf_op jit(solution)/shard_map/ppermute | solution.py:569
  287.7 1.2 collective-permute-done.23.refs_2_
  288.9 0.7 copy-done.17
  289.7 0.8 slice.815
  291.0 1.3 convert_add_fusion.3
  293.0 1.5 collective-permute-start.34
  294.5 1.4 collective-permute-start.33
  295.9 0.8 copy.28
  298.1 2.2 collective-permute-start.35
  300.3 2.0 collective-permute-start.37
  302.3 1.4 add_convert_fusion.14
  303.7 2.5 collective-permute-start.25
  306.2 2.0 collective-permute-start.27
  309.3 0.8 collective-permute-done.25
  310.2 2.8 collective-permute-done.27
  313.0 3.6 %collective-permute-done.26 = bf16[24,2304]{1,0:T(8,128)(2,1)S(1)} collective-permute-done((bf16[24,2304]{1,0:T(8,128)(2,1)S(1)}, bf16[24,2304]{1,0:T(8,128)(2,1)S(1)}, u32[]{:S(2)}, u32[]{:S(2)}) %collective-permute-start.26) | collective-permute-done | bytes 110624 | tf_op jit(solution)/shard_map/ppermute | solution.py:569
  316.6 1.1 convert_add_fusion.5
  317.7 0.7 reshape.242
  (176 shorter events, 13.8 us)
Async XLA Ops:
  7.2 4.1 %copy-start.42 = (f32[96]{0:T(128)S(1)}, f32[96]{0:T(128)}, u32[]{:S(2)}) copy-start(f32[96]{0:T(128)} %param.16) | copy-start | bytes 1156
  7.2 4.1 %copy-start.41 = (f32[240]{0:T(256)S(1)}, f32[240]{0:T(256)}, u32[]{:S(2)}) copy-start(f32[240]{0:T(256)} %param.18) | copy-start | bytes 2884
  7.2 4.1 %copy-start.29 = (f32[55296]{0:T(1024)S(1)}, f32[55296]{0:T(1024)}, u32[]{:S(2)}) copy-start(f32[55296]{0:T(1024)} %param.13) | copy-start | bytes 663556
  7.2 101.7 %all-gather.2.cloned.1.call-start = ((), (), s32[]{:S(2)}) async-start(), calls=%async_computation | async-start | bytes 10948608 | tf_op jit(solution)/shard_map/all_gather | solution.py:659
  11.5 9.2 %collective-permute-start.2 = (bf16[24,2432]{1,0:T(8,128)(2,1)S(1)}, bf16[24,2432]{1,0:T(8,128)(2,1)S(1)}, u32[]{:S(2)}, u32[]{:S(2)}) collective-permute-start(bf16[24,2432]{1,0:T(8,128)(2,1)S(1)} %pad_maximum_fusion.2), channel_id=1, source_target_pairs={{0,24},{8,16},{16,8},{24,0},{1,25},{9,17},{17,9},{25,1},{2,26},{10... | collective-permute-start | bytes 350216 | tf_op jit(solution)/shard_map/ppermute | solution.py:569
  16.7 9.9 %collective-permute-start.1 = (bf16[24,2432]{1,0:T(8,128)(2,1)S(1)}, bf16[24,2432]{1,0:T(8,128)(2,1)S(1)}, u32[]{:S(2)}, u32[]{:S(2)}) collective-permute-start(bf16[24,2432]{1,0:T(8,128)(2,1)S(1)} %pad_maximum_fusion.2), channel_id=1, source_target_pairs={{0,16},{8,24},{16,0},{24,8},{1,17},{9,25},{17,1},{25,9},{2,18},{10... | collective-permute-start | bytes 350216 | tf_op jit(solution)/shard_map/ppermute | solution.py:569
  16.7 9.9 %collective-permute-start = (bf16[24,2432]{1,0:T(8,128)(2,1)S(1)}, bf16[24,2432]{1,0:T(8,128)(2,1)S(1)}, u32[]{:S(2)}, u32[]{:S(2)}) collective-permute-start(bf16[24,2432]{1,0:T(8,128)(2,1)S(1)} %pad_maximum_fusion.2), channel_id=1, source_target_pairs={{0,8},{8,0},{16,24},{24,16},{1,9},{9,1},{17,25},{25,17},{2,10},{10... | collective-permute-start | bytes 350216 | tf_op jit(solution)/shard_map/ppermute | solution.py:569
  18.6 35.5 %copy-start.30 = (s32[768]{0:T(1024)}, s32[768]{0:T(1024)S(1)}, u32[]{:S(2)}) copy-start(s32[768]{0:T(1024)S(1)} %fusion.34.refs_11_) | copy-start | bytes 9220
  26.6 27.6 %copy-start.28 = (bf16[96,2432]{1,0:T(8,128)(2,1)}, bf16[96,2432]{1,0:T(8,128)(2,1)S(1)}, u32[]{:S(2)}) copy-start(bf16[96,2432]{1,0:T(8,128)(2,1)S(1)} %pad_maximum_fusion.refs_0_) | copy-start | bytes 1400836
  26.7 14.6 %collective-permute-start.5 = (bf16[96,2432]{1,0:T(8,128)(2,1)S(1)}, bf16[96,2432]{1,0:T(8,128)(2,1)S(1)}, u32[]{:S(2)}, u32[]{:S(2)}) collective-permute-start(bf16[96,2432]{1,0:T(8,128)(2,1)S(1)} %pad_maximum_fusion.refs_0_), channel_id=1, source_target_pairs={{0,6},{2,4},{4,2},{6,0},{1,7},{3,5},{5,3},{7,1},{8,14},{10,12},{12... | collective-permute-start | bytes 1400840 | tf_op jit(solution)/shard_map/ppermute | solution.py:569
  29.2 20.2 %collective-permute-start.4 = (bf16[96,2432]{1,0:T(8,128)(2,1)S(1)}, bf16[96,2432]{1,0:T(8,128)(2,1)S(1)}, u32[]{:S(2)}, u32[]{:S(2)}) collective-permute-start(bf16[96,2432]{1,0:T(8,128)(2,1)S(1)} %pad_maximum_fusion.refs_0_), channel_id=1, source_target_pairs={{0,4},{2,6},{4,0},{6,2},{1,5},{3,7},{5,1},{7,3},{8,12},{10,14},{12... | collective-permute-start | bytes 1400840 | tf_op jit(solution)/shard_map/ppermute | solution.py:569
  29.7 19.7 %collective-permute-start.3 = (bf16[96,2432]{1,0:T(8,128)(2,1)S(1)}, bf16[96,2432]{1,0:T(8,128)(2,1)S(1)}, u32[]{:S(2)}, u32[]{:S(2)}) collective-permute-start(bf16[96,2432]{1,0:T(8,128)(2,1)S(1)} %pad_maximum_fusion.refs_0_), channel_id=1, source_target_pairs={{0,2},{2,0},{4,6},{6,4},{1,3},{3,1},{5,7},{7,5},{8,10},{10,8},{12,... | collective-permute-start | bytes 1400840 | tf_op jit(solution)/shard_map/ppermute | solution.py:569
  31.7 18.2 %collective-permute-start.6 = (bf16[96,2432]{1,0:T(8,128)(2,1)S(1)}, bf16[96,2432]{1,0:T(8,128)(2,1)S(1)}, u32[]{:S(2)}, u32[]{:S(2)}) collective-permute-start(bf16[96,2432]{1,0:T(8,128)(2,1)S(1)} %pad_maximum_fusion.refs_0_), channel_id=1, source_target_pairs={{0,1},{1,0},{2,3},{3,2},{4,5},{5,4},{6,7},{7,6},{8,9},{9,8},{10,11... | collective-permute-start | bytes 1400840 | tf_op jit(solution)/shard_map/ppermute | solution.py:565
  41.3 14.4 %copy-start.34 = (bf16[96,2432]{1,0:T(8,128)(2,1)}, bf16[96,2432]{1,0:T(8,128)(2,1)S(1)}, u32[]{:S(2)}) copy-start(bf16[96,2432]{1,0:T(8,128)(2,1)S(1)} %collective-permute-done.5.refs_3_) | copy-start | bytes 1400836
  41.3 10.6 %collective-permute-start.9 = (bf16[96,2432]{1,0:T(8,128)(2,1)S(1)}, bf16[96,2432]{1,0:T(8,128)(2,1)S(1)}, u32[]{:S(2)}, u32[]{:S(2)}) collective-permute-start(bf16[96,2432]{1,0:T(8,128)(2,1)S(1)} %collective-permute-done.5.refs_3_), channel_id=1, source_target_pairs={{0,1},{1,0},{2,3},{3,2},{4,5},{5,4},{6,7},{7,6},{8,9},{9,8},{10,11... | collective-permute-start | bytes 1400840 | tf_op jit(solution)/shard_map/ppermute | solution.py:565
  49.4 6.3 %copy-start.35 = (bf16[96,2432]{1,0:T(8,128)(2,1)}, bf16[96,2432]{1,0:T(8,128)(2,1)S(1)}, u32[]{:S(2)}) copy-start(bf16[96,2432]{1,0:T(8,128)(2,1)S(1)} %collective-permute-done.4.refs_2_) | copy-start | bytes 1400836
  49.4 2.5 collective-permute-start.8
  49.4 6.3 %copy-start.36 = (bf16[96,2432]{1,0:T(8,128)(2,1)}, bf16[96,2432]{1,0:T(8,128)(2,1)S(1)}, u32[]{:S(2)}) copy-start(bf16[96,2432]{1,0:T(8,128)(2,1)S(1)} %collective-permute-done.3.refs_1_) | copy-start | bytes 1400836
  49.4 2.5 collective-permute-start.7
  49.9 5.8 %copy-start.37 = (bf16[96,2432]{1,0:T(8,128)(2,1)}, bf16[96,2432]{1,0:T(8,128)(2,1)S(1)}, u32[]{:S(2)}) copy-start(bf16[96,2432]{1,0:T(8,128)(2,1)S(1)} %collective-permute-done.6.refs_4_) | copy-start | bytes 1400836
  145.2 4.7 %collective-permute-start.10 = (bf16[1536,768]{1,0:T(8,128)(2,1)}, bf16[1536,768]{1,0:T(8,128)(2,1)S(1)}, u32[]{:S(2)}, u32[]{:S(2)}) collective-permute-start(bf16[1536,768]{1,0:T(8,128)(2,1)} %bitcast.30), channel_id=1, source_target_pairs={{0,1},{1,0},{2,3},{3,2},{4,5},{5,4},{6,7},{7,6},{8,9},{9,8},{10,11... | collective-permute-start | bytes 7077896 | tf_op jit(solution)/shard_map/ppermute | solution.py:565
  149.9 1.8 copy-start.7
  151.7 43.4 %collective-permute-start.13 = (bf16[384,768]{1,0:T(8,128)(2,1)}, bf16[384,768]{1,0:T(8,128)(2,1)S(1)}, u32[]{:S(2)}, u32[]{:S(2)}) collective-permute-start(bf16[384,768]{1,0:T(8,128)(2,1)} %get-tuple-element.101), channel_id=1, source_target_pairs={{0,6},{2,4},{4,2},{6,0},{1,7},{3,5},{5,3},{7,1},{8,14},{10,12},{12... | collective-permute-start | bytes 1769480 | tf_op jit(solution)/shard_map/ppermute | solution.py:569
  153.1 42.0 %collective-permute-start.12 = (bf16[384,768]{1,0:T(8,128)(2,1)}, bf16[384,768]{1,0:T(8,128)(2,1)S(1)}, u32[]{:S(2)}, u32[]{:S(2)}) collective-permute-start(bf16[384,768]{1,0:T(8,128)(2,1)} %get-tuple-element.102), channel_id=1, source_target_pairs={{0,4},{2,6},{4,0},{6,2},{1,5},{3,7},{5,1},{7,3},{8,12},{10,14},{12... | collective-permute-start | bytes 1769480 | tf_op jit(solution)/shard_map/ppermute | solution.py:569
  154.7 40.4 %collective-permute-start.11 = (bf16[384,768]{1,0:T(8,128)(2,1)S(1)}, bf16[384,768]{1,0:T(8,128)(2,1)S(1)}, u32[]{:S(2)}, u32[]{:S(2)}) collective-permute-start(bf16[384,768]{1,0:T(8,128)(2,1)S(1)} %get-tuple-element.103), channel_id=1, source_target_pairs={{0,2},{2,0},{4,6},{6,4},{1,3},{3,1},{5,7},{7,5},{8,10},{10,8},{12,... | collective-permute-start | bytes 1769480 | tf_op jit(solution)/shard_map/ppermute | solution.py:569
  196.8 6.6 %copy-start.6 = (bf16[384,3840]{1,0:T(8,128)(2,1)S(1)}, bf16[384,3840]{1,0:T(8,128)(2,1)}, u32[]{:S(2)}) copy-start(bf16[384,3840]{1,0:T(8,128)(2,1)} %get-tuple-element.67.refs_0_) | copy-start | bytes 8847364
  196.8 6.5 %collective-permute-start.14 = (bf16[384,3840]{1,0:T(8,128)(2,1)}, bf16[384,3840]{1,0:T(8,128)(2,1)S(1)}, u32[]{:S(2)}, u32[]{:S(2)}) collective-permute-start(bf16[384,3840]{1,0:T(8,128)(2,1)} %gate.3), channel_id=1, source_target_pairs={{0,1},{1,0},{2,3},{3,2},{4,5},{5,4},{6,7},{7,6},{8,9},{9,8},{10,11... | collective-permute-start | bytes 8847368 | tf_op jit(solution)/shard_map/ppermute | solution.py:565
  198.9 9.8 %collective-permute-start.20 = (bf16[96,768]{1,0:T(8,128)(2,1)S(1)}, bf16[96,768]{1,0:T(8,128)(2,1)S(1)}, u32[]{:S(2)}, u32[]{:S(2)}) collective-permute-start(bf16[96,768]{1,0:T(8,128)(2,1)S(1)} %get-tuple-element.89), channel_id=1, source_target_pairs={{0,24},{8,16},{16,8},{24,0},{1,25},{9,17},{17,9},{25,1},{2,26},{10... | collective-permute-start | bytes 442376 | tf_op jit(solution)/shard_map/ppermute | solution.py:569
  201.0 47.0 %collective-permute-start.19 = (bf16[96,768]{1,0:T(8,128)(2,1)S(1)}, bf16[96,768]{1,0:T(8,128)(2,1)S(1)}, u32[]{:S(2)}, u32[]{:S(2)}) collective-permute-start(bf16[96,768]{1,0:T(8,128)(2,1)S(1)} %get-tuple-element.90), channel_id=1, source_target_pairs={{0,16},{8,24},{16,0},{24,8},{1,17},{9,25},{17,1},{25,9},{2,18},{10... | collective-permute-start | bytes 442376 | tf_op jit(solution)/shard_map/ppermute | solution.py:569
  201.8 46.2 %collective-permute-start.18 = (bf16[96,768]{1,0:T(8,128)(2,1)S(1)}, bf16[96,768]{1,0:T(8,128)(2,1)S(1)}, u32[]{:S(2)}, u32[]{:S(2)}) collective-permute-start(bf16[96,768]{1,0:T(8,128)(2,1)S(1)} %get-tuple-element.91), channel_id=1, source_target_pairs={{0,8},{8,0},{16,24},{24,16},{1,9},{9,1},{17,25},{25,17},{2,10},{10... | collective-permute-start | bytes 442376 | tf_op jit(solution)/shard_map/ppermute | solution.py:569
  203.4 2.3 copy-start.5
  205.6 42.5 %collective-permute-start.17 = (bf16[96,3840]{1,0:T(8,128)(2,1)}, bf16[96,3840]{1,0:T(8,128)(2,1)S(1)}, u32[]{:S(2)}, u32[]{:S(2)}) collective-permute-start(bf16[96,3840]{1,0:T(8,128)(2,1)} %get-tuple-element.92), channel_id=1, source_target_pairs={{0,6},{2,4},{4,2},{6,0},{1,7},{3,5},{5,3},{7,1},{8,14},{10,12},{12... | collective-permute-start | bytes 2211848 | tf_op jit(solution)/shard_map/ppermute | solution.py:569
  207.1 41.0 %collective-permute-start.16 = (bf16[96,3840]{1,0:T(8,128)(2,1)}, bf16[96,3840]{1,0:T(8,128)(2,1)S(1)}, u32[]{:S(2)}, u32[]{:S(2)}) collective-permute-start(bf16[96,3840]{1,0:T(8,128)(2,1)} %get-tuple-element.93), channel_id=1, source_target_pairs={{0,4},{2,6},{4,0},{6,2},{1,5},{3,7},{5,1},{7,3},{8,12},{10,14},{12... | collective-permute-start | bytes 2211848 | tf_op jit(solution)/shard_map/ppermute | solution.py:569
  208.7 39.4 %copy-start.25 = (bf16[96,768]{1,0:T(8,128)(2,1)}, bf16[96,768]{1,0:T(8,128)(2,1)S(1)}, u32[]{:S(2)}) copy-start(bf16[96,768]{1,0:T(8,128)(2,1)S(1)} %collective-permute-done.20.refs_6_) | copy-start | bytes 442372
  208.7 39.5 %collective-permute-start.15 = (bf16[96,3840]{1,0:T(8,128)(2,1)}, bf16[96,3840]{1,0:T(8,128)(2,1)S(1)}, u32[]{:S(2)}, u32[]{:S(2)}) collective-permute-start(bf16[96,3840]{1,0:T(8,128)(2,1)} %get-tuple-element.94), channel_id=1, source_target_pairs={{0,2},{2,0},{4,6},{6,4},{1,3},{3,1},{5,7},{7,5},{8,10},{10,8},{12,... | collective-permute-start | bytes 2211848 | tf_op jit(solution)/shard_map/ppermute | solution.py:569
  249.5 1.7 copy-start.33
  249.5 4.8 %copy-start.1 = (bf16[96,3840]{1,0:T(8,128)(2,1)S(1)}, bf16[96,3840]{1,0:T(8,128)(2,1)}, u32[]{:S(2)}) copy-start(bf16[96,3840]{1,0:T(8,128)(2,1)} %copy-done) | copy-start | bytes 2211844
  249.5 4.8 %copy-start.3 = (bf16[96,3840]{1,0:T(8,128)(2,1)S(1)}, bf16[96,3840]{1,0:T(8,128)(2,1)}, u32[]{:S(2)}) copy-start(bf16[96,3840]{1,0:T(8,128)(2,1)} %copy-done.2) | copy-start | bytes 2211844
  249.5 15.0 %collective-permute-start.21 = (bf16[384,2304]{1,0:T(8,128)(2,1)}, bf16[384,2304]{1,0:T(8,128)(2,1)S(1)}, u32[]{:S(2)}, u32[]{:S(2)}) collective-permute-start(bf16[384,2304]{1,0:T(8,128)(2,1)} %gate.4), channel_id=1, source_target_pairs={{0,1},{1,0},{2,3},{3,2},{4,5},{5,4},{6,7},{7,6},{8,9},{9,8},{10,11... | collective-permute-start | bytes 5308424 | tf_op jit(solution)/shard_map/ppermute | solution.py:565
  253.5 11.0 %copy-start.12 = (bf16[384,2304]{1,0:T(8,128)(2,1)S(1)}, bf16[384,2304]{1,0:T(8,128)(2,1)}, u32[]{:S(2)}) copy-start(bf16[384,2304]{1,0:T(8,128)(2,1)} %get-tuple-element.76.refs_1_) | copy-start | bytes 5308420
  256.8 11.4 %collective-permute-start.28 = (bf16[24,3840]{1,0:T(8,128)(2,1)S(1)}, bf16[24,3840]{1,0:T(8,128)(2,1)S(1)}, u32[]{:S(2)}, u32[]{:S(2)}) collective-permute-start(bf16[24,3840]{1,0:T(8,128)(2,1)S(1)} %get-tuple-element.86), channel_id=1, source_target_pairs={{0,8},{8,0},{16,24},{24,16},{1,9},{9,1},{17,25},{25,17},{2,10},{10... | collective-permute-start | bytes 552968 | tf_op jit(solution)/shard_map/ppermute | solution.py:569
  262.5 20.3 %collective-permute-start.30 = (bf16[24,3840]{1,0:T(8,128)(2,1)}, bf16[24,3840]{1,0:T(8,128)(2,1)S(1)}, u32[]{:S(2)}, u32[]{:S(2)}) collective-permute-start(bf16[24,3840]{1,0:T(8,128)(2,1)} %get-tuple-element.87), channel_id=1, source_target_pairs={{0,24},{8,16},{16,8},{24,0},{1,25},{9,17},{17,9},{25,1},{2,26},{10... | collective-permute-start | bytes 552968 | tf_op jit(solution)/shard_map/ppermute | solution.py:569
  264.5 18.3 %collective-permute-start.29 = (bf16[24,3840]{1,0:T(8,128)(2,1)S(1)}, bf16[24,3840]{1,0:T(8,128)(2,1)S(1)}, u32[]{:S(2)}, u32[]{:S(2)}) collective-permute-start(bf16[24,3840]{1,0:T(8,128)(2,1)S(1)} %get-tuple-element.88), channel_id=1, source_target_pairs={{0,16},{8,24},{16,0},{24,8},{1,17},{9,25},{17,1},{25,9},{2,18},{10... | collective-permute-start | bytes 552968 | tf_op jit(solution)/shard_map/ppermute | solution.py:569
  266.1 21.6 %collective-permute-start.22 = (bf16[96,2304]{1,0:T(8,128)(2,1)}, bf16[96,2304]{1,0:T(8,128)(2,1)S(1)}, u32[]{:S(2)}, u32[]{:S(2)}) collective-permute-start(bf16[96,2304]{1,0:T(8,128)(2,1)} %get-tuple-element.98), channel_id=1, source_target_pairs={{0,2},{2,0},{4,6},{6,4},{1,3},{3,1},{5,7},{7,5},{8,10},{10,8},{12,... | collective-permute-start | bytes 1327112 | tf_op jit(solution)/shard_map/ppermute | solution.py:569
  266.7 21.0 %collective-permute-start.24 = (bf16[96,2304]{1,0:T(8,128)(2,1)}, bf16[96,2304]{1,0:T(8,128)(2,1)S(1)}, u32[]{:S(2)}, u32[]{:S(2)}) collective-permute-start(bf16[96,2304]{1,0:T(8,128)(2,1)} %get-tuple-element.99), channel_id=1, source_target_pairs={{0,6},{2,4},{4,2},{6,0},{1,7},{3,5},{5,3},{7,1},{8,14},{10,12},{12... | collective-permute-start | bytes 1327112 | tf_op jit(solution)/shard_map/ppermute | solution.py:569
  268.3 14.5 %copy-start.19 = (bf16[24,3840]{1,0:T(8,128)(2,1)}, bf16[24,3840]{1,0:T(8,128)(2,1)S(1)}, u32[]{:S(2)}) copy-start(bf16[24,3840]{1,0:T(8,128)(2,1)S(1)} %collective-permute-done.28.refs_4_) | copy-start | bytes 552964
  268.3 20.7 %collective-permute-start.23 = (bf16[96,2304]{1,0:T(8,128)(2,1)}, bf16[96,2304]{1,0:T(8,128)(2,1)S(1)}, u32[]{:S(2)}, u32[]{:S(2)}) collective-permute-start(bf16[96,2304]{1,0:T(8,128)(2,1)} %get-tuple-element.100), channel_id=1, source_target_pairs={{0,4},{2,6},{4,0},{6,2},{1,5},{3,7},{5,1},{7,3},{8,12},{10,14},{12... | collective-permute-start | bytes 1327112 | tf_op jit(solution)/shard_map/ppermute | solution.py:569
  282.8 7.8 %copy-start.32 = (bf16[32,96]{1,0:T(8,128)(2,1)S(1)}, bf16[32,96]{1,0:T(8,128)(2,1)}, u32[]{:S(2)}) copy-start(bf16[32,96]{1,0:T(8,128)(2,1)} %reshape.246) | copy-start | bytes 18436
  282.8 6.1 %copy-start.21 = (bf16[24,3840]{1,0:T(8,128)(2,1)}, bf16[24,3840]{1,0:T(8,128)(2,1)S(1)}, u32[]{:S(2)}) copy-start(bf16[24,3840]{1,0:T(8,128)(2,1)S(1)} %collective-permute-done.30.refs_6_) | copy-start | bytes 552964
  282.8 8.1 %copy-start.20 = (bf16[24,3840]{1,0:T(8,128)(2,1)S(1)}, bf16[24,3840]{1,0:T(8,128)(2,1)}, u32[]{:S(2)}) copy-start(bf16[24,3840]{1,0:T(8,128)(2,1)} %copy-done.19) | copy-start | bytes 552964
  282.8 6.1 %copy-start.23 = (bf16[24,3840]{1,0:T(8,128)(2,1)}, bf16[24,3840]{1,0:T(8,128)(2,1)S(1)}, u32[]{:S(2)}) copy-start(bf16[24,3840]{1,0:T(8,128)(2,1)S(1)} %collective-permute-done.29.refs_5_) | copy-start | bytes 552964
  290.6 11.7 %copy-start.14 = (bf16[96,2304]{1,0:T(8,128)(2,1)S(1)}, bf16[96,2304]{1,0:T(8,128)(2,1)}, u32[]{:S(2)}) copy-start(bf16[96,2304]{1,0:T(8,128)(2,1)} %copy-done.13) | copy-start | bytes 1327108
  290.6 11.7 %copy-start.16 = (bf16[96,2304]{1,0:T(8,128)(2,1)S(1)}, bf16[96,2304]{1,0:T(8,128)(2,1)}, u32[]{:S(2)}) copy-start(bf16[96,2304]{1,0:T(8,128)(2,1)} %copy-done.15) | copy-start | bytes 1327108
  290.6 11.7 %copy-start.18 = (bf16[96,2304]{1,0:T(8,128)(2,1)S(1)}, bf16[96,2304]{1,0:T(8,128)(2,1)}, u32[]{:S(2)}) copy-start(bf16[96,2304]{1,0:T(8,128)(2,1)} %copy-done.17) | copy-start | bytes 1327108
  290.9 1.5 collective-permute-start.31
  292.3 5.0 %collective-permute-start.32 = (bf16[4,384]{1,0:T(4,128)(2,1)S(1)}, bf16[4,384]{1,0:T(4,128)(2,1)S(1)}, u32[]{:S(2)}, u32[]{:S(2)}) collective-permute-start(bf16[4,384]{1,0:T(4,128)(2,1)S(1)} %get-tuple-element.110), channel_id=1, source_target_pairs={{0,2},{2,0},{4,6},{6,4},{1,3},{3,1},{5,7},{7,5},{8,10},{10,8},{12,... | collective-permute-start | bytes 9224 | tf_op jit(solution)/shard_map/ppermute | solution.py:569
  293.0 4.5 %collective-permute-start.34 = (bf16[4,384]{1,0:T(4,128)(2,1)S(1)}, bf16[4,384]{1,0:T(4,128)(2,1)S(1)}, u32[]{:S(2)}, u32[]{:S(2)}) collective-permute-start(bf16[4,384]{1,0:T(4,128)(2,1)S(1)} %get-tuple-element.111), channel_id=1, source_target_pairs={{0,6},{2,4},{4,2},{6,0},{1,7},{3,5},{5,3},{7,1},{8,14},{10,12},{12... | collective-permute-start | bytes 9224 | tf_op jit(solution)/shard_map/ppermute | solution.py:569
  294.5 3.6 %collective-permute-start.33 = (bf16[4,384]{1,0:T(4,128)(2,1)S(1)}, bf16[4,384]{1,0:T(4,128)(2,1)S(1)}, u32[]{:S(2)}, u32[]{:S(2)}) collective-permute-start(bf16[4,384]{1,0:T(4,128)(2,1)S(1)} %get-tuple-element.112), channel_id=1, source_target_pairs={{0,4},{2,6},{4,0},{6,2},{1,5},{3,7},{5,1},{7,3},{8,12},{10,14},{12... | collective-permute-start | bytes 9224 | tf_op jit(solution)/shard_map/ppermute | solution.py:569
  298.1 10.0 %collective-permute-start.35 = (bf16[1,384]{1,0:T(2,128)(2,1)S(1)}, bf16[1,384]{1,0:T(2,128)(2,1)S(1)}, u32[]{:S(2)}, u32[]{:S(2)}) collective-permute-start(bf16[1,384]{1,0:T(2,128)(2,1)S(1)} %get-tuple-element.107), channel_id=1, source_target_pairs={{0,8},{8,0},{16,24},{24,16},{1,9},{9,1},{17,25},{25,17},{2,10},{10... | collective-permute-start | bytes 2312 | tf_op jit(solution)/shard_map/ppermute | solution.py:569
  300.3 7.8 %collective-permute-start.37 = (bf16[1,384]{1,0:T(2,128)(2,1)S(1)}, bf16[1,384]{1,0:T(2,128)(2,1)S(1)}, u32[]{:S(2)}, u32[]{:S(2)}) collective-permute-start(bf16[1,384]{1,0:T(2,128)(2,1)S(1)} %get-tuple-element.108), channel_id=1, source_target_pairs={{0,24},{8,16},{16,8},{24,0},{1,25},{9,17},{17,9},{25,1},{2,26},{10... | collective-permute-start | bytes 2312 | tf_op jit(solution)/shard_map/ppermute | solution.py:569
  302.3 5.9 %collective-permute-start.36 = (bf16[1,384]{1,0:T(2,128)(2,1)S(1)}, bf16[1,384]{1,0:T(2,128)(2,1)S(1)}, u32[]{:S(2)}, u32[]{:S(2)}) collective-permute-start(bf16[1,384]{1,0:T(2,128)(2,1)S(1)} %get-tuple-element.109), channel_id=1, source_target_pairs={{0,16},{8,24},{16,0},{24,8},{1,17},{9,25},{17,1},{25,9},{2,18},{10... | collective-permute-start | bytes 2312 | tf_op jit(solution)/shard_map/ppermute | solution.py:569
  303.7 6.5 %collective-permute-start.25 = (bf16[24,2304]{1,0:T(8,128)(2,1)S(1)}, bf16[24,2304]{1,0:T(8,128)(2,1)S(1)}, u32[]{:S(2)}, u32[]{:S(2)}) collective-permute-start(bf16[24,2304]{1,0:T(8,128)(2,1)S(1)} %get-tuple-element.95), channel_id=1, source_target_pairs={{0,8},{8,0},{16,24},{24,16},{1,9},{9,1},{17,25},{25,17},{2,10},{10... | collective-permute-start | bytes 331784 | tf_op jit(solution)/shard_map/ppermute | solution.py:569
  306.2 6.8 %collective-permute-start.27 = (bf16[24,2304]{1,0:T(8,128)(2,1)S(1)}, bf16[24,2304]{1,0:T(8,128)(2,1)S(1)}, u32[]{:S(2)}, u32[]{:S(2)}) collective-permute-start(bf16[24,2304]{1,0:T(8,128)(2,1)S(1)} %get-tuple-element.96), channel_id=1, source_target_pairs={{0,24},{8,16},{16,8},{24,0},{1,25},{9,17},{17,9},{25,1},{2,26},{10... | collective-permute-start | bytes 331784 | tf_op jit(solution)/shard_map/ppermute | solution.py:569
  308.2 8.5 %collective-permute-start.26 = (bf16[24,2304]{1,0:T(8,128)(2,1)S(1)}, bf16[24,2304]{1,0:T(8,128)(2,1)S(1)}, u32[]{:S(2)}, u32[]{:S(2)}) collective-permute-start(bf16[24,2304]{1,0:T(8,128)(2,1)S(1)} %get-tuple-element.97), channel_id=1, source_target_pairs={{0,16},{8,24},{16,0},{24,8},{1,17},{9,25},{17,1},{25,9},{2,18},{10... | collective-permute-start | bytes 331784 | tf_op jit(solution)/shard_map/ppermute | solution.py:569
  (18 other events, 19.1 us)
Sparse Core Ops, SparseCore 0:
  11.3 97.5 all-gather.1
where the time goes:
time: 329 us; the launch traced here: 326 us
  Pallas kernels  161 us (49%)
  waiting for transfers between devices  65.5 us (20%)
  starting transfers between devices  45 us (14%)
  other arithmetic  21.3 us (6%)
  local copies, waits for them, and re-layouts  16.8 us (5%)
  between operations  15.8 us (5%)
    ppermute x30, starting transfers between devices, from_peer(): lax.ppermute(x, axes, [(i, i ^ k) for i in range(lax.axis_size(axes))])  44 us
    pallas_call x1, Pallas kernels, down_call(): pl.pallas_call(down_kernel, grid=(STEPS + 1,), in_specs=[part, part, whol...  39.9 us
    ppermute x30, waiting for transfers between devices, from_peer(): lax.ppermute(x, axes, [(i, i ^ k) for i in range(lax.axis_size(axes))])  39.9 us
    pallas_call x1, Pallas kernels, back_call(): pl.pallas_call(functools.partial(back_kernel, group, len(passed)), grid=(...  38.9 us
    pallas_call x1, Pallas kernels, up_call(): pl.pallas_call(up_kernel, grid_spec=pltpu.PrefetchScalarGridSpec(num_scal...  24.9 us
    all_gather x1, waiting for transfers between devices, shards(): mlp = join_owners(lax.all_gather(mlp, ALL, axis=0), rows)  20.8 us
    pallas_call x1, Pallas kernels, attn_call(): pl.pallas_call(attn_kernel, grid=(NBLK,), in_specs=[pl.BlockSpec(memory_s...  18.8 us
    pallas_call x1, Pallas kernels, qkv_call(): pl.pallas_call(qkv_kernel, grid=(ROWS // TILE,), in_specs=[ANY] * len(par...  13.6 us
  transfers between devices with their start and end apart: 39, of which 14 were waited for; matrix products, arithmetic and copies ran while one was open for 7% of the time, Pallas kernels for 38%

commit v1 on v0

v1 whole, which is shorter than its diff:
```python
import functools

import jax
import jax.numpy as jnp
from jax import lax
from jax.experimental import pallas as pl
from jax.experimental.pallas import tpu as pltpu
from jax.sharding import Mesh
from jax.sharding import PartitionSpec as P

HEADS = 12
HD = 64
ROWS = 1024
D = HEADS * HD
FF = 4 * D
PAIRS = HEADS // 2
BLK = 128
QB = 2 * BLK
WIN = QB + 2 * BLK
TILE = 256
EPS = 1e-06
ALL = ("a", "b", "f", "c")
bf16 = jnp.bfloat16
f32 = jnp.float32
VMEM_LIMIT = 60 * 1024 * 1024
ANY = pl.BlockSpec(memory_space=pl.ANY)


def cost(us):
    return pl.CostEstimate(flops=us * 1_100_000_000, bytes_accessed=us * 3_000_000, transcendentals=0)


def dot_nn(left, right):
    return lax.dot_general(left, right, (((1,), (0,)), ((), ())), preferred_element_type=f32)


def dot_nt(left, right):
    return lax.dot_general(left, right, (((1,), (1,)), ((), ())), preferred_element_type=f32)


def dot_tn(left, right):
    return lax.dot_general(left, right, (((0,), (0,)), ((), ())), preferred_element_type=f32)


def eye():
    rows = lax.broadcasted_iota(jnp.int32, (BLK, BLK), 0)
    cols = lax.broadcasted_iota(jnp.int32, (BLK, BLK), 1)
    return (rows == cols).astype(f32).astype(bf16)


def flip(one, block):
    return dot_nt(one, block).astype(bf16)


def norm_parts(values):
    center = values - jnp.mean(values, axis=-1, keepdims=True)
    scale = lax.rsqrt(jnp.mean(center * center, axis=-1, keepdims=True) + EPS)
    return center * scale, scale


def norm_back(grad, normed, scale, gain):
    inner = grad * gain
    first = jnp.mean(inner, axis=-1, keepdims=True)
    second = jnp.mean(inner * normed, axis=-1, keepdims=True)
    return scale * (inner - first - normed * second)


def col_sum(values):
    return jnp.sum(values, axis=0, keepdims=True)


def gelu_parts(u):
    half = 0.5 + 0.5 * lax.erf(u * 0.7071067811865476)
    e = jnp.exp2((u * u) * -0.7213475204444817)
    return u * half, half + (0.3989422804014327 * u) * e


def params(**kw):
    return pltpu.CompilerParams(vmem_limit_bytes=VMEM_LIMIT, **kw)


def whole(shape):
    return pl.BlockSpec(shape, lambda *_: (0,) * len(shape))


def gather_copies(parts, line_me, me_ref, source, target, sems):
    if len(parts) == 1:
        return [pltpu.make_async_copy(source(parts[0], None), target(None), sems.at[0])]
    half, copies = len(parts) // 2, []
    for n, part in enumerate(parts):
        for k in range(part.shape[0]):
            device = ((k ^ line_me) * half + (n % half ^ me_ref[1])) * 2 + (n // half ^ me_ref[2])
            copies.append(pltpu.make_async_copy(source(part, k), target(device), sems.at[n * part.shape[0] + k]))
    return copies


def copy_count(parts):
    return 1 if len(parts) == 1 else len(parts) * parts[0].shape[0]


def fill_segments(lens_ref, valid_ref, segc, segr):
    row_c = lax.broadcasted_iota(jnp.int32, (ROWS, BLK), 0)
    row_r = lax.broadcasted_iota(jnp.int32, (8, ROWS), 1)
    sum_c = jnp.zeros((ROWS, BLK), jnp.int32)
    sum_r = jnp.zeros((8, ROWS), jnp.int32)
    end = jnp.int32(0)
    for j in range(lens_ref.shape[1]):
        end = end + lens_ref[0, j]
        sum_c = sum_c + (row_c >= end).astype(jnp.int32)
        sum_r = sum_r + (row_r >= end).astype(jnp.int32)
    valid = valid_ref[0]
    segc[...] = jnp.where(row_c < valid, sum_c, -1)
    segr[...] = jnp.where(row_r < valid, sum_r, -1)


def block_place(segc, segr, i):
    start = pl.multiple_of(jnp.clip(i * (QB // BLK) - 1, 0, (ROWS - WIN) // BLK) * BLK, BLK)
    here = pl.ds(pl.multiple_of(i * QB, BLK), QB)
    window = pl.ds(start, WIN)
    rows = jnp.concatenate([segc[here, :]] * (WIN // BLK), axis=1)
    bias = jnp.where(rows == segr[0:1, window], 0.0, -1000000000.0).astype(f32)
    return here, window, jnp.concatenate([bias, bias], axis=0)


def lane_masks():
    low = (lax.broadcasted_iota(jnp.int32, (1, BLK), 1) < HD).astype(f32)
    return low.astype(bf16), (1.0 - low).astype(bf16)


def stack_pair(block, masks):
    return jnp.concatenate([block * masks[0], block * masks[1]], axis=0)


def pick_pair(values):
    low = lax.broadcasted_iota(jnp.int32, (1, BLK), 1) < HD
    return jnp.where(low, values[:QB], values[QB:])


def attend_kernel(count, passed, lens_ref, valid_ref, me_ref, *refs):
    parts, (x_ref, turn_ref, vec_ref) = refs[:count], refs[count : count + 3]
    q_ref, k_ref, v_ref, ht_ref, w_out, o_ref, lse_ref = refs[-16 - passed :][:7]
    stage, w_ref, qs, ks, vs, segc, segr, sems, out_sem = refs[-9:]
    i = pl.program_id(0)
    tiles = ROWS // TILE

    def fetch():
        def source(part, k):
            return part if k is None else part.at[k]

        return gather_copies(parts, me_ref[0], me_ref, source, lambda n: stage if n is None else stage.at[n], sems)

    def store():
        return pltpu.make_async_copy(w_ref, w_out, out_sem)

    @pl.when(i == 0)
    def _():
        for copy in fetch():
            copy.start()
        fill_segments(lens_ref, valid_ref, segc, segr)
        for copy in fetch():
            copy.wait()
        w_ref[...] = stage[...].astype(f32).reshape(D, 3 * D).astype(bf16)
        store().start()

    @pl.when(i < tiles)
    def _():
        rows = pl.ds(pl.multiple_of(i * TILE, TILE), TILE)
        normed, _ = norm_parts(x_ref[...])
        low = (normed * vec_ref[0:1] + vec_ref[1:2]).astype(bf16)
        q = ((dot_nn(low, w_ref[:, :D]) + vec_ref[2:3]).astype(bf16).astype(f32) * 0.125).astype(bf16)
        k = dot_nn(low, w_ref[:, D : 2 * D]).astype(bf16)
        v = (dot_nn(low, w_ref[:, 2 * D :]) + vec_ref[3:4]).astype(bf16)
        for value, ref, scratch in ((q, q_ref, qs), (k, k_ref, ks), (v, v_ref, vs)):
            ref[...] = value
            scratch[rows] = value
        turned = dot_nn(low, turn_ref[...]).astype(bf16)
        one = eye()
        for p in range(PAIRS):
            s = slice(p * BLK, (p + 1) * BLK)
            ht_ref[s] = flip(one, turned[:, s])

    @pl.when(i >= tiles)
    def _():
        here, window, bias = block_place(segc, segr, i - tiles)
        masks = lane_masks()
        for p in range(PAIRS):
            s = slice(p * BLK, (p + 1) * BLK)
            scores = dot_nt(stack_pair(qs[here, s], masks), ks[window, s]) + bias
            peak = jnp.max(scores, axis=1, keepdims=True)
            expo = jnp.exp(scores - peak)
            total = jnp.sum(expo, axis=1, keepdims=True)
            o_ref[:, s] = pick_pair(dot_nn(expo.astype(bf16), vs[window, s]) * (1.0 / total)).astype(bf16)
            lse_ref[0, :, p : p + 1] = peak + jnp.log(total)

    @pl.when(i == tiles + ROWS // QB - 1)
    def _():
        store().wait()


def attend_call(lens, valid, me, parts, x, turn, vec, passed=(), tokens=()):
    tiles = ROWS // TILE

    def first(i):
        return jnp.minimum(i, tiles - 1)

    def second(i):
        return jnp.maximum(i - tiles, 0)

    tok = pl.BlockSpec((TILE, D), lambda i: (first(i), 0))
    smem = pl.BlockSpec(memory_space=pltpu.SMEM)
    count, rows = len(parts), parts[0].shape[1]
    extra = list(passed) + list(tokens)
    out = pl.pallas_call(
        functools.partial(attend_kernel, count, len(passed)),
        grid=(tiles + ROWS // QB,),
        in_specs=[smem] * 3 + [ANY] * count + [tok, whole((D, D)), whole((16, D))] + [ANY] * len(extra),
        out_specs=[
            tok,
            tok,
            tok,
            pl.BlockSpec((D, TILE), lambda i: (0, first(i))),
            ANY,
            pl.BlockSpec((QB, D), lambda i: (second(i), 0)),
            pl.BlockSpec((1, 2 * QB, BLK), lambda i: (second(i), 0, 0)),
        ]
        + [ANY] * len(passed),
        out_shape=[jax.ShapeDtypeStruct((ROWS, D), bf16)] * 3
        + [
            jax.ShapeDtypeStruct((D, ROWS), bf16),
            jax.ShapeDtypeStruct((D, 3 * D), bf16),
            jax.ShapeDtypeStruct((ROWS, D), bf16),
            jax.ShapeDtypeStruct((ROWS // QB, 2 * QB, BLK), f32),
        ]
        + [jax.ShapeDtypeStruct(p.shape, p.dtype) for p in passed],
        scratch_shapes=[
            pltpu.VMEM((D // rows, rows, 3 * D), bf16),
            pltpu.VMEM((D, 3 * D), bf16),
            pltpu.VMEM((ROWS, D), bf16),
            pltpu.VMEM((ROWS, D), bf16),
            pltpu.VMEM((ROWS, D), bf16),
            pltpu.VMEM((ROWS, BLK), jnp.int32),
            pltpu.VMEM((8, ROWS), jnp.int32),
            pltpu.SemaphoreType.DMA((copy_count(parts),)),
            pltpu.SemaphoreType.DMA,
        ],
        input_output_aliases={6 + count + n: 7 + n for n in range(len(passed))},
        compiler_params=params(),
        cost_estimate=cost(25),
        name="attend",
    )(lens, valid, me, *parts, x, turn, vec, *extra)
    return out[:7], out[7:]


STEPS = FF // D


def up_kernel(count, me_ref, o_ref, x_ref, ct_ref, turn_ref, vec_ref, b_ref, *refs):
    parts = refs[:count]
    h, dzs, stage, wp, dw_ref, p_sems, w_sems, out_sem = refs[-8:]
    grads = 2 if count > 1 else 1
    outs = refs[-17 - grads : -8]
    x1_ref, a_ref, ht_ref, ot_ref, dz_ref, wp_out, w_ref, m_ref, gp_ref, *grad_refs = outs
    i = pl.program_id(0)
    tiles = ROWS // TILE

    def fetch(first):
        block = pl.ds(4, 1) if first else pl.ds(0, 4)

        def source(part, k):
            return part.at[block] if k is None else part.at[k, block]

        def target(n):
            return stage.at[block] if n is None else stage.at[block, n]

        return gather_copies(parts, 0, me_ref, source, target, p_sems if first else w_sems)

    def store():
        return pltpu.make_async_copy(wp, wp_out, out_sem)

    @pl.when(i == 0)
    def _():
        for copy in fetch(True):
            copy.start()
        for copy in fetch(False):
            copy.start()
        for copy in fetch(True):
            copy.wait()
        wp[...] = stage[4].astype(f32).reshape(D, D).astype(bf16)
        store().start()

    @pl.when(i < tiles)
    def _():
        rows = pl.ds(pl.multiple_of(i * TILE, TILE), TILE)
        branch = dot_nn(o_ref[...], wp[...]) + vec_ref[4:5]
        inner = x_ref[...] + vec_ref[5:6] * branch
        x1_ref[...] = inner
        a_ref[...] = branch.astype(bf16)
        normed, _ = norm_parts(inner)
        low = (normed * vec_ref[6:7] + vec_ref[7:8]).astype(bf16)
        h[rows] = low
        dz = (vec_ref[9:10] * ct_ref[...]).astype(bf16)
        dz_ref[...] = dz
        dzs[rows] = dz
        one = eye()
        turned = dot_nn(low, turn_ref[...]).astype(bf16)
        turned_o = dot_nn(o_ref[...], turn_ref[...]).astype(bf16)
        for p in range(PAIRS):
            s = slice(p * BLK, (p + 1) * BLK)
            ht_ref[s] = flip(one, turned[:, s])
            ot_ref[s] = flip(one, turned_o[:, s])

    @pl.when(i == tiles)
    def _():
        for copy in fetch(False):
            copy.wait()
        store().wait()

    @pl.when(i >= tiles)
    def _():
        chunk = (i - tiles) ^ (me_ref[0] if count > 1 else 0)
        w_ref[0] = stage[chunk].astype(f32).reshape(D, D).astype(bf16)
        for n in range(D // TILE):
            c = slice(n * TILE, (n + 1) * TILE)
            for t in range(tiles):
                r = slice(t * TILE, (t + 1) * TILE)
                m, gp = gelu_parts(dot_nn(h[r], w_ref[0, :, c]) + b_ref[:, c])
                m_ref[r, c] = m.astype(bf16)
                gp_ref[r, c] = gp.astype(bf16)
        for n in range(D // TILE):
            c = slice(n * TILE, (n + 1) * TILE)
            dw_ref[c] = dot_tn(m_ref[:, c], dzs[...])
        if grads == 1:
            grad_refs[0][...] = dw_ref[...].astype(bf16)
        else:
            blocks, _, size, _ = grad_refs[0].shape
            for k in range(blocks):
                for c, ref in enumerate(grad_refs):
                    row = ((k ^ me_ref[1]) * 2 + (c ^ me_ref[2])) * size
                    ref[k, 0] = dw_ref[pl.ds(pl.multiple_of(row, 8), size), :].astype(bf16)


def up_call(me, o, x, ct, turn, vec, b, parts, tokens=()):
    count = len(parts)
    tiles = ROWS // TILE
    _, n, r, _ = (1,) + parts[0].shape[1:] if count == 1 else (1, D // parts[0].shape[2], parts[0].shape[2], D)

    def first(i):
        return jnp.minimum(i, tiles - 1)

    def chunk(i, me):
        return jnp.maximum(i - tiles, 0) ^ (me[0] if count > 1 else 0)

    tok = pl.BlockSpec((TILE, D), lambda i, me: (first(i), 0))
    feat = pl.BlockSpec((D, TILE), lambda i, me: (0, first(i)))
    part = pl.BlockSpec((ROWS, D), lambda i, me: (0, chunk(i, me)))
    if count > 1:
        blocks = count // 2
        spec = pl.BlockSpec((blocks, 1, 4 * r, D), lambda i, me: (0, jnp.maximum(i - tiles, 0), 0, 0))
        grad_specs, grad_shapes = [spec] * 2, [jax.ShapeDtypeStruct((blocks, STEPS, 4 * r, D), bf16)] * 2
    else:
        grad_specs = [pl.BlockSpec((D, D), lambda i, me: (chunk(i, me), 0))]
        grad_shapes = [jax.ShapeDtypeStruct((FF, D), bf16)]
    return pl.pallas_call(
        functools.partial(up_kernel, count),
        grid_spec=pltpu.PrefetchScalarGridSpec(
            num_scalar_prefetch=1,
            grid=(tiles + STEPS,),
            in_specs=[tok, tok, tok, whole((D, D)), whole((16, D)), pl.BlockSpec((1, D), lambda i, me: (0, chunk(i, me)))]
            + [ANY] * (count + len(tokens)),
            out_specs=[
                tok,
                tok,
                feat,
                feat,
                tok,
                ANY,
                pl.BlockSpec((1, D, D), lambda i, me: (chunk(i, me), 0, 0)),
                part,
                part,
            ]
            + grad_specs,
            scratch_shapes=[
                pltpu.VMEM((ROWS, D), bf16),
                pltpu.VMEM((ROWS, D), bf16),
                pltpu.VMEM((5, n, r, D), bf16),
                pltpu.VMEM((D, D), bf16),
                pltpu.VMEM((D, D), f32),
                pltpu.SemaphoreType.DMA((copy_count(parts),)),
                pltpu.SemaphoreType.DMA((copy_count(parts),)),
                pltpu.SemaphoreType.DMA,
            ],
        ),
        out_shape=[
            jax.ShapeDtypeStruct((ROWS, D), f32),
            jax.ShapeDtypeStruct((ROWS, D), bf16),
            jax.ShapeDtypeStruct((D, ROWS), bf16),
            jax.ShapeDtypeStruct((D, ROWS), bf16),
            jax.ShapeDtypeStruct((ROWS, D), bf16),
            jax.ShapeDtypeStruct((D, D), bf16),
            jax.ShapeDtypeStruct((STEPS, D, D), bf16),
            jax.ShapeDtypeStruct((ROWS, FF), bf16),
            jax.ShapeDtypeStruct((ROWS, FF), bf16),
        ]
        + grad_shapes,
        compiler_params=params(),
        cost_estimate=cost(26),
        name="mlp_up",
    )(me, o, x, ct, turn, vec, b, *parts, *tokens)


def down_kernel(
    count, me_ref, m_ref, gp_ref, dz_ref, ht_ref, w1_ref, x1_ref, ct_ref, a_ref, ot_ref, wp_ref, dzt_ref, vec_ref, *refs
):
    parts = refs[:count]
    out_ref, dx_ref, do_ref, keep_ref, away_ref, db1_ref, sums_ref, _, z_acc, dh_acc, dwp_acc, w2_ref, sems = refs[-13:]
    j = pl.program_id(0)

    def fetch(step):
        if count == 1:
            return [pltpu.make_async_copy(parts[0].at[step], w2_ref.at[step], sems.at[step, 0])]
        half, copies = count // 2, []
        for n, part in enumerate(parts):
            place = (n % half ^ me_ref[1]) * 2 + (n // half ^ me_ref[2])
            copies.append(pltpu.make_async_copy(part.at[step], w2_ref.at[step, place], sems.at[step, n]))
        return copies

    @pl.when(j == 0)
    def _():
        for step in range(STEPS):
            for copy in fetch(step):
                copy.start()
        z_acc[...] = jnp.zeros_like(z_acc)
        dh_acc[...] = jnp.zeros_like(dh_acc)
        dwp_acc[...] = jnp.zeros_like(dwp_acc)
        sums_ref[...] = jnp.zeros_like(sums_ref)

    @pl.when(j < STEPS)
    def _():
        for copy in fetch(j):
            copy.wait()
        w1 = w1_ref[0]
        w2 = w2_ref[j].reshape(D, D)
        du = (dot_nt(dz_ref[...], w2) * gp_ref[...].astype(f32)).astype(bf16)
        db1_ref[...] = col_sum(du.astype(f32))
        keep_ref[...] = dot_nn(ht_ref[: D // 2], du).astype(bf16)
        away_ref[...] = dot_nn(ht_ref[D // 2 :], du).astype(bf16)
        z_acc[...] += dot_nn(m_ref[...], w2)
        dh_acc[...] += dot_nt(du, w1)

    @pl.when(j >= STEPS)
    def _():
        r = pl.ds(pl.multiple_of((j - STEPS) * TILE, TILE), TILE)
        inner, ct, branch = x1_ref[...], ct_ref[...], z_acc[r] + vec_ref[8:9]
        out_ref[...] = inner + vec_ref[9:10] * branch
        normed, scale = norm_parts(inner)
        dh = dh_acc[r]
        dx = ct + norm_back(dh, normed, scale, vec_ref[6:7])
        dx_ref[...] = dx
        da = (vec_ref[5:6] * dx).astype(bf16)
        do_ref[...] = dot_nt(da, wp_ref[...]).astype(bf16)
        dwp_acc[...] += dot_nn(ot_ref[...], da)
        adds = (da.astype(f32), dx * a_ref[...].astype(f32), dh * normed, dh, dzt_ref[...].astype(f32), ct * branch)
        sums_ref[...] += jnp.concatenate([col_sum(v) for v in adds] + [jnp.zeros((2, D), f32)], axis=0)

    @pl.when(j == STEPS + ROWS // TILE - 1)
    def _():
        keep_ref[...] = dwp_acc[: D // 2].astype(bf16)
        away_ref[...] = dwp_acc[D // 2 :].astype(bf16)


def down_call(me, m, gp, dz, ht, w1, parts, x1, ct, a, ot, wp, vec, passed, tokens):
    count = len(parts)
    size = parts[0].shape[-2]

    def last(j):
        return jnp.minimum(j, STEPS - 1)

    def row(j):
        return jnp.maximum(j - STEPS, 0)

    part = pl.BlockSpec((ROWS, D), lambda j: (0, last(j)))
    grad = pl.BlockSpec((D // 2, D), lambda j: (0, jnp.minimum(j, STEPS)))
    tile = pl.BlockSpec((TILE, D), lambda j: (row(j), 0))
    return pl.pallas_call(
        functools.partial(down_kernel, count),
        grid=(STEPS + ROWS // TILE,),
        in_specs=[
            pl.BlockSpec(memory_space=pltpu.SMEM),
            part,
            part,
            whole((ROWS, D)),
            whole((D, ROWS)),
            pl.BlockSpec((1, D, D), lambda j: (last(j), 0, 0)),
            tile,
            tile,
            tile,
            pl.BlockSpec((D, TILE), lambda j: (0, row(j))),
            whole((D, D)),
            tile,
            whole((16, D)),
        ]
        + [ANY] * (count + 1 + len(tokens)),
        out_specs=[
            tile,
            tile,
            tile,
            grad,
            grad,
            pl.BlockSpec((1, D), lambda j: (0, last(j))),
            whole((8, D)),
            ANY,
        ],
        out_shape=[
            jax.ShapeDtypeStruct((ROWS, D), f32),
            jax.ShapeDtypeStruct((ROWS, D), f32),
            jax.ShapeDtypeStruct((ROWS, D), bf16),
            jax.ShapeDtypeStruct((D // 2, FF + D), bf16),
            jax.ShapeDtypeStruct((D // 2, FF + D), bf16),
            jax.ShapeDtypeStruct((1, FF), f32),
            jax.ShapeDtypeStruct((8, D), f32),
            jax.ShapeDtypeStruct(passed.shape, passed.dtype),
        ],
        scratch_shapes=[
            pltpu.VMEM((ROWS, D), f32),
            pltpu.VMEM((ROWS, D), f32),
            pltpu.VMEM((D, D), f32),
            pltpu.VMEM((STEPS, D // size, size, D), bf16),
            pltpu.SemaphoreType.DMA((STEPS, count)),
        ],
        input_output_aliases={13 + count: 7},
        compiler_params=params(),
        cost_estimate=cost(35),
        name="mlp_down",
    )(me, m, gp, dz, ht, w1, x1, ct, a, ot, wp, dz, vec, *parts, passed, *tokens)


def back_kernel(passed, lens_ref, valid_ref, q_ref, k_ref, v_ref, do_ref, o_ref, lse_ref, ht_hbm, *refs):
    dq_out, dk_out, dv_out, keep_ref, away_ref, sums_ref = refs[-16 - passed :][:6]
    segc, segr, dk_acc, dv_acc, dq_ref, dk_ref, dv_ref, ht_ref, sems, ht_sem = refs[-10:]
    i = pl.program_id(0)
    steps = ROWS // QB

    def fetch():
        return pltpu.make_async_copy(ht_hbm, ht_ref, ht_sem)

    def store(n):
        return pltpu.make_async_copy((dq_ref, dk_ref, dv_ref)[n], (dq_out, dk_out, dv_out)[n], sems.at[n])

    @pl.when(i == 0)
    def _():
        fetch().start()
        fill_segments(lens_ref, valid_ref, segc, segr)
        dk_acc[...] = jnp.zeros_like(dk_acc)
        dv_acc[...] = jnp.zeros_like(dv_acc)

    @pl.when(i < steps)
    def _():
        here, window, bias = block_place(segc, segr, i)
        masks = lane_masks()
        for p in range(PAIRS):
            s = slice(p * BLK, (p + 1) * BLK)
            queries = stack_pair(q_ref[:, s], masks)
            grads = stack_pair(do_ref[:, s], masks)
            o = o_ref[:, s].astype(f32)
            center = jnp.sum(grads.astype(f32) * jnp.concatenate([o, o], axis=0), axis=1, keepdims=True)
            probs = jnp.exp(dot_nt(queries, k_ref[window, s]) + bias - lse_ref[0, :, p : p + 1])
            dscores = (probs * (dot_nt(grads, v_ref[window, s]) - center)).astype(bf16)
            dv_acc[window, s] += dot_tn(probs.astype(bf16), grads)
            dk_acc[window, s] += dot_tn(dscores, queries)
            dq_ref[here, s] = (pick_pair(dot_nn(dscores, k_ref[window, s])) * 0.125).astype(bf16)

    def weights(ref):
        away_ref[...] = dot_nn(ht_ref[D // 2 :], ref[...]).astype(bf16)
        keep_ref[...] = dot_nn(ht_ref[: D // 2], ref[...]).astype(bf16)

    @pl.when(i == steps)
    def _():
        dk_ref[...] = dk_acc[...].astype(bf16)
        dv_ref[...] = dv_acc[...].astype(bf16)
        for n in range(3):
            store(n).start()
        fetch().wait()
        weights(dq_ref)
        dbq = col_sum(dq_ref[...].astype(f32))
        dbv = col_sum(dv_ref[...].astype(f32))
        sums_ref[...] = jnp.concatenate([dbq, dbv, jnp.zeros((6, D), f32)], axis=0)

    @pl.when(i == steps + 1)
    def _():
        weights(dk_ref)

    @pl.when(i == steps + 2)
    def _():
        weights(dv_ref)
        for n in range(3):
            store(n).wait()


def back_call(lens, valid, q, k, v, do, o, lse, ht, passed=(), tokens=()):
    steps = ROWS // QB

    def last(i):
        return jnp.minimum(i, steps - 1)

    tok = pl.BlockSpec((QB, D), lambda i: (last(i), 0))
    full = whole((ROWS, D))
    grad = pl.BlockSpec((D // 2, D), lambda i: (0, jnp.maximum(i - steps, 0)))
    extra = list(passed) + list(tokens)
    out = pl.pallas_call(
        functools.partial(back_kernel, len(passed)),
        grid=(steps + 3,),
        in_specs=[
            pl.BlockSpec(memory_space=pltpu.SMEM),
            pl.BlockSpec(memory_space=pltpu.SMEM),
            tok,
            full,
            full,
            tok,
            tok,
            pl.BlockSpec((1, 2 * QB, BLK), lambda i: (last(i), 0, 0)),
            ANY,
        ]
        + [ANY] * len(extra),
        out_specs=[ANY] * 3 + [grad, grad, whole((8, D))] + [ANY] * len(passed),
        out_shape=[jax.ShapeDtypeStruct((ROWS, D), bf16)] * 3
        + [jax.ShapeDtypeStruct((D // 2, 3 * D), bf16)] * 2
        + [jax.ShapeDtypeStruct((8, D), f32)]
        + [jax.ShapeDtypeStruct(p.shape, p.dtype) for p in passed],
        scratch_shapes=[
            pltpu.VMEM((ROWS, BLK), jnp.int32),
            pltpu.VMEM((8, ROWS), jnp.int32),
            pltpu.VMEM((ROWS, D), f32),
            pltpu.VMEM((ROWS, D), f32),
            pltpu.VMEM((ROWS, D), bf16),
            pltpu.VMEM((ROWS, D), bf16),
            pltpu.VMEM((ROWS, D), bf16),
            pltpu.VMEM((D, ROWS), bf16),
            pltpu.SemaphoreType.DMA((3,)),
            pltpu.SemaphoreType.DMA,
        ],
        input_output_aliases={9 + n: 6 + n for n in range(len(passed))},
        compiler_params=params(),
        cost_estimate=cost(33),
        name="attend_back",
    )(lens, valid, q, k, v, do, o, lse, ht, *extra)
    return out[:6], out[6:]


def input_kernel(passed, dq_ref, dk_ref, dv_ref, w_ref, x_ref, dx1_ref, vec_ref, *refs):
    dx_ref, sums_ref = refs[len(refs) - 2 - passed :][:2]
    i = pl.program_id(0)
    dh = dot_nt(dq_ref[...], w_ref[:, :D]) + dot_nt(dk_ref[...], w_ref[:, D : 2 * D]) + dot_nt(dv_ref[...], w_ref[:, 2 * D :])
    normed, scale = norm_parts(x_ref[...])
    dx_ref[...] = dx1_ref[...] + norm_back(dh, normed, scale, vec_ref[0:1])
    sums = jnp.concatenate([col_sum(dh * normed), col_sum(dh), jnp.zeros((6, D), f32)], axis=0)

    @pl.when(i == 0)
    def _():
        sums_ref[...] = sums

    @pl.when(i > 0)
    def _():
        sums_ref[...] += sums


def input_call(dq, dk, dv, w, x, dx1, vec, passed=(), tokens=()):
    tok = pl.BlockSpec((TILE, D), lambda i: (i, 0))
    extra = list(passed) + list(tokens)
    out = pl.pallas_call(
        functools.partial(input_kernel, len(passed)),
        grid=(ROWS // TILE,),
        in_specs=[tok, tok, tok, whole((D, 3 * D)), tok, tok, whole((16, D))] + [ANY] * len(extra),
        out_specs=[tok, whole((8, D))] + [ANY] * len(passed),
        out_shape=[jax.ShapeDtypeStruct((ROWS, D), f32), jax.ShapeDtypeStruct((8, D), f32)]
        + [jax.ShapeDtypeStruct(p.shape, p.dtype) for p in passed],
        input_output_aliases={7 + n: 2 + n for n in range(len(passed))},
        compiler_params=params(),
        cost_estimate=cost(13),
        name="input_back",
    )(dq, dk, dv, w, x, dx1, vec, *extra)
    return out[:2], out[2:]


def swap_cores(x):
    return lax.ppermute(x, "c", [(0, 1), (1, 0)])


def from_peer(x, axes, k):
    return lax.ppermute(x, axes, [(i, i ^ k) for i in range(lax.axis_size(axes))])


def gate_kernel(*refs):
    del refs


def gate(arrays, tokens):
    out = pl.pallas_call(
        gate_kernel,
        in_specs=[ANY] * (len(arrays) + len(tokens)),
        out_specs=[ANY] * len(arrays),
        out_shape=[jax.ShapeDtypeStruct(a.shape, a.dtype) for a in arrays],
        input_output_aliases={n: n for n in range(len(arrays))},
        name="gate",
    )(*arrays, *tokens)
    return list(out)


def own_order(rows):
    place = jnp.arange(D, dtype=jnp.int32)
    k, rest = place % rows, place // rows
    na, nb, nf = lax.axis_size("a"), lax.axis_size("b"), lax.axis_size("f")
    a, rest = rest % na ^ lax.axis_index("a"), rest // na
    f, rest = rest % nf ^ lax.axis_index("f"), rest // nf
    b, c = rest % nb ^ lax.axis_index("b"), rest // nb ^ lax.axis_index("c")
    return (((a * nb + b) * nf + f) * 2 + c) * rows + k


def line(shard):
    return [shard] + [from_peer(shard, "a", k) for k in range(1, lax.axis_size("a"))]


def spread(shard, axis):
    return lax.all_to_all(jnp.broadcast_to(shard[None], (lax.axis_size(axis),) + shard.shape), axis, 0, 0)


def gather_plane(stack):
    return [stack] + [from_peer(stack, ("b", "f"), k) for k in range(1, lax.axis_size(("b", "f")))]


def by_owner(parts, order, natural_line=False):
    if natural_line:
        index = jnp.arange(lax.axis_size("a")) ^ lax.axis_index("a")
        parts = [jnp.take(p, index, axis=0) for p in parts]
    return jnp.take(jnp.concatenate(parts, axis=0), jnp.argsort(order), axis=0)


def add(terms):
    total = 0.0
    for array, low, high in terms:
        total = total + array[low:high].astype(f32)
    return total


def plain(arrays):
    return [(g, 0, g.shape[0]) for g in arrays]


def exchange(terms, axes):
    count = lax.axis_size(axes)
    size = (terms[0][2] - terms[0][1]) // count

    def block(k):
        return [(t, low + k * size, low + (k + 1) * size) for t, low, _ in terms]

    return block(0), [from_peer(add(block(k)).astype(bf16), axes, k) for k in range(1, count)]


def hold(terms, array):
    return [(array,) + terms[0][1:]] + terms[1:]


def shards(inputs, img_lens, valid_rows, w_qkv, w_proj, w_fc1, b_fc1, w_fc2, vectors, cotangent):
    devices = lax.axis_size(ALL)
    rows = D // devices
    slots = rows * BLK
    na, nb, nf = lax.axis_size("a"), lax.axis_size("b"), lax.axis_size("f")
    direct = na == STEPS and rows % 8 == 0
    me = jnp.stack([lax.axis_index("a"), lax.axis_index(("b", "f")), lax.axis_index("c")]).astype(jnp.int32)
    small = jnp.concatenate([vectors, b_fc1])
    small = jnp.pad(small, (0, slots - small.shape[0])).reshape(rows, BLK)
    head = jnp.concatenate([w_qkv.reshape(rows, 3 * D), small], axis=1).astype(bf16)
    wide = [w_fc1.reshape(rows, 4, D), w_proj.reshape(rows, 1, D)]
    wide = jnp.concatenate([jnp.swapaxes(t.astype(bf16), 0, 1) for t in wide], axis=0)
    tall = w_fc2.reshape(4 * rows, D).astype(bf16)

    order = own_order(rows)
    owners = order[::rows] // rows
    turn = (jnp.arange(D, dtype=jnp.int32)[:, None] == order[None, :]).astype(bf16)
    head = line(head)
    small = gather_plane(jnp.stack([t[:, 3 * D :] for t in head]))
    head = jnp.stack([t[:, : 3 * D] for t in head])
    head_parts = gather_plane(head)
    (wide,) = gate([wide], small[1:2])
    wide = spread(wide, "a")
    (tall,) = gate([tall], [wide])
    tall = spread(tall, "a")
    small = jnp.concatenate(small, axis=0).reshape(-1, BLK)
    small = jnp.concatenate([small, swap_cores(small)], axis=0)
    small = jnp.dot(turn, small, preferred_element_type=f32).reshape(devices, slots)
    nvec = vectors.shape[0]
    vec = jnp.pad(small[:, :nvec].reshape(10, D), ((0, 6), (0, 0)))
    b1 = small[:, nvec : nvec + b_fc1.shape[0]].reshape(1, FF)
    (wide,) = gate([wide], head_parts[1:])
    wide_parts = gather_plane(wide)
    head_parts = head_parts + [swap_cores(p) for p in head_parts]
    if not direct:
        head_parts = [by_owner(head_parts, owners).reshape(-1, D // 32, 3 * D)]
    (q, k, v, h1t, wqkv, o, lse), _ = attend_call(img_lens, valid_rows, me, head_parts, inputs, turn, vec)
    *wide_parts, tall = gate(wide_parts + [tall], [o])
    tall_parts = gather_plane(tall)
    wide_parts = wide_parts + [swap_cores(p) for p in wide_parts]
    if not direct:
        wide_parts = [jnp.swapaxes(by_owner(wide_parts, owners, True), 0, 1).reshape(5, 32, D // 32, D)]
    x1, a, h2t, ot, dz, wp, w1, m, gp, *dw2 = up_call(me, o, inputs, cotangent, turn, vec, b1, wide_parts)
    if direct:
        keep2, away2 = [g.reshape(FF // 2, D) for g in dw2]
    else:
        dw2 = jnp.take(dw2[0].reshape(devices, 4 * rows, D), owners, axis=0).reshape(FF, D)
        keep2, away2 = dw2[: FF // 2], dw2[FF // 2 :]
    tall_parts = tall_parts + [swap_cores(p) for p in tall_parts]
    if not direct:
        tall_parts = [by_owner(tall_parts, owners, True).reshape(STEPS, 8, D // 8, D)]

    bf = ("b", "f")
    core2 = swap_cores(gate([away2], tall_parts[1 : len(tall_parts) // 2])[0])
    up2, up2_got = exchange(plain([keep2, core2]), bf)
    result, dx1, do, keep, away, db1, sums2, keep2 = down_call(
        me, m, gp, dz, h2t, w1, tall_parts, x1, cotangent, a, ot, wp, vec, passed=keep2, tokens=[core2]
    )
    core = swap_cores(gate([away], up2_got)[0])
    up2, up2_last = exchange(hold(up2, keep2) + plain(up2_got), "a")
    mid, mid_got = exchange(plain([keep, core]), bf)

    (dq, dk, dv, keep1, away1, sums_a), (keep, keep2) = back_call(
        img_lens, valid_rows, q, k, v, do, o, lse, h1t, passed=[keep, keep2], tokens=[core]
    )
    core1 = swap_cores(gate([away1], mid_got + up2_last)[0])
    mid, mid_last = exchange(hold(mid, keep) + plain(mid_got), "a")
    second, second_got = exchange(plain([keep1, core1]), bf)

    (d_input, sums0), (keep, keep1, keep2) = input_call(
        dq, dk, dv, wqkv, inputs, dx1, vec, passed=[keep, keep1, keep2], tokens=[core1]
    )
    g_fc2 = add(hold(up2, keep2) + plain(up2_last))
    sums0, sums_a, sums2, db1 = gate([sums0, sums_a, sums2, db1], second_got + mid_last)
    second, second_last = exchange(hold(second, keep1) + plain(second_got), "a")
    gvec = jnp.concatenate([sums0[:2], sums_a[:2], sums2[:6]], axis=0).reshape(devices, nvec)
    gsmall = jnp.concatenate([gvec, db1.reshape(devices, b_fc1.shape[0])], axis=1)
    gsmall = jnp.pad(gsmall, ((0, 0), (0, -gsmall.shape[1] % BLK))).astype(bf16)
    gsmall = lax.all_to_all(gsmall.reshape(devices, 1, -1), ALL, 0, 0)
    gsmall = jnp.sum(gsmall.astype(f32), axis=0).reshape(-1)

    g_mid = add(hold(mid, keep) + plain(mid_last))
    g_fc1, g_proj = g_mid[:, :FF], g_mid[:, FF:]
    g_qkv = add(second + plain(second_last))
    return (
        result,
        d_input,
        g_qkv.reshape(-1),
        g_proj.reshape(-1),
        g_fc1.reshape(-1),
        gsmall[nvec : nvec + b_fc1.shape[0]],
        g_fc2.reshape(-1),
        gsmall[:nvec],
    )


def solution(mesh):
    dp, fsdp = mesh.shape["dp"], mesh.shape["fsdp"]
    fine = Mesh(mesh.devices.reshape(dp // 2, 2, fsdp // 2, 2), ALL)
    rows, flat = P(ALL, None), P(ALL)
    return jax.shard_map(
        shards,
        mesh=fine,
        in_specs=(rows, rows, flat, flat, flat, flat, flat, flat, flat, rows),
        out_specs=(rows, rows, flat, flat, flat, flat, flat, flat),
        check_vma=False,
    )
```

time: 329 us -> 289 us (0.88)
  Pallas kernels: 161 us -> 130 us
  waiting for transfers between devices: 65.5 us -> 45.1 us
  starting transfers between devices: 45 us -> 59.1 us
  between operations: 15.8 us -> 2.35 us
  local copies, waits for them, and re-layouts: 16.8 us -> 25.6 us
    pallas_call x9 -> x12, Pallas kernels: 147 us -> 120 us  [the longest x1 37.4 us: down_call(): pl.pallas_call(functools.partial(down_kernel, count), grid=(STEPS + ROWS...]
    all_gather x1 -> x0, waiting for transfers between devices: 20.8 us -> none  [shards(): mlp = join_owners(lax.all_gather(mlp, ALL, axis=0), rows)]
    all_to_all x0 -> x3, starting transfers between devices: none -> 12.4 us  [the longest x2 7.75 us: spread(): lax.all_to_all(jnp.broadcast_to(shard[None], (lax.axis_size(axis),) + sha...]
    unnamed x95 -> x111, local copies, waits for them, and re-layouts: 6.68 us -> 13.1 us
    ppermute x30 -> x33, waiting for transfers between devices: 39.9 us -> 39.1 us  [from_peer(): lax.ppermute(x, axes, [(i, i ^ k) for i in range(lax.axis_size(axes))])]
    convert_element_type x8 -> x6, other arithmetic: 11.4 us -> 10.9 us  [exchange(): add(block(k)).astype(bf16)]
    ppermute x30 -> x33, starting transfers between devices: 44 us -> 44 us  [from_peer(): lax.ppermute(x, axes, [(i, i ^ k) for i in range(lax.axis_size(axes))])]
  transfers between devices with their start and end apart: 39 -> 52, of which waited for: 14 -> 12; matrix products, arithmetic and copies ran while one was open for 7% -> 9% of each run, Pallas kernels for 38% -> 46%
where the time goes in v1:
time: 289 us; the launch traced here: 285 us
  Pallas kernels  130 us (45%)
  starting transfers between devices  59.1 us (20%)
  waiting for transfers between devices  45.1 us (16%)
  local copies, waits for them, and re-layouts  25.6 us (9%)
  other arithmetic  22 us (8%)
    ppermute x33, starting transfers between devices, from_peer(): lax.ppermute(x, axes, [(i, i ^ k) for i in range(lax.axis_size(axes))])  44 us
    ppermute x33, waiting for transfers between devices, from_peer(): lax.ppermute(x, axes, [(i, i ^ k) for i in range(lax.axis_size(axes))])  39.1 us
    pallas_call x1, Pallas kernels, down_call(): pl.pallas_call(functools.partial(down_kernel, count), grid=(STEPS + ROWS...  37.4 us
    pallas_call x1, Pallas kernels, up_call(): pl.pallas_call(functools.partial(up_kernel, count), grid_spec=pltpu.Prefe...  29.8 us
    pallas_call x1, Pallas kernels, back_call(): pl.pallas_call(functools.partial(back_kernel, len(passed)), grid=(steps +...  29.1 us
    pallas_call x1, Pallas kernels, attend_call(): pl.pallas_call(functools.partial(attend_kernel, count, len(passed)), grid...  23.4 us
    unnamed x111, local copies, waits for them, and re-layouts  13.1 us
    convert_element_type x6, other arithmetic, exchange(): add(block(k)).astype(bf16)  10.9 us
  transfers between devices with their start and end apart: 52, of which 12 were waited for; matrix products, arithmetic and copies ran while one was open for 9% of the time, Pallas kernels for 46%

profile of v1, /device:TPU:0, one launch (start us, length us, event | category | flops | bytes accessed | tf_op | source)
XLA Modules:
  0.0 285.0 jit_solution(17997150251206866693)
XLA Ops:
  2.1 0.9 convert.37
  3.3 5.1 %collective-permute-start.2 = (bf16[24,2432]{1,0:T(8,128)(2,1)S(1)}, bf16[24,2432]{1,0:T(8,128)(2,1)S(1)}, u32[]{:S(2)}, u32[]{:S(2)}) collective-permute-start(bf16[24,2432]{1,0:T(8,128)(2,1)S(1)} %pad_maximum_fusion.2), channel_id=1, source_target_pairs={{0,24},{8,16},{16,8},{24,0},{1,25},{9,17},{17,9},{25,1},{2,26},{10... | collective-permute-start | bytes 350216 | tf_op jit(solution)/shard_map/ppermute | solution.py:689
  9.3 1.4 fusion.1.refs_9_.turn_ref
  13.1 5.1 %collective-permute-done.1 = bf16[24,2432]{1,0:T(8,128)(2,1)S(1)} collective-permute-done((bf16[24,2432]{1,0:T(8,128)(2,1)S(1)}, bf16[24,2432]{1,0:T(8,128)(2,1)S(1)}, u32[]{:S(2)}, u32[]{:S(2)}) %collective-permute-start.1) | collective-permute-done | bytes 116768 | tf_op jit(solution)/shard_map/ppermute | solution.py:689
  18.2 1.6 collective-permute-start.10
  19.8 1.5 collective-permute-start.11
  21.9 1.6 collective-permute-start.3
  23.5 1.5 collective-permute-start.4
  25.6 1.8 broadcast_in_dim.4
  27.5 3.7 %all-to-all-start = ((bf16[4,5,24,768]{3,2,1,0:T(8,128)(2,1)}), bf16[4,5,24,768]{3,2,1,0:T(8,128)(2,1)S(1)}, u32[]{:S(2)}, u32[]{:S(2)}) async-start(bf16[4,5,24,768]{3,2,1,0:T(8,128)(2,1)} %broadcast_in_dim.4), calls=%async_computation | async-start | bytes 1474560 | tf_op jit(solution)/shard_map/all_to_all | solution.py:723
  31.4 3.4 %collective-permute-done.3.refs_1_ = bf16[4,24,2304]{2,1,0:T(8,128)(2,1)S(1)} collective-permute-done((bf16[4,24,2304]{2,1,0:T(8,128)(2,1)S(1)}, bf16[4,24,2304]{2,1,0:T(8,128)(2,1)S(1)}, u32[]{:S(2)}, u32[]{:S(2)}) %collective-permute-start.3) | collective-permute-done | bytes 442400 | tf_op jit(solution)/shard_map/ppermute | solution.py:689
  34.7 2.0 collective-permute-done.4.refs_2_
  36.7 6.7 %collective-permute-done.5.refs_3_ = bf16[4,24,2304]{2,1,0:T(8,128)(2,1)} collective-permute-done((bf16[4,24,2304]{2,1,0:T(8,128)(2,1)S(1)}, bf16[4,24,2304]{2,1,0:T(8,128)(2,1)}, u32[]{:S(2)}, u32[]{:S(2)}) %collective-permute-start.5) | collective-permute-done | bytes 442400 | tf_op jit(solution)/shard_map/ppermute | solution.py:689
  46.7 1.5 all-to-all-done.refs_0_.refs_1_
  48.2 0.9 copy-done
  49.1 1.2 collective-permute-start.14
  50.3 0.9 broadcast_in_dim.5
  51.2 4.0 %all-to-all-start.1 = ((bf16[4,96,768]{2,1,0:T(8,128)(2,1)}), bf16[4,96,768]{2,1,0:T(8,128)(2,1)S(1)}, u32[]{:S(2)}, u32[]{:S(2)}) async-start(bf16[4,96,768]{2,1,0:T(8,128)(2,1)} %broadcast_in_dim.5), calls=%async_computation.1 | async-start | bytes 1179648 | tf_op jit(solution)/shard_map/all_to_all | solution.py:723
  55.2 1.6 collective-permute-start.15
  57.6 23.4 %attend.1 = (bf16[1024,768]{1,0:T(8,128)(2,1)}, bf16[1024,768]{1,0:T(8,128)(2,1)}, bf16[1024,768]{1,0:T(8,128)(2,1)}, bf16[768,1024]{1,0:T(8,128)(2,1)}, bf16[76...) custom-call(s32[1,12]{1,0:T(1,128)} %lens_ref.3, s32[1]{0:T(128)S(6)} %copy.74.valid_ref, ...), custom_call_target="tpu_custom_call" | custom-call | flops 27499999232 | bytes 75000000 | tf_op jit(solution)/shard_map/attend/pallas_call | solution.py:213
  81.0 7.7 %collective-permute-done.16.refs_3_ = bf16[4,5,24,768]{3,2,1,0:T(8,128)(2,1)S(1)} collective-permute-done((bf16[4,5,24,768]{3,2,1,0:T(8,128)(2,1)S(1)}, bf16[4,5,24,768]{3,2,1,0:T(8,128)(2,1)S(1)}, u32[]{:S(2)}, u32[]{:S(2)}) %collective-permute-start.16) | collective-permute-done | bytes 737312 | tf_op jit(solution)/shard_map/ppermute | solution.py:689
  88.8 0.9 copy-done.22
  90.9 0.8 slice.395
  92.4 0.9 collective-permute-start.21
  93.3 1.2 collective-permute-start.22
  94.6 1.4 collective-permute-start.23
  96.0 0.9 copy-done.46
  96.9 29.8 %mlp_up.1 = (f32[1024,768]{1,0:T(8,128)}, bf16[1024,768]{1,0:T(8,128)(2,1)}, bf16[768,1024]{1,0:T(8,128)(2,1)}, bf16[768,1024]{1,0:T(8,128)(2,1)}, bf16[1024,768...) custom-call(s32[3]{0:T(128)} %pad_add_fusion.me_ref, ...), custom_call_target="tpu_custom_call" | custom-call | flops 28600000512 | bytes 78000000 | tf_op jit(solution)/shard_map/mlp_up/pallas_call | solution.py:363
  127.9 1.1 copy-done.8
  130.1 2.5 collective-permute-done.28.refs_9_
  134.1 1.1 collective-permute-start.29
  135.2 0.9 collective-permute-start.30
  136.1 1.4 collective-permute-start.31
  138.4 0.8 copy-done.50
  139.2 37.4 %mlp_down.1 = (f32[1024,768]{1,0:T(8,128)}, f32[1024,768]{1,0:T(8,128)}, bf16[1024,768]{1,0:T(8,128)(2,1)}, bf16[384,3840]{1,0:T(8,128)(2,1)}, bf16[384,3840]{1,...) custom-call(s32[3]{0:T(128)} %pad_add_fusion.me_ref, ...), custom_call_target="tpu_custom_call", output_to_operand_aliasing={{7}: (21, {})} | custom-call | flops 38499999744 | bytes 105000000 | tf_op jit(solution)/shard_map/mlp_down/pallas_call | solution.py:484
  176.7 0.8 copy-done.12
  178.3 2.1 add_convert_fusion.9
  180.4 1.8 collective-permute-start.36
  182.2 2.3 collective-permute-start.37
  184.9 2.0 add_convert_fusion
  187.1 1.1 collective-permute-start.33
  188.2 0.9 collective-permute-start.34
  189.2 1.4 collective-permute-start.35
  190.6 29.1 %attend_back.1 = (bf16[1024,768]{1,0:T(8,128)(2,1)}, bf16[1024,768]{1,0:T(8,128)(2,1)}, bf16[1024,768]{1,0:T(8,128)(2,1)}, bf16[384,2304]{1,0:T(8,128)(2,1)}, bf...) custom-call(s32[1,12]{1,0:T(1,128)} %lens_ref.3, ...), custom_call_target="tpu_custom_call", output_to_operand_aliasing={{6}: (9, {}), {7}: (10, {})} | custom-call | flops 36300001280 | bytes 99000000 | tf_op jit(solution)/shard_map/attend_back/pallas_call | solution.py:609
  219.8 2.4 collective-permute-done.35.refs_3_
  222.3 0.9 copy-done.4
  223.2 3.0 %add_convert_fusion.8 = (bf16[24,3840]{1,0:T(8,128)(2,1)}, bf16[24,3840]{1,0:T(8,128)(2,1)}, bf16[24,3840]{1,0:T(8,128)(2,1)}) fusion(bf16[96,3840]{1,0:T(8,128)(2,1)} %copy-done.4, bf16[96,3840]{1,0:T(8,128)(2,1)} %copy-done.3, bf16[96,3840]{1,0:T(8,128)(2,1)} %copy-done.2, bf16[384,3840]{1,0:T(8,128)(2,1)} %copy-done.5, ...), kind=kLoop, calls=%fused_computation.20 | loop fusion | flops 2764800 | bytes 3317760 | tf_op jit(solution)/shard_map/convert_element_type | solution.py:755
  226.2 1.4 collective-permute-start.46
  227.6 2.7 collective-permute-start.47
  230.6 1.5 add_convert_fusion.5
  232.3 1.1 collective-permute-start.40
  233.4 0.9 collective-permute-start.41
  234.4 10.7 %input_back.1 = (f32[1024,768]{1,0:T(8,128)}, f32[8,768]{1,0:T(8,128)}, bf16[384,3840]{1,0:T(8,128)(2,1)}, bf16[384,2304]{1,0:T(8,128)(2,1)}, bf16[1536,768]{1,0:T(8,128)(2,1)}) custom-call(bf16[1024,768]{1,0:T(8,128)(2,1)} %get-tuple-element.83.dq_ref, ...), custom_call_target="tpu_custom_call", output_to_operand_aliasing={{2}: (7, {}), {3}: (8, {}), {4}: (9, {})} | custom-call | flops 14300000256 | bytes 39000000 | tf_op jit(solution)/shard_map/input_back/pallas_call | solution.py:669
  245.1 1.5 collective-permute-start.42
  246.6 1.6 convert_add_fusion.3
  248.2 1.4 convert_add_fusion.4
  251.8 5.3 %collective-permute-done.42.refs_6_ = bf16[96,2304]{1,0:T(8,128)(2,1)S(1)} collective-permute-done((bf16[96,2304]{1,0:T(8,128)(2,1)S(1)}, bf16[96,2304]{1,0:T(8,128)(2,1)S(1)}, u32[]{:S(2)}, u32[]{:S(2)}) %collective-permute-start.42) | collective-permute-done | bytes 442400 | tf_op jit(solution)/shard_map/ppermute | solution.py:689
  263.0 4.7 %all-to-all-start.2 = ((bf16[32,2,192]{2,1,0:T(2,128)(2,1)}), bf16[32,2,192]{2,1,0:T(2,128)(2,1)S(1)}, u32[]{:S(2)}, u32[]{:S(2)}) async-start(bf16[32,2,192]{2,1,0:T(2,128)(2,1)} %reshape.227), calls=%async_computation.2 | async-start | bytes 65536 | tf_op jit(solution)/shard_map/all_to_all | solution.py:840
  267.7 1.7 add_convert_fusion.14
  269.4 1.8 collective-permute-start.43
  271.2 2.4 collective-permute-start.44
  273.8 1.1 all-to-all-done.2
  276.3 6.5 %collective-permute-done.44 = bf16[24,2304]{1,0:T(8,128)(2,1)S(1)} collective-permute-done((bf16[24,2304]{1,0:T(8,128)(2,1)S(1)}, bf16[24,2304]{1,0:T(8,128)(2,1)S(1)}, u32[]{:S(2)}, u32[]{:S(2)}) %collective-permute-start.44) | collective-permute-done | bytes 110624 | tf_op jit(solution)/shard_map/ppermute | solution.py:689
  282.8 1.2 convert_add_fusion.5
  (229 shorter events, 28.5 us)
Async XLA Ops:
  0.6 10.7 %copy-start.39 = (f32[73728]{0:T(1024)S(1)}, f32[73728]{0:T(1024)}, u32[]{:S(2)}) copy-start(f32[73728]{0:T(1024)} %param.15) | copy-start | bytes 884740
  0.6 10.9 %copy-start.43 = (f32[18432]{0:T(1024)S(1)}, f32[18432]{0:T(1024)}, u32[]{:S(2)}) copy-start(f32[18432]{0:T(1024)} %param.14) | copy-start | bytes 221188
  0.7 10.9 %copy-start.40 = (f32[73728]{0:T(1024)S(1)}, f32[73728]{0:T(1024)}, u32[]{:S(2)}) copy-start(f32[73728]{0:T(1024)} %param.17) | copy-start | bytes 884740
  3.3 9.9 %collective-permute-start.2 = (bf16[24,2432]{1,0:T(8,128)(2,1)S(1)}, bf16[24,2432]{1,0:T(8,128)(2,1)S(1)}, u32[]{:S(2)}, u32[]{:S(2)}) collective-permute-start(bf16[24,2432]{1,0:T(8,128)(2,1)S(1)} %pad_maximum_fusion.2), channel_id=1, source_target_pairs={{0,24},{8,16},{16,8},{24,0},{1,25},{9,17},{17,9},{25,1},{2,26},{10... | collective-permute-start | bytes 350216 | tf_op jit(solution)/shard_map/ppermute | solution.py:689
  8.4 9.8 %collective-permute-start.1 = (bf16[24,2432]{1,0:T(8,128)(2,1)S(1)}, bf16[24,2432]{1,0:T(8,128)(2,1)S(1)}, u32[]{:S(2)}, u32[]{:S(2)}) collective-permute-start(bf16[24,2432]{1,0:T(8,128)(2,1)S(1)} %pad_maximum_fusion.2), channel_id=1, source_target_pairs={{0,16},{8,24},{16,0},{24,8},{1,17},{9,25},{17,1},{25,9},{2,18},{10... | collective-permute-start | bytes 350216 | tf_op jit(solution)/shard_map/ppermute | solution.py:689
  8.4 9.8 %collective-permute-start = (bf16[24,2432]{1,0:T(8,128)(2,1)S(1)}, bf16[24,2432]{1,0:T(8,128)(2,1)S(1)}, u32[]{:S(2)}, u32[]{:S(2)}) collective-permute-start(bf16[24,2432]{1,0:T(8,128)(2,1)S(1)} %pad_maximum_fusion.2), channel_id=1, source_target_pairs={{0,8},{8,0},{16,24},{24,16},{1,9},{9,1},{17,25},{25,17},{2,10},{10... | collective-permute-start | bytes 350216 | tf_op jit(solution)/shard_map/ppermute | solution.py:689
  18.2 6.8 %collective-permute-start.10 = (bf16[4,24,128]{2,1,0:T(8,128)(2,1)S(1)}, bf16[4,24,128]{2,1,0:T(8,128)(2,1)S(1)}, u32[]{:S(2)}, u32[]{:S(2)}) collective-permute-start(bf16[4,24,128]{2,1,0:T(8,128)(2,1)S(1)} %pad_maximum_fusion.3), channel_id=1, source_target_pairs={{0,2},{2,0},{4,6},{6,4},{1,3},{3,1},{5,7},{7,5},{8,10},{10,8},{12,... | collective-permute-start | bytes 73736 | tf_op jit(solution)/shard_map/ppermute | solution.py:689
  19.8 11.4 %collective-permute-start.11 = (bf16[4,24,128]{2,1,0:T(8,128)(2,1)S(1)}, bf16[4,24,128]{2,1,0:T(8,128)(2,1)S(1)}, u32[]{:S(2)}, u32[]{:S(2)}) collective-permute-start(bf16[4,24,128]{2,1,0:T(8,128)(2,1)S(1)} %pad_maximum_fusion.3), channel_id=1, source_target_pairs={{0,4},{2,6},{4,0},{6,2},{1,5},{3,7},{5,1},{7,3},{8,12},{10,14},{12... | collective-permute-start | bytes 73736 | tf_op jit(solution)/shard_map/ppermute | solution.py:689
  21.3 22.1 %collective-permute-start.12 = (bf16[4,24,128]{2,1,0:T(8,128)(2,1)S(1)}, bf16[4,24,128]{2,1,0:T(8,128)(2,1)S(1)}, u32[]{:S(2)}, u32[]{:S(2)}) collective-permute-start(bf16[4,24,128]{2,1,0:T(8,128)(2,1)S(1)} %pad_maximum_fusion.3), channel_id=1, source_target_pairs={{0,6},{2,4},{4,2},{6,0},{1,7},{3,5},{5,3},{7,1},{8,14},{10,12},{12... | collective-permute-start | bytes 73736 | tf_op jit(solution)/shard_map/ppermute | solution.py:689
  21.9 23.9 %copy-start.36 = (bf16[4,24,2304]{2,1,0:T(8,128)(2,1)}, bf16[4,24,2304]{2,1,0:T(8,128)(2,1)S(1)}, u32[]{:S(2)}) copy-start(bf16[4,24,2304]{2,1,0:T(8,128)(2,1)S(1)} %pad_maximum_fusion.refs_0_) | copy-start | bytes 1327108
  21.9 12.8 %collective-permute-start.3 = (bf16[4,24,2304]{2,1,0:T(8,128)(2,1)S(1)}, bf16[4,24,2304]{2,1,0:T(8,128)(2,1)S(1)}, u32[]{:S(2)}, u32[]{:S(2)}) collective-permute-start(bf16[4,24,2304]{2,1,0:T(8,128)(2,1)S(1)} %pad_maximum_fusion.refs_0_), channel_id=1, source_target_pairs={{0,2},{2,0},{4,6},{6,4},{1,3},{3,1},{5,7},{7,5},{8,10},{10,8},{12,... | collective-permute-start | bytes 1327112 | tf_op jit(solution)/shard_map/ppermute | solution.py:689
  23.5 13.2 %collective-permute-start.4 = (bf16[4,24,2304]{2,1,0:T(8,128)(2,1)S(1)}, bf16[4,24,2304]{2,1,0:T(8,128)(2,1)}, u32[]{:S(2)}, u32[]{:S(2)}) collective-permute-start(bf16[4,24,2304]{2,1,0:T(8,128)(2,1)S(1)} %pad_maximum_fusion.refs_0_), channel_id=1, source_target_pairs={{0,4},{2,6},{4,0},{6,2},{1,5},{3,7},{5,1},{7,3},{8,12},{10,14},{12... | collective-permute-start | bytes 1327112 | tf_op jit(solution)/shard_map/ppermute | solution.py:689
  25.0 18.4 %collective-permute-start.5 = (bf16[4,24,2304]{2,1,0:T(8,128)(2,1)S(1)}, bf16[4,24,2304]{2,1,0:T(8,128)(2,1)}, u32[]{:S(2)}, u32[]{:S(2)}) collective-permute-start(bf16[4,24,2304]{2,1,0:T(8,128)(2,1)S(1)} %pad_maximum_fusion.refs_0_), channel_id=1, source_target_pairs={{0,6},{2,4},{4,2},{6,0},{1,7},{3,5},{5,3},{7,1},{8,14},{10,12},{12... | collective-permute-start | bytes 1327112 | tf_op jit(solution)/shard_map/ppermute | solution.py:689
  27.5 20.7 %all-to-all-start = ((bf16[4,5,24,768]{3,2,1,0:T(8,128)(2,1)}), bf16[4,5,24,768]{3,2,1,0:T(8,128)(2,1)S(1)}, u32[]{:S(2)}, u32[]{:S(2)}) async-start(bf16[4,5,24,768]{3,2,1,0:T(8,128)(2,1)} %broadcast_in_dim.4), calls=%async_computation | async-start | bytes 1474560 | tf_op jit(solution)/shard_map/all_to_all | solution.py:723
  31.3 23.9 %collective-permute-start.6 = (bf16[4,24,2304]{2,1,0:T(8,128)(2,1)S(1)}, bf16[4,24,2304]{2,1,0:T(8,128)(2,1)}, u32[]{:S(2)}, u32[]{:S(2)}) collective-permute-start(bf16[4,24,2304]{2,1,0:T(8,128)(2,1)S(1)} %pad_maximum_fusion.refs_0_), channel_id=1, source_target_pairs={{0,1},{1,0},{2,3},{3,2},{4,5},{5,4},{6,7},{7,6},{8,9},{9,8},{10,11... | collective-permute-start | bytes 1327112 | tf_op jit(solution)/shard_map/ppermute | solution.py:685
  34.7 14.3 %copy-start.37 = (bf16[4,24,2304]{2,1,0:T(8,128)(2,1)}, bf16[4,24,2304]{2,1,0:T(8,128)(2,1)S(1)}, u32[]{:S(2)}) copy-start(bf16[4,24,2304]{2,1,0:T(8,128)(2,1)S(1)} %collective-permute-done.3.refs_1_) | copy-start | bytes 1327108
  34.7 22.0 %collective-permute-start.7 = (bf16[4,24,2304]{2,1,0:T(8,128)(2,1)S(1)}, bf16[4,24,2304]{2,1,0:T(8,128)(2,1)}, u32[]{:S(2)}, u32[]{:S(2)}) collective-permute-start(bf16[4,24,2304]{2,1,0:T(8,128)(2,1)S(1)} %collective-permute-done.3.refs_1_), channel_id=1, source_target_pairs={{0,1},{1,0},{2,3},{3,2},{4,5},{5,4},{6,7},{7,6},{8,9},{9,8},{10,11... | collective-permute-start | bytes 1327112 | tf_op jit(solution)/shard_map/ppermute | solution.py:685
  36.7 20.9 %collective-permute-start.8 = (bf16[4,24,2304]{2,1,0:T(8,128)(2,1)}, bf16[4,24,2304]{2,1,0:T(8,128)(2,1)}, u32[]{:S(2)}, u32[]{:S(2)}) collective-permute-start(bf16[4,24,2304]{2,1,0:T(8,128)(2,1)} %collective-permute-done.4.refs_2_), channel_id=1, source_target_pairs={{0,1},{1,0},{2,3},{3,2},{4,5},{5,4},{6,7},{7,6},{8,9},{9,8},{10,11... | collective-permute-start | bytes 1327112 | tf_op jit(solution)/shard_map/ppermute | solution.py:685
  43.4 14.2 %collective-permute-start.9 = (bf16[4,24,2304]{2,1,0:T(8,128)(2,1)}, bf16[4,24,2304]{2,1,0:T(8,128)(2,1)}, u32[]{:S(2)}, u32[]{:S(2)}) collective-permute-start(bf16[4,24,2304]{2,1,0:T(8,128)(2,1)} %collective-permute-done.5.refs_3_), channel_id=1, source_target_pairs={{0,1},{1,0},{2,3},{3,2},{4,5},{5,4},{6,7},{7,6},{8,9},{9,8},{10,11... | collective-permute-start | bytes 1327112 | tf_op jit(solution)/shard_map/ppermute | solution.py:685
  43.4 1.9 collective-permute-start.13
  49.1 6.1 %copy-start.1 = (bf16[4,5,24,768]{3,2,1,0:T(8,128)(2,1)S(1)}, bf16[4,5,24,768]{3,2,1,0:T(8,128)(2,1)}, u32[]{:S(2)}) copy-start(bf16[4,5,24,768]{3,2,1,0:T(8,128)(2,1)} %gate.9.refs_0_) | copy-start | bytes 2211844
  49.1 31.9 %collective-permute-start.14 = (bf16[4,5,24,768]{3,2,1,0:T(8,128)(2,1)}, bf16[4,5,24,768]{3,2,1,0:T(8,128)(2,1)S(1)}, u32[]{:S(2)}, u32[]{:S(2)}) collective-permute-start(bf16[4,5,24,768]{3,2,1,0:T(8,128)(2,1)} %gate.9.refs_0_), channel_id=1, source_target_pairs={{0,2},{2,0},{4,6},{6,4},{1,3},{3,1},{5,7},{7,5},{8,10},{10,8},{12,... | collective-permute-start | bytes 2211848 | tf_op jit(solution)/shard_map/ppermute | solution.py:689
  51.2 37.6 %all-to-all-start.1 = ((bf16[4,96,768]{2,1,0:T(8,128)(2,1)}), bf16[4,96,768]{2,1,0:T(8,128)(2,1)S(1)}, u32[]{:S(2)}, u32[]{:S(2)}) async-start(bf16[4,96,768]{2,1,0:T(8,128)(2,1)} %broadcast_in_dim.5), calls=%async_computation.1 | async-start | bytes 1179648 | tf_op jit(solution)/shard_map/all_to_all | solution.py:723
  55.2 25.8 %collective-permute-start.15 = (bf16[4,5,24,768]{3,2,1,0:T(8,128)(2,1)S(1)}, bf16[4,5,24,768]{3,2,1,0:T(8,128)(2,1)S(1)}, u32[]{:S(2)}, u32[]{:S(2)}) collective-permute-start(bf16[4,5,24,768]{3,2,1,0:T(8,128)(2,1)S(1)} %copy-done.1), channel_id=1, source_target_pairs={{0,4},{2,6},{4,0},{6,2},{1,5},{3,7},{5,1},{7,3},{8,12},{10,14},{12... | collective-permute-start | bytes 2211848 | tf_op jit(solution)/shard_map/ppermute | solution.py:689
  56.8 32.0 %collective-permute-start.16 = (bf16[4,5,24,768]{3,2,1,0:T(8,128)(2,1)S(1)}, bf16[4,5,24,768]{3,2,1,0:T(8,128)(2,1)S(1)}, u32[]{:S(2)}, u32[]{:S(2)}) collective-permute-start(bf16[4,5,24,768]{3,2,1,0:T(8,128)(2,1)S(1)} %copy-done.1), channel_id=1, source_target_pairs={{0,6},{2,4},{4,2},{6,0},{1,7},{3,5},{5,3},{7,1},{8,14},{10,12},{12... | collective-permute-start | bytes 2211848 | tf_op jit(solution)/shard_map/ppermute | solution.py:689
  81.0 7.7 %copy-start.20 = (bf16[4,5,24,768]{3,2,1,0:T(8,128)(2,1)}, bf16[4,5,24,768]{3,2,1,0:T(8,128)(2,1)S(1)}, u32[]{:S(2)}) copy-start(bf16[4,5,24,768]{3,2,1,0:T(8,128)(2,1)S(1)} %collective-permute-done.14.refs_1_) | copy-start | bytes 2211844
  81.0 7.7 %copy-start.21 = (bf16[4,5,24,768]{3,2,1,0:T(8,128)(2,1)}, bf16[4,5,24,768]{3,2,1,0:T(8,128)(2,1)S(1)}, u32[]{:S(2)}) copy-start(bf16[4,5,24,768]{3,2,1,0:T(8,128)(2,1)S(1)} %collective-permute-done.15.refs_2_) | copy-start | bytes 2211844
  89.9 3.5 %collective-permute-start.17 = (bf16[4,5,24,768]{3,2,1,0:T(8,128)(2,1)}, bf16[4,5,24,768]{3,2,1,0:T(8,128)(2,1)S(1)}, u32[]{:S(2)}, u32[]{:S(2)}) collective-permute-start(bf16[4,5,24,768]{3,2,1,0:T(8,128)(2,1)} %get-tuple-element.57.refs_0_), channel_id=1, source_target_pairs={{0,1},{1,0},{2,3},{3,2},{4,5},{5,4},{6,7},{7,6},{8,9},{9,8},{10,11... | collective-permute-start | bytes 2211848 | tf_op jit(solution)/shard_map/ppermute | solution.py:685
  89.9 4.7 %collective-permute-start.18 = (bf16[4,5,24,768]{3,2,1,0:T(8,128)(2,1)}, bf16[4,5,24,768]{3,2,1,0:T(8,128)(2,1)S(1)}, u32[]{:S(2)}, u32[]{:S(2)}) collective-permute-start(bf16[4,5,24,768]{3,2,1,0:T(8,128)(2,1)} %get-tuple-element.58.refs_1_), channel_id=1, source_target_pairs={{0,1},{1,0},{2,3},{3,2},{4,5},{5,4},{6,7},{7,6},{8,9},{9,8},{10,11... | collective-permute-start | bytes 2211848 | tf_op jit(solution)/shard_map/ppermute | solution.py:685
  90.4 5.6 %collective-permute-start.19 = (bf16[4,5,24,768]{3,2,1,0:T(8,128)(2,1)}, bf16[4,5,24,768]{3,2,1,0:T(8,128)(2,1)S(1)}, u32[]{:S(2)}, u32[]{:S(2)}) collective-permute-start(bf16[4,5,24,768]{3,2,1,0:T(8,128)(2,1)} %get-tuple-element.59.refs_2_), channel_id=1, source_target_pairs={{0,1},{1,0},{2,3},{3,2},{4,5},{5,4},{6,7},{7,6},{8,9},{9,8},{10,11... | collective-permute-start | bytes 2211848 | tf_op jit(solution)/shard_map/ppermute | solution.py:685
  90.4 5.6 %collective-permute-start.20 = (bf16[4,5,24,768]{3,2,1,0:T(8,128)(2,1)}, bf16[4,5,24,768]{3,2,1,0:T(8,128)(2,1)}, u32[]{:S(2)}, u32[]{:S(2)}) collective-permute-start(bf16[4,5,24,768]{3,2,1,0:T(8,128)(2,1)} %get-tuple-element.60.refs_3_), channel_id=1, source_target_pairs={{0,1},{1,0},{2,3},{3,2},{4,5},{5,4},{6,7},{7,6},{8,9},{9,8},{10,11... | collective-permute-start | bytes 2211848 | tf_op jit(solution)/shard_map/ppermute | solution.py:685
  92.4 34.3 %collective-permute-start.21 = (bf16[4,96,768]{2,1,0:T(8,128)(2,1)}, bf16[4,96,768]{2,1,0:T(8,128)(2,1)S(1)}, u32[]{:S(2)}, u32[]{:S(2)}) collective-permute-start(bf16[4,96,768]{2,1,0:T(8,128)(2,1)} %get-tuple-element.70.refs_0_), channel_id=1, source_target_pairs={{0,2},{2,0},{4,6},{6,4},{1,3},{3,1},{5,7},{7,5},{8,10},{10,8},{12,... | collective-permute-start | bytes 1769480 | tf_op jit(solution)/shard_map/ppermute | solution.py:689
  93.3 33.4 %collective-permute-start.22 = (bf16[4,96,768]{2,1,0:T(8,128)(2,1)}, bf16[4,96,768]{2,1,0:T(8,128)(2,1)S(1)}, u32[]{:S(2)}, u32[]{:S(2)}) collective-permute-start(bf16[4,96,768]{2,1,0:T(8,128)(2,1)} %get-tuple-element.70.refs_0_), channel_id=1, source_target_pairs={{0,4},{2,6},{4,0},{6,2},{1,5},{3,7},{5,1},{7,3},{8,12},{10,14},{12... | collective-permute-start | bytes 1769480 | tf_op jit(solution)/shard_map/ppermute | solution.py:689
  94.6 32.2 %collective-permute-start.23 = (bf16[4,96,768]{2,1,0:T(8,128)(2,1)}, bf16[4,96,768]{2,1,0:T(8,128)(2,1)S(1)}, u32[]{:S(2)}, u32[]{:S(2)}) collective-permute-start(bf16[4,96,768]{2,1,0:T(8,128)(2,1)} %get-tuple-element.70.refs_0_), channel_id=1, source_target_pairs={{0,6},{2,4},{4,2},{6,0},{1,7},{3,5},{5,3},{7,1},{8,14},{10,12},{12... | collective-permute-start | bytes 1769480 | tf_op jit(solution)/shard_map/ppermute | solution.py:689
  127.9 4.7 %collective-permute-start.28 = (bf16[1536,768]{1,0:T(8,128)(2,1)}, bf16[1536,768]{1,0:T(8,128)(2,1)S(1)}, u32[]{:S(2)}, u32[]{:S(2)}) collective-permute-start(bf16[1536,768]{1,0:T(8,128)(2,1)} %gate.12), channel_id=1, source_target_pairs={{0,1},{1,0},{2,3},{3,2},{4,5},{5,4},{6,7},{7,6},{8,9},{9,8},{10,11... | collective-permute-start | bytes 7077896 | tf_op jit(solution)/shard_map/ppermute | solution.py:685
  129.0 6.2 %collective-permute-start.24 = (bf16[4,96,768]{2,1,0:T(8,128)(2,1)S(1)}, bf16[4,96,768]{2,1,0:T(8,128)(2,1)S(1)}, u32[]{:S(2)}, u32[]{:S(2)}) collective-permute-start(bf16[4,96,768]{2,1,0:T(8,128)(2,1)S(1)} %copy-done.8), channel_id=1, source_target_pairs={{0,1},{1,0},{2,3},{3,2},{4,5},{5,4},{6,7},{7,6},{8,9},{9,8},{10,11... | collective-permute-start | bytes 1769480 | tf_op jit(solution)/shard_map/ppermute | solution.py:685
  129.0 7.1 %collective-permute-start.25 = (bf16[4,96,768]{2,1,0:T(8,128)(2,1)}, bf16[4,96,768]{2,1,0:T(8,128)(2,1)S(1)}, u32[]{:S(2)}, u32[]{:S(2)}) collective-permute-start(bf16[4,96,768]{2,1,0:T(8,128)(2,1)} %copy-done.26), channel_id=1, source_target_pairs={{0,1},{1,0},{2,3},{3,2},{4,5},{5,4},{6,7},{7,6},{8,9},{9,8},{10,11... | collective-permute-start | bytes 1769480 | tf_op jit(solution)/shard_map/ppermute | solution.py:685
  129.5 8.1 %collective-permute-start.26 = (bf16[4,96,768]{2,1,0:T(8,128)(2,1)}, bf16[4,96,768]{2,1,0:T(8,128)(2,1)S(1)}, u32[]{:S(2)}, u32[]{:S(2)}) collective-permute-start(bf16[4,96,768]{2,1,0:T(8,128)(2,1)} %copy-done.27), channel_id=1, source_target_pairs={{0,1},{1,0},{2,3},{3,2},{4,5},{5,4},{6,7},{7,6},{8,9},{9,8},{10,11... | collective-permute-start | bytes 1769480 | tf_op jit(solution)/shard_map/ppermute | solution.py:685
  129.5 8.1 %collective-permute-start.27 = (bf16[4,96,768]{2,1,0:T(8,128)(2,1)}, bf16[4,96,768]{2,1,0:T(8,128)(2,1)S(1)}, u32[]{:S(2)}, u32[]{:S(2)}) collective-permute-start(bf16[4,96,768]{2,1,0:T(8,128)(2,1)} %copy-done.28), channel_id=1, source_target_pairs={{0,1},{1,0},{2,3},{3,2},{4,5},{5,4},{6,7},{7,6},{8,9},{9,8},{10,11... | collective-permute-start | bytes 1769480 | tf_op jit(solution)/shard_map/ppermute | solution.py:685
  134.1 42.6 %collective-permute-start.29 = (bf16[384,768]{1,0:T(8,128)(2,1)S(1)}, bf16[384,768]{1,0:T(8,128)(2,1)S(1)}, u32[]{:S(2)}, u32[]{:S(2)}) collective-permute-start(bf16[384,768]{1,0:T(8,128)(2,1)S(1)} %get-tuple-element.121), channel_id=1, source_target_pairs={{0,2},{2,0},{4,6},{6,4},{1,3},{3,1},{5,7},{7,5},{8,10},{10,8},{12,... | collective-permute-start | bytes 1769480 | tf_op jit(solution)/shard_map/ppermute | solution.py:689
  135.2 41.5 %collective-permute-start.30 = (bf16[384,768]{1,0:T(8,128)(2,1)S(1)}, bf16[384,768]{1,0:T(8,128)(2,1)S(1)}, u32[]{:S(2)}, u32[]{:S(2)}) collective-permute-start(bf16[384,768]{1,0:T(8,128)(2,1)S(1)} %get-tuple-element.120), channel_id=1, source_target_pairs={{0,4},{2,6},{4,0},{6,2},{1,5},{3,7},{5,1},{7,3},{8,12},{10,14},{12... | collective-permute-start | bytes 1769480 | tf_op jit(solution)/shard_map/ppermute | solution.py:689
  136.1 40.5 %collective-permute-start.31 = (bf16[384,768]{1,0:T(8,128)(2,1)S(1)}, bf16[384,768]{1,0:T(8,128)(2,1)S(1)}, u32[]{:S(2)}, u32[]{:S(2)}) collective-permute-start(bf16[384,768]{1,0:T(8,128)(2,1)S(1)} %get-tuple-element.119), channel_id=1, source_target_pairs={{0,6},{2,4},{4,2},{6,0},{1,7},{3,5},{5,3},{7,1},{8,14},{10,12},{12... | collective-permute-start | bytes 1769480 | tf_op jit(solution)/shard_map/ppermute | solution.py:689
  178.3 6.6 %copy-start.6 = (bf16[384,3840]{1,0:T(8,128)(2,1)S(1)}, bf16[384,3840]{1,0:T(8,128)(2,1)}, u32[]{:S(2)}) copy-start(bf16[384,3840]{1,0:T(8,128)(2,1)} %get-tuple-element.80.refs_0_) | copy-start | bytes 8847364
  178.3 6.5 %collective-permute-start.32 = (bf16[384,3840]{1,0:T(8,128)(2,1)}, bf16[384,3840]{1,0:T(8,128)(2,1)S(1)}, u32[]{:S(2)}, u32[]{:S(2)}) collective-permute-start(bf16[384,3840]{1,0:T(8,128)(2,1)} %gate.13), channel_id=1, source_target_pairs={{0,1},{1,0},{2,3},{3,2},{4,5},{5,4},{6,7},{7,6},{8,9},{9,8},{10,11... | collective-permute-start | bytes 8847368 | tf_op jit(solution)/shard_map/ppermute | solution.py:685
  180.4 8.8 %collective-permute-start.36 = (bf16[96,768]{1,0:T(8,128)(2,1)S(1)}, bf16[96,768]{1,0:T(8,128)(2,1)S(1)}, u32[]{:S(2)}, u32[]{:S(2)}) collective-permute-start(bf16[96,768]{1,0:T(8,128)(2,1)S(1)} %get-tuple-element.109), channel_id=1, source_target_pairs={{0,8},{8,0},{16,24},{24,16},{1,9},{9,1},{17,25},{25,17},{2,10},{10... | collective-permute-start | bytes 442376 | tf_op jit(solution)/shard_map/ppermute | solution.py:689
  182.2 37.5 %collective-permute-start.37 = (bf16[96,768]{1,0:T(8,128)(2,1)S(1)}, bf16[96,768]{1,0:T(8,128)(2,1)S(1)}, u32[]{:S(2)}, u32[]{:S(2)}) collective-permute-start(bf16[96,768]{1,0:T(8,128)(2,1)S(1)} %get-tuple-element.108), channel_id=1, source_target_pairs={{0,16},{8,24},{16,0},{24,8},{1,17},{9,25},{17,1},{25,9},{2,18},{10... | collective-permute-start | bytes 442376 | tf_op jit(solution)/shard_map/ppermute | solution.py:689
  184.6 35.2 %collective-permute-start.38 = (bf16[96,768]{1,0:T(8,128)(2,1)S(1)}, bf16[96,768]{1,0:T(8,128)(2,1)S(1)}, u32[]{:S(2)}, u32[]{:S(2)}) collective-permute-start(bf16[96,768]{1,0:T(8,128)(2,1)S(1)} %get-tuple-element.107), channel_id=1, source_target_pairs={{0,24},{8,16},{16,8},{24,0},{1,25},{9,17},{17,9},{25,1},{2,26},{10... | collective-permute-start | bytes 442376 | tf_op jit(solution)/shard_map/ppermute | solution.py:689
  187.1 32.7 %collective-permute-start.33 = (bf16[96,3840]{1,0:T(8,128)(2,1)}, bf16[96,3840]{1,0:T(8,128)(2,1)S(1)}, u32[]{:S(2)}, u32[]{:S(2)}) collective-permute-start(bf16[96,3840]{1,0:T(8,128)(2,1)} %get-tuple-element.112), channel_id=1, source_target_pairs={{0,2},{2,0},{4,6},{6,4},{1,3},{3,1},{5,7},{7,5},{8,10},{10,8},{12,... | collective-permute-start | bytes 2211848 | tf_op jit(solution)/shard_map/ppermute | solution.py:689
  188.2 31.6 %collective-permute-start.34 = (bf16[96,3840]{1,0:T(8,128)(2,1)}, bf16[96,3840]{1,0:T(8,128)(2,1)S(1)}, u32[]{:S(2)}, u32[]{:S(2)}) collective-permute-start(bf16[96,3840]{1,0:T(8,128)(2,1)} %get-tuple-element.111), channel_id=1, source_target_pairs={{0,4},{2,6},{4,0},{6,2},{1,5},{3,7},{5,1},{7,3},{8,12},{10,14},{12... | collective-permute-start | bytes 2211848 | tf_op jit(solution)/shard_map/ppermute | solution.py:689
  189.2 30.6 %copy-start.29 = (bf16[96,768]{1,0:T(8,128)(2,1)}, bf16[96,768]{1,0:T(8,128)(2,1)S(1)}, u32[]{:S(2)}) copy-start(bf16[96,768]{1,0:T(8,128)(2,1)S(1)} %collective-permute-done.36.refs_4_) | copy-start | bytes 442372
  189.2 33.1 %collective-permute-start.35 = (bf16[96,3840]{1,0:T(8,128)(2,1)}, bf16[96,3840]{1,0:T(8,128)(2,1)S(1)}, u32[]{:S(2)}, u32[]{:S(2)}) collective-permute-start(bf16[96,3840]{1,0:T(8,128)(2,1)} %get-tuple-element.110), channel_id=1, source_target_pairs={{0,6},{2,4},{4,2},{6,0},{1,7},{3,5},{5,3},{7,1},{8,14},{10,12},{12... | collective-permute-start | bytes 2211848 | tf_op jit(solution)/shard_map/ppermute | solution.py:689
  223.2 7.4 %copy-start.15 = (bf16[384,2304]{1,0:T(8,128)(2,1)S(1)}, bf16[384,2304]{1,0:T(8,128)(2,1)}, u32[]{:S(2)}) copy-start(bf16[384,2304]{1,0:T(8,128)(2,1)} %get-tuple-element.89.refs_1_) | copy-start | bytes 5308420
  223.2 7.4 %collective-permute-start.39 = (bf16[384,2304]{1,0:T(8,128)(2,1)}, bf16[384,2304]{1,0:T(8,128)(2,1)S(1)}, u32[]{:S(2)}, u32[]{:S(2)}) collective-permute-start(bf16[384,2304]{1,0:T(8,128)(2,1)} %gate.14), channel_id=1, source_target_pairs={{0,1},{1,0},{2,3},{3,2},{4,5},{5,4},{6,7},{7,6},{8,9},{9,8},{10,11... | collective-permute-start | bytes 5308424 | tf_op jit(solution)/shard_map/ppermute | solution.py:685
  226.2 18.9 %collective-permute-start.46 = (bf16[24,3840]{1,0:T(8,128)(2,1)}, bf16[24,3840]{1,0:T(8,128)(2,1)S(1)}, u32[]{:S(2)}, u32[]{:S(2)}) collective-permute-start(bf16[24,3840]{1,0:T(8,128)(2,1)} %get-tuple-element.104), channel_id=1, source_target_pairs={{0,8},{8,0},{16,24},{24,16},{1,9},{9,1},{17,25},{25,17},{2,10},{10... | collective-permute-start | bytes 552968 | tf_op jit(solution)/shard_map/ppermute | solution.py:689
  227.6 19.0 %collective-permute-start.47 = (bf16[24,3840]{1,0:T(8,128)(2,1)}, bf16[24,3840]{1,0:T(8,128)(2,1)S(1)}, u32[]{:S(2)}, u32[]{:S(2)}) collective-permute-start(bf16[24,3840]{1,0:T(8,128)(2,1)} %get-tuple-element.106), channel_id=1, source_target_pairs={{0,16},{8,24},{16,0},{24,8},{1,17},{9,25},{17,1},{25,9},{2,18},{10... | collective-permute-start | bytes 552968 | tf_op jit(solution)/shard_map/ppermute | solution.py:689
  230.2 16.4 %collective-permute-start.48 = (bf16[24,3840]{1,0:T(8,128)(2,1)}, bf16[24,3840]{1,0:T(8,128)(2,1)S(1)}, u32[]{:S(2)}, u32[]{:S(2)}) collective-permute-start(bf16[24,3840]{1,0:T(8,128)(2,1)} %get-tuple-element.105), channel_id=1, source_target_pairs={{0,24},{8,16},{16,8},{24,0},{1,25},{9,17},{17,9},{25,1},{2,26},{10... | collective-permute-start | bytes 552968 | tf_op jit(solution)/shard_map/ppermute | solution.py:689
  232.3 19.5 %collective-permute-start.40 = (bf16[96,2304]{1,0:T(8,128)(2,1)}, bf16[96,2304]{1,0:T(8,128)(2,1)S(1)}, u32[]{:S(2)}, u32[]{:S(2)}) collective-permute-start(bf16[96,2304]{1,0:T(8,128)(2,1)} %get-tuple-element.116), channel_id=1, source_target_pairs={{0,2},{2,0},{4,6},{6,4},{1,3},{3,1},{5,7},{7,5},{8,10},{10,8},{12,... | collective-permute-start | bytes 1327112 | tf_op jit(solution)/shard_map/ppermute | solution.py:689
  233.4 18.4 %collective-permute-start.41 = (bf16[96,2304]{1,0:T(8,128)(2,1)}, bf16[96,2304]{1,0:T(8,128)(2,1)S(1)}, u32[]{:S(2)}, u32[]{:S(2)}) collective-permute-start(bf16[96,2304]{1,0:T(8,128)(2,1)} %get-tuple-element.118), channel_id=1, source_target_pairs={{0,4},{2,6},{4,0},{6,2},{1,5},{3,7},{5,1},{7,3},{8,12},{10,14},{12... | collective-permute-start | bytes 1327112 | tf_op jit(solution)/shard_map/ppermute | solution.py:689
  234.4 10.7 %copy-start.38 = (bf16[96,2304]{1,0:T(8,128)(2,1)S(1)}, bf16[96,2304]{1,0:T(8,128)(2,1)}, u32[]{:S(2)}) copy-start(bf16[96,2304]{1,0:T(8,128)(2,1)} %get-tuple-element.117) | copy-start | bytes 1327108
  245.1 12.0 %collective-permute-start.42 = (bf16[96,2304]{1,0:T(8,128)(2,1)S(1)}, bf16[96,2304]{1,0:T(8,128)(2,1)S(1)}, u32[]{:S(2)}, u32[]{:S(2)}) collective-permute-start(bf16[96,2304]{1,0:T(8,128)(2,1)S(1)} %copy-done.38), channel_id=1, source_target_pairs={{0,6},{2,4},{4,2},{6,0},{1,7},{3,5},{5,3},{7,1},{8,14},{10,12},{12... | collective-permute-start | bytes 1327112 | tf_op jit(solution)/shard_map/ppermute | solution.py:689
  263.0 11.9 %all-to-all-start.2 = ((bf16[32,2,192]{2,1,0:T(2,128)(2,1)}), bf16[32,2,192]{2,1,0:T(2,128)(2,1)S(1)}, u32[]{:S(2)}, u32[]{:S(2)}) async-start(bf16[32,2,192]{2,1,0:T(2,128)(2,1)} %reshape.227), calls=%async_computation.2 | async-start | bytes 65536 | tf_op jit(solution)/shard_map/all_to_all | solution.py:840
  269.4 6.9 %collective-permute-start.43 = (bf16[24,2304]{1,0:T(8,128)(2,1)S(1)}, bf16[24,2304]{1,0:T(8,128)(2,1)S(1)}, u32[]{:S(2)}, u32[]{:S(2)}) collective-permute-start(bf16[24,2304]{1,0:T(8,128)(2,1)S(1)} %get-tuple-element.113), channel_id=1, source_target_pairs={{0,8},{8,0},{16,24},{24,16},{1,9},{9,1},{17,25},{25,17},{2,10},{10... | collective-permute-start | bytes 331784 | tf_op jit(solution)/shard_map/ppermute | solution.py:689
  271.2 11.6 %collective-permute-start.44 = (bf16[24,2304]{1,0:T(8,128)(2,1)S(1)}, bf16[24,2304]{1,0:T(8,128)(2,1)S(1)}, u32[]{:S(2)}, u32[]{:S(2)}) collective-permute-start(bf16[24,2304]{1,0:T(8,128)(2,1)S(1)} %get-tuple-element.115), channel_id=1, source_target_pairs={{0,16},{8,24},{16,0},{24,8},{1,17},{9,25},{17,1},{25,9},{2,18},{10... | collective-permute-start | bytes 331784 | tf_op jit(solution)/shard_map/ppermute | solution.py:689
  273.6 9.2 %collective-permute-start.45 = (bf16[24,2304]{1,0:T(8,128)(2,1)S(1)}, bf16[24,2304]{1,0:T(8,128)(2,1)S(1)}, u32[]{:S(2)}, u32[]{:S(2)}) collective-permute-start(bf16[24,2304]{1,0:T(8,128)(2,1)S(1)} %get-tuple-element.114), channel_id=1, source_target_pairs={{0,24},{8,16},{16,8},{24,0},{1,25},{9,17},{17,9},{25,1},{2,26},{10... | collective-permute-start | bytes 331784 | tf_op jit(solution)/shard_map/ppermute | solution.py:689
  (39 other events, 76.3 us)

commit v2 on v1

--- a/solution.py
+++ b/solution.py
@@ -42,16 +42,6 @@
     return lax.dot_general(left, right, (((0,), (0,)), ((), ())), preferred_element_type=f32)
 
 
-def eye():
-    rows = lax.broadcasted_iota(jnp.int32, (BLK, BLK), 0)
-    cols = lax.broadcasted_iota(jnp.int32, (BLK, BLK), 1)
-    return (rows == cols).astype(f32).astype(bf16)
-
-
-def flip(one, block):
-    return dot_nt(one, block).astype(bf16)
-
-
 def norm_parts(values):
     center = values - jnp.mean(values, axis=-1, keepdims=True)
     scale = lax.rsqrt(jnp.mean(center * center, axis=-1, keepdims=True) + EPS)
@@ -173,11 +163,7 @@
         for value, ref, scratch in ((q, q_ref, qs), (k, k_ref, ks), (v, v_ref, vs)):
             ref[...] = value
             scratch[rows] = value
-        turned = dot_nn(low, turn_ref[...]).astype(bf16)
-        one = eye()
-        for p in range(PAIRS):
-            s = slice(p * BLK, (p + 1) * BLK)
-            ht_ref[s] = flip(one, turned[:, s])
+        ht_ref[...] = dot_nt(turn_ref[...], low).astype(bf16)
 
     @pl.when(i >= tiles)
     def _():
@@ -301,13 +287,8 @@
         dz = (vec_ref[9:10] * ct_ref[...]).astype(bf16)
         dz_ref[...] = dz
         dzs[rows] = dz
-        one = eye()
-        turned = dot_nn(low, turn_ref[...]).astype(bf16)
-        turned_o = dot_nn(o_ref[...], turn_ref[...]).astype(bf16)
-        for p in range(PAIRS):
-            s = slice(p * BLK, (p + 1) * BLK)
-            ht_ref[s] = flip(one, turned[:, s])
-            ot_ref[s] = flip(one, turned_o[:, s])
+        ht_ref[...] = dot_nt(turn_ref[...], low).astype(bf16)
+        ot_ref[...] = dot_nt(turn_ref[...], o_ref[...]).astype(bf16)
 
     @pl.when(i == tiles)
     def _():
@@ -745,14 +726,19 @@
     return [(g, 0, g.shape[0]) for g in arrays]
 
 
-def exchange(terms, axes):
+def blocks(terms, axes):
     count = lax.axis_size(axes)
     size = (terms[0][2] - terms[0][1]) // count
 
     def block(k):
         return [(t, low + k * size, low + (k + 1) * size) for t, low, _ in terms]
 
-    return block(0), [from_peer(add(block(k)).astype(bf16), axes, k) for k in range(1, count)]
+    return block(0), [add(block(k)).astype(bf16) for k in range(1, count)]
+
+
+def exchange(terms, axes):
+    mine, sends = blocks(terms, axes)
+    return mine, [from_peer(t, axes, k + 1) for k, t in enumerate(sends)]
 
 
 def hold(terms, array):
@@ -775,7 +761,7 @@
 
     order = own_order(rows)
     owners = order[::rows] // rows
-    turn = (jnp.arange(D, dtype=jnp.int32)[:, None] == order[None, :]).astype(bf16)
+    turn = (order[:, None] == jnp.arange(D, dtype=jnp.int32)[None, :]).astype(bf16)
     head = line(head)
     small = gather_plane(jnp.stack([t[:, 3 * D :] for t in head]))
     head = jnp.stack([t[:, : 3 * D] for t in head])
@@ -786,7 +772,7 @@
     tall = spread(tall, "a")
     small = jnp.concatenate(small, axis=0).reshape(-1, BLK)
     small = jnp.concatenate([small, swap_cores(small)], axis=0)
-    small = jnp.dot(turn, small, preferred_element_type=f32).reshape(devices, slots)
+    small = dot_tn(turn, small).reshape(devices, slots)
     nvec = vectors.shape[0]
     vec = jnp.pad(small[:, :nvec].reshape(10, D), ((0, 6), (0, 0)))
     b1 = small[:, nvec : nvec + b_fc1.shape[0]].reshape(1, FF)
@@ -831,9 +817,10 @@
     (d_input, sums0), (keep, keep1, keep2) = input_call(
         dq, dk, dv, wqkv, inputs, dx1, vec, passed=[keep, keep1, keep2], tokens=[core1]
     )
+    second, second_sends = blocks(hold(second, keep1) + plain(second_got), "a")
+    sums0, sums_a, sums2, db1, keep, keep2 = gate([sums0, sums_a, sums2, db1, keep, keep2], second_sends + mid_last)
+    second_last = [from_peer(t, "a", k + 1) for k, t in enumerate(second_sends)]
     g_fc2 = add(hold(up2, keep2) + plain(up2_last))
-    sums0, sums_a, sums2, db1 = gate([sums0, sums_a, sums2, db1], second_got + mid_last)
-    second, second_last = exchange(hold(second, keep1) + plain(second_got), "a")
     gvec = jnp.concatenate([sums0[:2], sums_a[:2], sums2[:6]], axis=0).reshape(devices, nvec)
     gsmall = jnp.concatenate([gvec, db1.reshape(devices, b_fc1.shape[0])], axis=1)
     gsmall = jnp.pad(gsmall, ((0, 0), (0, -gsmall.shape[1] % BLK))).astype(bf16)

time: 289 us -> 285 us (0.986)
    unnamed x111 -> x105, local copies, waits for them, and re-layouts: 13.1 us -> 11.7 us
  transfers between devices with their start and end apart: 52 -> 52, of which waited for: 12 -> 12; matrix products, arithmetic and copies ran while one was open for 9% -> 11% of each run, Pallas kernels for 46% -> 46%
where the time goes in v2:
time: 285 us; the launch traced here: 280 us
  Pallas kernels  129 us (45%)
  starting transfers between devices  57 us (20%)
  waiting for transfers between devices  45.7 us (16%)
  local copies, waits for them, and re-layouts  22.8 us (8%)
  other arithmetic  22.4 us (8%)
    ppermute x33, starting transfers between devices, from_peer(): lax.ppermute(x, axes, [(i, i ^ k) for i in range(lax.axis_size(axes))])  44 us
    pallas_call x1, Pallas kernels, down_call(): pl.pallas_call(functools.partial(down_kernel, count), grid=(STEPS + ROWS...  37.4 us
    ppermute x33, waiting for transfers between devices, from_peer(): lax.ppermute(x, axes, [(i, i ^ k) for i in range(lax.axis_size(axes))])  36.9 us
    pallas_call x1, Pallas kernels, up_call(): pl.pallas_call(functools.partial(up_kernel, count), grid_spec=pltpu.Prefe...  29.2 us
    pallas_call x1, Pallas kernels, back_call(): pl.pallas_call(functools.partial(back_kernel, len(passed)), grid=(steps +...  29.1 us
    pallas_call x1, Pallas kernels, attend_call(): pl.pallas_call(functools.partial(attend_kernel, count, len(passed)), grid...  22.6 us
    convert_element_type x6, other arithmetic, blocks(): return (block(0), [add(block(k)).astype(bf16) for k in range(1, count)])  12.3 us
    unnamed x105, local copies, waits for them, and re-layouts  11.7 us
  transfers between devices with their start and end apart: 52, of which 12 were waited for; matrix products, arithmetic and copies ran while one was open for 11% of the time, Pallas kernels for 46%

profile of v2, /device:TPU:0, one launch (start us, length us, event | category | flops | bytes accessed | tf_op | source)
XLA Modules:
  0.0 280.3 jit_solution(14026066968292196494)
XLA Ops:
  2.1 0.9 convert.37
  3.3 5.1 %collective-permute-start.2 = (bf16[24,2432]{1,0:T(8,128)(2,1)S(1)}, bf16[24,2432]{1,0:T(8,128)(2,1)S(1)}, u32[]{:S(2)}, u32[]{:S(2)}) collective-permute-start(bf16[24,2432]{1,0:T(8,128)(2,1)S(1)} %pad_maximum_fusion.2), channel_id=1, source_target_pairs={{0,24},{8,16},{16,8},{24,0},{1,25},{9,17},{17,9},{25,1},{2,26},{10... | collective-permute-start | bytes 350216 | tf_op jit(solution)/shard_map/ppermute | solution.py:670
  9.3 1.3 fusion.1.refs_9_.turn_ref
  13.0 5.3 %collective-permute-done.1 = bf16[24,2432]{1,0:T(8,128)(2,1)S(1)} collective-permute-done((bf16[24,2432]{1,0:T(8,128)(2,1)S(1)}, bf16[24,2432]{1,0:T(8,128)(2,1)S(1)}, u32[]{:S(2)}, u32[]{:S(2)}) %collective-permute-start.1) | collective-permute-done | bytes 116768 | tf_op jit(solution)/shard_map/ppermute | solution.py:670
  18.2 1.6 collective-permute-start.10
  19.8 1.5 collective-permute-start.11
  21.9 1.6 collective-permute-start.3
  23.5 1.5 collective-permute-start.4
  25.6 1.8 broadcast_in_dim.4
  27.5 3.7 %all-to-all-start = ((bf16[4,5,24,768]{3,2,1,0:T(8,128)(2,1)}), bf16[4,5,24,768]{3,2,1,0:T(8,128)(2,1)S(1)}, u32[]{:S(2)}, u32[]{:S(2)}) async-start(bf16[4,5,24,768]{3,2,1,0:T(8,128)(2,1)} %broadcast_in_dim.4), calls=%async_computation | async-start | bytes 1474560 | tf_op jit(solution)/shard_map/all_to_all | solution.py:704
  31.4 3.5 %collective-permute-done.3.refs_1_ = bf16[4,24,2304]{2,1,0:T(8,128)(2,1)} collective-permute-done((bf16[4,24,2304]{2,1,0:T(8,128)(2,1)S(1)}, bf16[4,24,2304]{2,1,0:T(8,128)(2,1)}, u32[]{:S(2)}, u32[]{:S(2)}) %collective-permute-start.3) | collective-permute-done | bytes 442400 | tf_op jit(solution)/shard_map/ppermute | solution.py:670
  34.8 1.9 collective-permute-done.4.refs_2_
  36.7 6.7 %collective-permute-done.5.refs_3_ = bf16[4,24,2304]{2,1,0:T(8,128)(2,1)} collective-permute-done((bf16[4,24,2304]{2,1,0:T(8,128)(2,1)S(1)}, bf16[4,24,2304]{2,1,0:T(8,128)(2,1)}, u32[]{:S(2)}, u32[]{:S(2)}) %collective-permute-start.5) | collective-permute-done | bytes 442400 | tf_op jit(solution)/shard_map/ppermute | solution.py:670
  45.3 0.9 fusion
  47.1 1.1 all-to-all-done.refs_0_.refs_1_
  48.2 0.9 copy-done.1
  49.1 1.2 collective-permute-start.14
  50.2 0.9 broadcast_in_dim.5
  51.1 4.0 %all-to-all-start.1 = ((bf16[4,96,768]{2,1,0:T(8,128)(2,1)}), bf16[4,96,768]{2,1,0:T(8,128)(2,1)S(1)}, u32[]{:S(2)}, u32[]{:S(2)}) async-start(bf16[4,96,768]{2,1,0:T(8,128)(2,1)} %broadcast_in_dim.5), calls=%async_computation.1 | async-start | bytes 1179648 | tf_op jit(solution)/shard_map/all_to_all | solution.py:704
  55.1 1.6 collective-permute-start.15
  56.7 0.9 collective-permute-start.16
  57.6 22.6 %attend.1 = (bf16[1024,768]{1,0:T(8,128)(2,1)}, bf16[1024,768]{1,0:T(8,128)(2,1)}, bf16[1024,768]{1,0:T(8,128)(2,1)}, bf16[768,1024]{1,0:T(8,128)(2,1)}, bf16[76...) custom-call(s32[1,12]{1,0:T(1,128)} %lens_ref.3, s32[1]{0:T(128)S(6)} %copy.78.valid_ref, ...), custom_call_target="tpu_custom_call" | custom-call | flops 27499999232 | bytes 75000000 | tf_op jit(solution)/shard_map/attend/pallas_call | solution.py:199
  80.2 9.0 %collective-permute-done.16.refs_3_ = bf16[4,5,24,768]{3,2,1,0:T(8,128)(2,1)} collective-permute-done((bf16[4,5,24,768]{3,2,1,0:T(8,128)(2,1)S(1)}, bf16[4,5,24,768]{3,2,1,0:T(8,128)(2,1)}, u32[]{:S(2)}, u32[]{:S(2)}) %collective-permute-start.16) | collective-permute-done | bytes 737312 | tf_op jit(solution)/shard_map/ppermute | solution.py:670
  91.8 0.8 collective-permute-start.21
  92.7 1.2 collective-permute-start.22
  94.6 1.5 collective-permute-start.23
  96.1 0.9 copy-done.43
  97.0 29.2 %mlp_up.1 = (f32[1024,768]{1,0:T(8,128)}, bf16[1024,768]{1,0:T(8,128)(2,1)}, bf16[768,1024]{1,0:T(8,128)(2,1)}, bf16[768,1024]{1,0:T(8,128)(2,1)}, bf16[1024,768...) custom-call(s32[3]{0:T(128)} %pad_add_fusion.me_ref, ...), custom_call_target="tpu_custom_call" | custom-call | flops 28600000512 | bytes 78000000 | tf_op jit(solution)/shard_map/mlp_up/pallas_call | solution.py:344
  126.3 0.8 copy-done.21
  127.5 1.1 copy-done.9
  129.7 2.5 collective-permute-done.28.refs_9_
  132.2 1.6 fusion.2
  133.8 1.2 collective-permute-start.29
  135.8 1.5 collective-permute-start.31
  137.4 0.8 copy-done.46
  138.2 0.9 copy-done.47
  139.0 37.4 %mlp_down.1 = (f32[1024,768]{1,0:T(8,128)}, f32[1024,768]{1,0:T(8,128)}, bf16[1024,768]{1,0:T(8,128)(2,1)}, bf16[384,3840]{1,0:T(8,128)(2,1)}, bf16[384,3840]{1,...) custom-call(s32[3]{0:T(128)} %pad_add_fusion.me_ref, ...), custom_call_target="tpu_custom_call", output_to_operand_aliasing={{7}: (21, {})} | custom-call | flops 38499999744 | bytes 105000000 | tf_op jit(solution)/shard_map/mlp_down/pallas_call | solution.py:465
  176.5 0.9 copy-done.12
  177.4 0.8 copy-done.13
  178.2 2.1 add_convert_fusion.9
  180.3 1.8 collective-permute-start.36
  182.1 2.3 collective-permute-start.37
  184.8 2.0 add_convert_fusion
  187.0 1.2 collective-permute-start.33
  189.0 1.5 collective-permute-start.35
  190.5 29.1 %attend_back.1 = (bf16[1024,768]{1,0:T(8,128)(2,1)}, bf16[1024,768]{1,0:T(8,128)(2,1)}, bf16[1024,768]{1,0:T(8,128)(2,1)}, bf16[384,2304]{1,0:T(8,128)(2,1)}, bf...) custom-call(s32[1,12]{1,0:T(1,128)} %lens_ref.3, ...), custom_call_target="tpu_custom_call", output_to_operand_aliasing={{6}: (9, {}), {7}: (10, {})} | custom-call | flops 36300001280 | bytes 99000000 | tf_op jit(solution)/shard_map/attend_back/pallas_call | solution.py:590
  219.7 2.4 collective-permute-done.35.refs_3_
  222.2 0.9 copy-done.6
  223.1 3.0 %add_convert_fusion.8 = (bf16[24,3840]{1,0:T(8,128)(2,1)}, bf16[24,3840]{1,0:T(8,128)(2,1)}, bf16[24,3840]{1,0:T(8,128)(2,1)}) fusion(bf16[96,3840]{1,0:T(8,128)(2,1)} %copy-done.6, bf16[96,3840]{1,0:T(8,128)(2,1)} %copy-done.5, bf16[96,3840]{1,0:T(8,128)(2,1)} %copy-done.4, bf16[384,3840]{1,0:T(8,128)(2,1)} %copy-done.7, ...), kind=kLoop, calls=%fused_computation.20 | loop fusion | flops 2764800 | bytes 3317760 | tf_op jit(solution)/shard_map/convert_element_type | solution.py:736
  226.1 1.4 collective-permute-start.46
  227.4 2.7 collective-permute-start.47
  230.1 1.5 add_convert_fusion.5
  231.6 1.2 collective-permute-start.40
  233.6 1.5 collective-permute-start.42
  235.1 10.7 %input_back.1 = (f32[1024,768]{1,0:T(8,128)}, f32[8,768]{1,0:T(8,128)}, bf16[384,3840]{1,0:T(8,128)(2,1)}, bf16[384,2304]{1,0:T(8,128)(2,1)}, bf16[1536,768]{1,0:T(8,128)(2,1)}) custom-call(bf16[1024,768]{1,0:T(8,128)(2,1)} %get-tuple-element.85.dq_ref, ...), custom_call_target="tpu_custom_call", output_to_operand_aliasing={{2}: (7, {}), {3}: (8, {}), {4}: (9, {})} | custom-call | flops 14300000256 | bytes 39000000 | tf_op jit(solution)/shard_map/input_back/pallas_call | solution.py:650
  246.3 8.1 %collective-permute-done.42 = bf16[96,2304]{1,0:T(8,128)(2,1)S(1)} collective-permute-done((bf16[96,2304]{1,0:T(8,128)(2,1)S(1)}, bf16[96,2304]{1,0:T(8,128)(2,1)S(1)}, u32[]{:S(2)}, u32[]{:S(2)}) %collective-permute-start.42) | collective-permute-done | bytes 442400 | tf_op jit(solution)/shard_map/ppermute | solution.py:670
  254.4 2.0 add_convert_fusion.14
  257.2 1.7 convert_add_fusion.3
  259.3 0.9 collective-permute-start.44
  260.2 3.2 %collective-permute-start.45 = (bf16[24,2304]{1,0:T(8,128)(2,1)S(1)}, bf16[24,2304]{1,0:T(8,128)(2,1)S(1)}, u32[]{:S(2)}, u32[]{:S(2)}) collective-permute-start(bf16[24,2304]{1,0:T(8,128)(2,1)S(1)} %copy-done.30), channel_id=1, source_target_pairs={{0,24},{8,16},{16,8},{24,0},{1,25},{9,17},{17,9},{25,1},{2,26},{10... | collective-permute-start | bytes 331784 | tf_op jit(solution)/shard_map/ppermute | solution.py:670
  267.1 2.6 all-to-all-start.2
  269.7 1.4 convert_add_fusion.4
  273.2 3.7 %all-to-all-done.2 = bf16[32,2,192]{2,1,0:T(2,128)(2,1)S(1)} async-done(((bf16[32,2,192]{2,1,0:T(2,128)(2,1)}), bf16[32,2,192]{2,1,0:T(2,128)(2,1)S(1)}, u32[]{:S(2)}, u32[]{:S(2)}) %all-to-all-start.2) | async-done | bytes 24608 | tf_op jit(solution)/shard_map/all_to_all | solution.py:827
  278.3 1.1 convert_add_fusion.5
  (223 shorter events, 25.6 us)
Async XLA Ops:
  0.6 10.6 %copy-start.33 = (f32[73728]{0:T(1024)S(1)}, f32[73728]{0:T(1024)}, u32[]{:S(2)}) copy-start(f32[73728]{0:T(1024)} %param.15) | copy-start | bytes 884740
  0.6 10.7 %copy-start.38 = (f32[18432]{0:T(1024)S(1)}, f32[18432]{0:T(1024)}, u32[]{:S(2)}) copy-start(f32[18432]{0:T(1024)} %param.14) | copy-start | bytes 221188
  0.7 10.8 %copy-start.34 = (f32[73728]{0:T(1024)S(1)}, f32[73728]{0:T(1024)}, u32[]{:S(2)}) copy-start(f32[73728]{0:T(1024)} %param.17) | copy-start | bytes 884740
  3.3 9.7 %collective-permute-start.2 = (bf16[24,2432]{1,0:T(8,128)(2,1)S(1)}, bf16[24,2432]{1,0:T(8,128)(2,1)S(1)}, u32[]{:S(2)}, u32[]{:S(2)}) collective-permute-start(bf16[24,2432]{1,0:T(8,128)(2,1)S(1)} %pad_maximum_fusion.2), channel_id=1, source_target_pairs={{0,24},{8,16},{16,8},{24,0},{1,25},{9,17},{17,9},{25,1},{2,26},{10... | collective-permute-start | bytes 350216 | tf_op jit(solution)/shard_map/ppermute | solution.py:670
  8.4 9.8 %collective-permute-start.1 = (bf16[24,2432]{1,0:T(8,128)(2,1)S(1)}, bf16[24,2432]{1,0:T(8,128)(2,1)S(1)}, u32[]{:S(2)}, u32[]{:S(2)}) collective-permute-start(bf16[24,2432]{1,0:T(8,128)(2,1)S(1)} %pad_maximum_fusion.2), channel_id=1, source_target_pairs={{0,16},{8,24},{16,0},{24,8},{1,17},{9,25},{17,1},{25,9},{2,18},{10... | collective-permute-start | bytes 350216 | tf_op jit(solution)/shard_map/ppermute | solution.py:670
  8.4 9.8 %collective-permute-start = (bf16[24,2432]{1,0:T(8,128)(2,1)S(1)}, bf16[24,2432]{1,0:T(8,128)(2,1)S(1)}, u32[]{:S(2)}, u32[]{:S(2)}) collective-permute-start(bf16[24,2432]{1,0:T(8,128)(2,1)S(1)} %pad_maximum_fusion.2), channel_id=1, source_target_pairs={{0,8},{8,0},{16,24},{24,16},{1,9},{9,1},{17,25},{25,17},{2,10},{10... | collective-permute-start | bytes 350216 | tf_op jit(solution)/shard_map/ppermute | solution.py:670
  18.2 6.8 %collective-permute-start.10 = (bf16[4,24,128]{2,1,0:T(8,128)(2,1)S(1)}, bf16[4,24,128]{2,1,0:T(8,128)(2,1)S(1)}, u32[]{:S(2)}, u32[]{:S(2)}) collective-permute-start(bf16[4,24,128]{2,1,0:T(8,128)(2,1)S(1)} %pad_maximum_fusion.3), channel_id=1, source_target_pairs={{0,2},{2,0},{4,6},{6,4},{1,3},{3,1},{5,7},{7,5},{8,10},{10,8},{12,... | collective-permute-start | bytes 73736 | tf_op jit(solution)/shard_map/ppermute | solution.py:670
  19.8 11.4 %collective-permute-start.11 = (bf16[4,24,128]{2,1,0:T(8,128)(2,1)S(1)}, bf16[4,24,128]{2,1,0:T(8,128)(2,1)S(1)}, u32[]{:S(2)}, u32[]{:S(2)}) collective-permute-start(bf16[4,24,128]{2,1,0:T(8,128)(2,1)S(1)} %pad_maximum_fusion.3), channel_id=1, source_target_pairs={{0,4},{2,6},{4,0},{6,2},{1,5},{3,7},{5,1},{7,3},{8,12},{10,14},{12... | collective-permute-start | bytes 73736 | tf_op jit(solution)/shard_map/ppermute | solution.py:670
  21.3 22.1 %collective-permute-start.12 = (bf16[4,24,128]{2,1,0:T(8,128)(2,1)S(1)}, bf16[4,24,128]{2,1,0:T(8,128)(2,1)S(1)}, u32[]{:S(2)}, u32[]{:S(2)}) collective-permute-start(bf16[4,24,128]{2,1,0:T(8,128)(2,1)S(1)} %pad_maximum_fusion.3), channel_id=1, source_target_pairs={{0,6},{2,4},{4,2},{6,0},{1,7},{3,5},{5,3},{7,1},{8,14},{10,12},{12... | collective-permute-start | bytes 73736 | tf_op jit(solution)/shard_map/ppermute | solution.py:670
  21.9 24.3 %copy-start.29 = (bf16[4,24,2304]{2,1,0:T(8,128)(2,1)}, bf16[4,24,2304]{2,1,0:T(8,128)(2,1)S(1)}, u32[]{:S(2)}) copy-start(bf16[4,24,2304]{2,1,0:T(8,128)(2,1)S(1)} %pad_maximum_fusion.refs_0_) | copy-start | bytes 1327108
  21.9 12.9 %collective-permute-start.3 = (bf16[4,24,2304]{2,1,0:T(8,128)(2,1)S(1)}, bf16[4,24,2304]{2,1,0:T(8,128)(2,1)}, u32[]{:S(2)}, u32[]{:S(2)}) collective-permute-start(bf16[4,24,2304]{2,1,0:T(8,128)(2,1)S(1)} %pad_maximum_fusion.refs_0_), channel_id=1, source_target_pairs={{0,2},{2,0},{4,6},{6,4},{1,3},{3,1},{5,7},{7,5},{8,10},{10,8},{12,... | collective-permute-start | bytes 1327112 | tf_op jit(solution)/shard_map/ppermute | solution.py:670
  23.5 13.2 %collective-permute-start.4 = (bf16[4,24,2304]{2,1,0:T(8,128)(2,1)S(1)}, bf16[4,24,2304]{2,1,0:T(8,128)(2,1)}, u32[]{:S(2)}, u32[]{:S(2)}) collective-permute-start(bf16[4,24,2304]{2,1,0:T(8,128)(2,1)S(1)} %pad_maximum_fusion.refs_0_), channel_id=1, source_target_pairs={{0,4},{2,6},{4,0},{6,2},{1,5},{3,7},{5,1},{7,3},{8,12},{10,14},{12... | collective-permute-start | bytes 1327112 | tf_op jit(solution)/shard_map/ppermute | solution.py:670
  25.0 18.4 %collective-permute-start.5 = (bf16[4,24,2304]{2,1,0:T(8,128)(2,1)S(1)}, bf16[4,24,2304]{2,1,0:T(8,128)(2,1)}, u32[]{:S(2)}, u32[]{:S(2)}) collective-permute-start(bf16[4,24,2304]{2,1,0:T(8,128)(2,1)S(1)} %pad_maximum_fusion.refs_0_), channel_id=1, source_target_pairs={{0,6},{2,4},{4,2},{6,0},{1,7},{3,5},{5,3},{7,1},{8,14},{10,12},{12... | collective-permute-start | bytes 1327112 | tf_op jit(solution)/shard_map/ppermute | solution.py:670
  27.5 20.7 %all-to-all-start = ((bf16[4,5,24,768]{3,2,1,0:T(8,128)(2,1)}), bf16[4,5,24,768]{3,2,1,0:T(8,128)(2,1)S(1)}, u32[]{:S(2)}, u32[]{:S(2)}) async-start(bf16[4,5,24,768]{3,2,1,0:T(8,128)(2,1)} %broadcast_in_dim.4), calls=%async_computation | async-start | bytes 1474560 | tf_op jit(solution)/shard_map/all_to_all | solution.py:704
  31.3 23.9 %collective-permute-start.6 = (bf16[4,24,2304]{2,1,0:T(8,128)(2,1)S(1)}, bf16[4,24,2304]{2,1,0:T(8,128)(2,1)}, u32[]{:S(2)}, u32[]{:S(2)}) collective-permute-start(bf16[4,24,2304]{2,1,0:T(8,128)(2,1)S(1)} %pad_maximum_fusion.refs_0_), channel_id=1, source_target_pairs={{0,1},{1,0},{2,3},{3,2},{4,5},{5,4},{6,7},{7,6},{8,9},{9,8},{10,11... | collective-permute-start | bytes 1327112 | tf_op jit(solution)/shard_map/ppermute | solution.py:666
  34.8 21.9 %collective-permute-start.7 = (bf16[4,24,2304]{2,1,0:T(8,128)(2,1)}, bf16[4,24,2304]{2,1,0:T(8,128)(2,1)}, u32[]{:S(2)}, u32[]{:S(2)}) collective-permute-start(bf16[4,24,2304]{2,1,0:T(8,128)(2,1)} %collective-permute-done.3.refs_1_), channel_id=1, source_target_pairs={{0,1},{1,0},{2,3},{3,2},{4,5},{5,4},{6,7},{7,6},{8,9},{9,8},{10,11... | collective-permute-start | bytes 1327112 | tf_op jit(solution)/shard_map/ppermute | solution.py:666
  36.7 20.8 %collective-permute-start.8 = (bf16[4,24,2304]{2,1,0:T(8,128)(2,1)}, bf16[4,24,2304]{2,1,0:T(8,128)(2,1)}, u32[]{:S(2)}, u32[]{:S(2)}) collective-permute-start(bf16[4,24,2304]{2,1,0:T(8,128)(2,1)} %collective-permute-done.4.refs_2_), channel_id=1, source_target_pairs={{0,1},{1,0},{2,3},{3,2},{4,5},{5,4},{6,7},{7,6},{8,9},{9,8},{10,11... | collective-permute-start | bytes 1327112 | tf_op jit(solution)/shard_map/ppermute | solution.py:666
  43.4 14.2 %collective-permute-start.9 = (bf16[4,24,2304]{2,1,0:T(8,128)(2,1)}, bf16[4,24,2304]{2,1,0:T(8,128)(2,1)}, u32[]{:S(2)}, u32[]{:S(2)}) collective-permute-start(bf16[4,24,2304]{2,1,0:T(8,128)(2,1)} %collective-permute-done.5.refs_3_), channel_id=1, source_target_pairs={{0,1},{1,0},{2,3},{3,2},{4,5},{5,4},{6,7},{7,6},{8,9},{9,8},{10,11... | collective-permute-start | bytes 1327112 | tf_op jit(solution)/shard_map/ppermute | solution.py:666
  43.4 1.9 collective-permute-start.13
  49.1 31.1 %collective-permute-start.14 = (bf16[4,5,24,768]{3,2,1,0:T(8,128)(2,1)}, bf16[4,5,24,768]{3,2,1,0:T(8,128)(2,1)S(1)}, u32[]{:S(2)}, u32[]{:S(2)}) collective-permute-start(bf16[4,5,24,768]{3,2,1,0:T(8,128)(2,1)} %gate.9.refs_0_), channel_id=1, source_target_pairs={{0,2},{2,0},{4,6},{6,4},{1,3},{3,1},{5,7},{7,5},{8,10},{10,8},{12,... | collective-permute-start | bytes 2211848 | tf_op jit(solution)/shard_map/ppermute | solution.py:670
  51.1 38.1 %all-to-all-start.1 = ((bf16[4,96,768]{2,1,0:T(8,128)(2,1)}), bf16[4,96,768]{2,1,0:T(8,128)(2,1)S(1)}, u32[]{:S(2)}, u32[]{:S(2)}) async-start(bf16[4,96,768]{2,1,0:T(8,128)(2,1)} %broadcast_in_dim.5), calls=%async_computation.1 | async-start | bytes 1179648 | tf_op jit(solution)/shard_map/all_to_all | solution.py:704
  55.1 25.1 %collective-permute-start.15 = (bf16[4,5,24,768]{3,2,1,0:T(8,128)(2,1)S(1)}, bf16[4,5,24,768]{3,2,1,0:T(8,128)(2,1)S(1)}, u32[]{:S(2)}, u32[]{:S(2)}) collective-permute-start(bf16[4,5,24,768]{3,2,1,0:T(8,128)(2,1)S(1)} %copy-done.2), channel_id=1, source_target_pairs={{0,4},{2,6},{4,0},{6,2},{1,5},{3,7},{5,1},{7,3},{8,12},{10,14},{12... | collective-permute-start | bytes 2211848 | tf_op jit(solution)/shard_map/ppermute | solution.py:670
  56.7 32.5 %collective-permute-start.16 = (bf16[4,5,24,768]{3,2,1,0:T(8,128)(2,1)S(1)}, bf16[4,5,24,768]{3,2,1,0:T(8,128)(2,1)}, u32[]{:S(2)}, u32[]{:S(2)}) collective-permute-start(bf16[4,5,24,768]{3,2,1,0:T(8,128)(2,1)S(1)} %copy-done.2), channel_id=1, source_target_pairs={{0,6},{2,4},{4,2},{6,0},{1,7},{3,5},{5,3},{7,1},{8,14},{10,12},{12... | collective-permute-start | bytes 2211848 | tf_op jit(solution)/shard_map/ppermute | solution.py:670
  80.2 9.0 %copy-start.17 = (bf16[4,5,24,768]{3,2,1,0:T(8,128)(2,1)}, bf16[4,5,24,768]{3,2,1,0:T(8,128)(2,1)S(1)}, u32[]{:S(2)}) copy-start(bf16[4,5,24,768]{3,2,1,0:T(8,128)(2,1)S(1)} %collective-permute-done.14.refs_1_) | copy-start | bytes 2211844
  80.2 9.0 %copy-start.18 = (bf16[4,5,24,768]{3,2,1,0:T(8,128)(2,1)}, bf16[4,5,24,768]{3,2,1,0:T(8,128)(2,1)S(1)}, u32[]{:S(2)}) copy-start(bf16[4,5,24,768]{3,2,1,0:T(8,128)(2,1)S(1)} %collective-permute-done.15.refs_2_) | copy-start | bytes 2211844
  90.0 2.6 collective-permute-start.17
  90.0 4.5 %collective-permute-start.18 = (bf16[4,5,24,768]{3,2,1,0:T(8,128)(2,1)}, bf16[4,5,24,768]{3,2,1,0:T(8,128)(2,1)S(1)}, u32[]{:S(2)}, u32[]{:S(2)}) collective-permute-start(bf16[4,5,24,768]{3,2,1,0:T(8,128)(2,1)} %get-tuple-element.60.refs_1_), channel_id=1, source_target_pairs={{0,1},{1,0},{2,3},{3,2},{4,5},{5,4},{6,7},{7,6},{8,9},{9,8},{10,11... | collective-permute-start | bytes 2211848 | tf_op jit(solution)/shard_map/ppermute | solution.py:666
  90.5 5.5 %collective-permute-start.19 = (bf16[4,5,24,768]{3,2,1,0:T(8,128)(2,1)}, bf16[4,5,24,768]{3,2,1,0:T(8,128)(2,1)S(1)}, u32[]{:S(2)}, u32[]{:S(2)}) collective-permute-start(bf16[4,5,24,768]{3,2,1,0:T(8,128)(2,1)} %get-tuple-element.61.refs_2_), channel_id=1, source_target_pairs={{0,1},{1,0},{2,3},{3,2},{4,5},{5,4},{6,7},{7,6},{8,9},{9,8},{10,11... | collective-permute-start | bytes 2211848 | tf_op jit(solution)/shard_map/ppermute | solution.py:666
  90.5 5.5 %collective-permute-start.20 = (bf16[4,5,24,768]{3,2,1,0:T(8,128)(2,1)}, bf16[4,5,24,768]{3,2,1,0:T(8,128)(2,1)}, u32[]{:S(2)}, u32[]{:S(2)}) collective-permute-start(bf16[4,5,24,768]{3,2,1,0:T(8,128)(2,1)} %get-tuple-element.62.refs_3_), channel_id=1, source_target_pairs={{0,1},{1,0},{2,3},{3,2},{4,5},{5,4},{6,7},{7,6},{8,9},{9,8},{10,11... | collective-permute-start | bytes 2211848 | tf_op jit(solution)/shard_map/ppermute | solution.py:666
  91.8 34.5 %collective-permute-start.21 = (bf16[4,96,768]{2,1,0:T(8,128)(2,1)}, bf16[4,96,768]{2,1,0:T(8,128)(2,1)S(1)}, u32[]{:S(2)}, u32[]{:S(2)}) collective-permute-start(bf16[4,96,768]{2,1,0:T(8,128)(2,1)} %get-tuple-element.72.refs_0_), channel_id=1, source_target_pairs={{0,2},{2,0},{4,6},{6,4},{1,3},{3,1},{5,7},{7,5},{8,10},{10,8},{12,... | collective-permute-start | bytes 1769480 | tf_op jit(solution)/shard_map/ppermute | solution.py:670
  92.7 33.6 %collective-permute-start.22 = (bf16[4,96,768]{2,1,0:T(8,128)(2,1)}, bf16[4,96,768]{2,1,0:T(8,128)(2,1)S(1)}, u32[]{:S(2)}, u32[]{:S(2)}) collective-permute-start(bf16[4,96,768]{2,1,0:T(8,128)(2,1)} %get-tuple-element.72.refs_0_), channel_id=1, source_target_pairs={{0,4},{2,6},{4,0},{6,2},{1,5},{3,7},{5,1},{7,3},{8,12},{10,14},{12... | collective-permute-start | bytes 1769480 | tf_op jit(solution)/shard_map/ppermute | solution.py:670
  94.6 31.8 %collective-permute-start.23 = (bf16[4,96,768]{2,1,0:T(8,128)(2,1)}, bf16[4,96,768]{2,1,0:T(8,128)(2,1)S(1)}, u32[]{:S(2)}, u32[]{:S(2)}) collective-permute-start(bf16[4,96,768]{2,1,0:T(8,128)(2,1)} %get-tuple-element.72.refs_0_), channel_id=1, source_target_pairs={{0,6},{2,4},{4,2},{6,0},{1,7},{3,5},{5,3},{7,1},{8,14},{10,12},{12... | collective-permute-start | bytes 1769480 | tf_op jit(solution)/shard_map/ppermute | solution.py:670
  127.5 4.7 %collective-permute-start.28 = (bf16[1536,768]{1,0:T(8,128)(2,1)}, bf16[1536,768]{1,0:T(8,128)(2,1)S(1)}, u32[]{:S(2)}, u32[]{:S(2)}) collective-permute-start(bf16[1536,768]{1,0:T(8,128)(2,1)} %gate.12), channel_id=1, source_target_pairs={{0,1},{1,0},{2,3},{3,2},{4,5},{5,4},{6,7},{7,6},{8,9},{9,8},{10,11... | collective-permute-start | bytes 7077896 | tf_op jit(solution)/shard_map/ppermute | solution.py:666
  128.5 6.5 %collective-permute-start.24 = (bf16[4,96,768]{2,1,0:T(8,128)(2,1)S(1)}, bf16[4,96,768]{2,1,0:T(8,128)(2,1)S(1)}, u32[]{:S(2)}, u32[]{:S(2)}) collective-permute-start(bf16[4,96,768]{2,1,0:T(8,128)(2,1)S(1)} %copy-done.9), channel_id=1, source_target_pairs={{0,1},{1,0},{2,3},{3,2},{4,5},{5,4},{6,7},{7,6},{8,9},{9,8},{10,11... | collective-permute-start | bytes 1769480 | tf_op jit(solution)/shard_map/ppermute | solution.py:666
  128.5 7.3 %collective-permute-start.25 = (bf16[4,96,768]{2,1,0:T(8,128)(2,1)}, bf16[4,96,768]{2,1,0:T(8,128)(2,1)S(1)}, u32[]{:S(2)}, u32[]{:S(2)}) collective-permute-start(bf16[4,96,768]{2,1,0:T(8,128)(2,1)} %copy-done.20), channel_id=1, source_target_pairs={{0,1},{1,0},{2,3},{3,2},{4,5},{5,4},{6,7},{7,6},{8,9},{9,8},{10,11... | collective-permute-start | bytes 1769480 | tf_op jit(solution)/shard_map/ppermute | solution.py:666
  129.0 8.3 %collective-permute-start.26 = (bf16[4,96,768]{2,1,0:T(8,128)(2,1)}, bf16[4,96,768]{2,1,0:T(8,128)(2,1)S(1)}, u32[]{:S(2)}, u32[]{:S(2)}) collective-permute-start(bf16[4,96,768]{2,1,0:T(8,128)(2,1)} %copy-done.21), channel_id=1, source_target_pairs={{0,1},{1,0},{2,3},{3,2},{4,5},{5,4},{6,7},{7,6},{8,9},{9,8},{10,11... | collective-permute-start | bytes 1769480 | tf_op jit(solution)/shard_map/ppermute | solution.py:666
  129.0 8.3 %collective-permute-start.27 = (bf16[4,96,768]{2,1,0:T(8,128)(2,1)}, bf16[4,96,768]{2,1,0:T(8,128)(2,1)S(1)}, u32[]{:S(2)}, u32[]{:S(2)}) collective-permute-start(bf16[4,96,768]{2,1,0:T(8,128)(2,1)} %copy-done.22), channel_id=1, source_target_pairs={{0,1},{1,0},{2,3},{3,2},{4,5},{5,4},{6,7},{7,6},{8,9},{9,8},{10,11... | collective-permute-start | bytes 1769480 | tf_op jit(solution)/shard_map/ppermute | solution.py:666
  133.8 42.6 %collective-permute-start.29 = (bf16[384,768]{1,0:T(8,128)(2,1)}, bf16[384,768]{1,0:T(8,128)(2,1)S(1)}, u32[]{:S(2)}, u32[]{:S(2)}) collective-permute-start(bf16[384,768]{1,0:T(8,128)(2,1)} %get-tuple-element.125), channel_id=1, source_target_pairs={{0,2},{2,0},{4,6},{6,4},{1,3},{3,1},{5,7},{7,5},{8,10},{10,8},{12,... | collective-permute-start | bytes 1769480 | tf_op jit(solution)/shard_map/ppermute | solution.py:670
  135.0 41.5 %collective-permute-start.30 = (bf16[384,768]{1,0:T(8,128)(2,1)S(1)}, bf16[384,768]{1,0:T(8,128)(2,1)S(1)}, u32[]{:S(2)}, u32[]{:S(2)}) collective-permute-start(bf16[384,768]{1,0:T(8,128)(2,1)S(1)} %get-tuple-element.124), channel_id=1, source_target_pairs={{0,4},{2,6},{4,0},{6,2},{1,5},{3,7},{5,1},{7,3},{8,12},{10,14},{12... | collective-permute-start | bytes 1769480 | tf_op jit(solution)/shard_map/ppermute | solution.py:670
  135.8 40.7 %collective-permute-start.31 = (bf16[384,768]{1,0:T(8,128)(2,1)S(1)}, bf16[384,768]{1,0:T(8,128)(2,1)S(1)}, u32[]{:S(2)}, u32[]{:S(2)}) collective-permute-start(bf16[384,768]{1,0:T(8,128)(2,1)S(1)} %get-tuple-element.123), channel_id=1, source_target_pairs={{0,6},{2,4},{4,2},{6,0},{1,7},{3,5},{5,3},{7,1},{8,14},{10,12},{12... | collective-permute-start | bytes 1769480 | tf_op jit(solution)/shard_map/ppermute | solution.py:670
  178.2 6.5 %collective-permute-start.32 = (bf16[384,3840]{1,0:T(8,128)(2,1)}, bf16[384,3840]{1,0:T(8,128)(2,1)S(1)}, u32[]{:S(2)}, u32[]{:S(2)}) collective-permute-start(bf16[384,3840]{1,0:T(8,128)(2,1)} %gate.13), channel_id=1, source_target_pairs={{0,1},{1,0},{2,3},{3,2},{4,5},{5,4},{6,7},{7,6},{8,9},{9,8},{10,11... | collective-permute-start | bytes 8847368 | tf_op jit(solution)/shard_map/ppermute | solution.py:666
  180.3 8.7 %collective-permute-start.36 = (bf16[96,768]{1,0:T(8,128)(2,1)S(1)}, bf16[96,768]{1,0:T(8,128)(2,1)S(1)}, u32[]{:S(2)}, u32[]{:S(2)}) collective-permute-start(bf16[96,768]{1,0:T(8,128)(2,1)S(1)} %get-tuple-element.113), channel_id=1, source_target_pairs={{0,8},{8,0},{16,24},{24,16},{1,9},{9,1},{17,25},{25,17},{2,10},{10... | collective-permute-start | bytes 442376 | tf_op jit(solution)/shard_map/ppermute | solution.py:670
  182.1 37.6 %collective-permute-start.37 = (bf16[96,768]{1,0:T(8,128)(2,1)S(1)}, bf16[96,768]{1,0:T(8,128)(2,1)S(1)}, u32[]{:S(2)}, u32[]{:S(2)}) collective-permute-start(bf16[96,768]{1,0:T(8,128)(2,1)S(1)} %get-tuple-element.112), channel_id=1, source_target_pairs={{0,16},{8,24},{16,0},{24,8},{1,17},{9,25},{17,1},{25,9},{2,18},{10... | collective-permute-start | bytes 442376 | tf_op jit(solution)/shard_map/ppermute | solution.py:670
  184.4 35.2 %collective-permute-start.38 = (bf16[96,768]{1,0:T(8,128)(2,1)S(1)}, bf16[96,768]{1,0:T(8,128)(2,1)S(1)}, u32[]{:S(2)}, u32[]{:S(2)}) collective-permute-start(bf16[96,768]{1,0:T(8,128)(2,1)S(1)} %get-tuple-element.111), channel_id=1, source_target_pairs={{0,24},{8,16},{16,8},{24,0},{1,25},{9,17},{17,9},{25,1},{2,26},{10... | collective-permute-start | bytes 442376 | tf_op jit(solution)/shard_map/ppermute | solution.py:670
  187.0 32.7 %collective-permute-start.33 = (bf16[96,3840]{1,0:T(8,128)(2,1)}, bf16[96,3840]{1,0:T(8,128)(2,1)S(1)}, u32[]{:S(2)}, u32[]{:S(2)}) collective-permute-start(bf16[96,3840]{1,0:T(8,128)(2,1)} %get-tuple-element.116), channel_id=1, source_target_pairs={{0,2},{2,0},{4,6},{6,4},{1,3},{3,1},{5,7},{7,5},{8,10},{10,8},{12,... | collective-permute-start | bytes 2211848 | tf_op jit(solution)/shard_map/ppermute | solution.py:670
  188.2 31.5 %collective-permute-start.34 = (bf16[96,3840]{1,0:T(8,128)(2,1)}, bf16[96,3840]{1,0:T(8,128)(2,1)S(1)}, u32[]{:S(2)}, u32[]{:S(2)}) collective-permute-start(bf16[96,3840]{1,0:T(8,128)(2,1)} %get-tuple-element.115), channel_id=1, source_target_pairs={{0,4},{2,6},{4,0},{6,2},{1,5},{3,7},{5,1},{7,3},{8,12},{10,14},{12... | collective-permute-start | bytes 2211848 | tf_op jit(solution)/shard_map/ppermute | solution.py:670
  189.0 30.7 %copy-start.23 = (bf16[96,768]{1,0:T(8,128)(2,1)}, bf16[96,768]{1,0:T(8,128)(2,1)S(1)}, u32[]{:S(2)}) copy-start(bf16[96,768]{1,0:T(8,128)(2,1)S(1)} %collective-permute-done.36.refs_4_) | copy-start | bytes 442372
  189.0 33.2 %collective-permute-start.35 = (bf16[96,3840]{1,0:T(8,128)(2,1)}, bf16[96,3840]{1,0:T(8,128)(2,1)S(1)}, u32[]{:S(2)}, u32[]{:S(2)}) collective-permute-start(bf16[96,3840]{1,0:T(8,128)(2,1)} %get-tuple-element.114), channel_id=1, source_target_pairs={{0,6},{2,4},{4,2},{6,0},{1,7},{3,5},{5,3},{7,1},{8,14},{10,12},{12... | collective-permute-start | bytes 2211848 | tf_op jit(solution)/shard_map/ppermute | solution.py:670
  223.1 7.1 %collective-permute-start.39 = (bf16[384,2304]{1,0:T(8,128)(2,1)}, bf16[384,2304]{1,0:T(8,128)(2,1)S(1)}, u32[]{:S(2)}, u32[]{:S(2)}) collective-permute-start(bf16[384,2304]{1,0:T(8,128)(2,1)} %gate.14), channel_id=1, source_target_pairs={{0,1},{1,0},{2,3},{3,2},{4,5},{5,4},{6,7},{7,6},{8,9},{9,8},{10,11... | collective-permute-start | bytes 5308424 | tf_op jit(solution)/shard_map/ppermute | solution.py:666
  226.1 30.4 %collective-permute-start.46 = (bf16[24,3840]{1,0:T(8,128)(2,1)}, bf16[24,3840]{1,0:T(8,128)(2,1)}, u32[]{:S(2)}, u32[]{:S(2)}) collective-permute-start(bf16[24,3840]{1,0:T(8,128)(2,1)} %get-tuple-element.108), channel_id=1, source_target_pairs={{0,8},{8,0},{16,24},{24,16},{1,9},{9,1},{17,25},{25,17},{2,10},{10... | collective-permute-start | bytes 552968 | tf_op jit(solution)/shard_map/ppermute | solution.py:670
  227.4 29.0 %collective-permute-start.47 = (bf16[24,3840]{1,0:T(8,128)(2,1)}, bf16[24,3840]{1,0:T(8,128)(2,1)}, u32[]{:S(2)}, u32[]{:S(2)}) collective-permute-start(bf16[24,3840]{1,0:T(8,128)(2,1)} %get-tuple-element.110), channel_id=1, source_target_pairs={{0,16},{8,24},{16,0},{24,8},{1,17},{9,25},{17,1},{25,9},{2,18},{10... | collective-permute-start | bytes 552968 | tf_op jit(solution)/shard_map/ppermute | solution.py:670
  231.6 14.2 %collective-permute-start.40 = (bf16[96,2304]{1,0:T(8,128)(2,1)}, bf16[96,2304]{1,0:T(8,128)(2,1)S(1)}, u32[]{:S(2)}, u32[]{:S(2)}) collective-permute-start(bf16[96,2304]{1,0:T(8,128)(2,1)} %get-tuple-element.120), channel_id=1, source_target_pairs={{0,2},{2,0},{4,6},{6,4},{1,3},{3,1},{5,7},{7,5},{8,10},{10,8},{12,... | collective-permute-start | bytes 1327112 | tf_op jit(solution)/shard_map/ppermute | solution.py:670
  232.8 13.4 %collective-permute-start.41 = (bf16[96,2304]{1,0:T(8,128)(2,1)}, bf16[96,2304]{1,0:T(8,128)(2,1)S(1)}, u32[]{:S(2)}, u32[]{:S(2)}) collective-permute-start(bf16[96,2304]{1,0:T(8,128)(2,1)} %get-tuple-element.122), channel_id=1, source_target_pairs={{0,4},{2,6},{4,0},{6,2},{1,5},{3,7},{5,1},{7,3},{8,12},{10,14},{12... | collective-permute-start | bytes 1327112 | tf_op jit(solution)/shard_map/ppermute | solution.py:670
  233.6 20.8 %collective-permute-start.42 = (bf16[96,2304]{1,0:T(8,128)(2,1)S(1)}, bf16[96,2304]{1,0:T(8,128)(2,1)S(1)}, u32[]{:S(2)}, u32[]{:S(2)}) collective-permute-start(bf16[96,2304]{1,0:T(8,128)(2,1)S(1)} %get-tuple-element.121), channel_id=1, source_target_pairs={{0,6},{2,4},{4,2},{6,0},{1,7},{3,5},{5,3},{7,1},{8,14},{10,12},{12... | collective-permute-start | bytes 1327112 | tf_op jit(solution)/shard_map/ppermute | solution.py:670
  235.1 10.7 %copy-start.35 = (bf16[24,3840]{1,0:T(8,128)(2,1)S(1)}, bf16[24,3840]{1,0:T(8,128)(2,1)}, u32[]{:S(2)}) copy-start(bf16[24,3840]{1,0:T(8,128)(2,1)} %get-tuple-element.109) | copy-start | bytes 552964
  245.8 10.6 %collective-permute-start.48 = (bf16[24,3840]{1,0:T(8,128)(2,1)S(1)}, bf16[24,3840]{1,0:T(8,128)(2,1)S(1)}, u32[]{:S(2)}, u32[]{:S(2)}) collective-permute-start(bf16[24,3840]{1,0:T(8,128)(2,1)S(1)} %copy-done.35), channel_id=1, source_target_pairs={{0,24},{8,16},{16,8},{24,0},{1,25},{9,17},{17,9},{25,1},{2,26},{10... | collective-permute-start | bytes 552968 | tf_op jit(solution)/shard_map/ppermute | solution.py:670
  257.1 7.8 %copy-start.40 = (f32[1,3072]{1,0:T(1,128)S(1)}, f32[1,3072]{1,0:T(1,128)}, u32[]{:S(2)}) copy-start(f32[1,3072]{1,0:T(1,128)} %get-tuple-element.106) | copy-start | bytes 36868
  257.2 12.5 %copy-start.24 = (bf16[96,768]{1,0:T(8,128)(2,1)S(1)}, bf16[96,768]{1,0:T(8,128)(2,1)}, u32[]{:S(2)}) copy-start(bf16[96,768]{1,0:T(8,128)(2,1)} %copy-done.23) | copy-start | bytes 442372
  257.2 12.5 %copy-start.26 = (bf16[96,768]{1,0:T(8,128)(2,1)S(1)}, bf16[96,768]{1,0:T(8,128)(2,1)}, u32[]{:S(2)}) copy-start(bf16[96,768]{1,0:T(8,128)(2,1)} %copy-done.25) | copy-start | bytes 442372
  257.2 12.5 %copy-start.28 = (bf16[96,768]{1,0:T(8,128)(2,1)S(1)}, bf16[96,768]{1,0:T(8,128)(2,1)}, u32[]{:S(2)}) copy-start(bf16[96,768]{1,0:T(8,128)(2,1)} %copy-done.27) | copy-start | bytes 442372
  258.9 19.4 %collective-permute-start.43 = (bf16[24,2304]{1,0:T(8,128)(2,1)S(1)}, bf16[24,2304]{1,0:T(8,128)(2,1)S(1)}, u32[]{:S(2)}, u32[]{:S(2)}) collective-permute-start(bf16[24,2304]{1,0:T(8,128)(2,1)S(1)} %copy-done.32), channel_id=1, source_target_pairs={{0,8},{8,0},{16,24},{24,16},{1,9},{9,1},{17,25},{25,17},{2,10},{10... | collective-permute-start | bytes 331784 | tf_op jit(solution)/shard_map/ppermute | solution.py:670
  259.3 18.9 %collective-permute-start.44 = (bf16[24,2304]{1,0:T(8,128)(2,1)S(1)}, bf16[24,2304]{1,0:T(8,128)(2,1)S(1)}, u32[]{:S(2)}, u32[]{:S(2)}) collective-permute-start(bf16[24,2304]{1,0:T(8,128)(2,1)S(1)} %copy-done.31), channel_id=1, source_target_pairs={{0,16},{8,24},{16,0},{24,8},{1,17},{9,25},{17,1},{25,9},{2,18},{10... | collective-permute-start | bytes 331784 | tf_op jit(solution)/shard_map/ppermute | solution.py:670
  260.2 18.1 %collective-permute-start.45 = (bf16[24,2304]{1,0:T(8,128)(2,1)S(1)}, bf16[24,2304]{1,0:T(8,128)(2,1)S(1)}, u32[]{:S(2)}, u32[]{:S(2)}) collective-permute-start(bf16[24,2304]{1,0:T(8,128)(2,1)S(1)} %copy-done.30), channel_id=1, source_target_pairs={{0,24},{8,16},{16,8},{24,0},{1,25},{9,17},{17,9},{25,1},{2,26},{10... | collective-permute-start | bytes 331784 | tf_op jit(solution)/shard_map/ppermute | solution.py:670
  267.1 9.8 %all-to-all-start.2 = ((bf16[32,2,192]{2,1,0:T(2,128)(2,1)}), bf16[32,2,192]{2,1,0:T(2,128)(2,1)S(1)}, u32[]{:S(2)}, u32[]{:S(2)}) async-start(bf16[32,2,192]{2,1,0:T(2,128)(2,1)} %reshape.227), calls=%async_computation.2 | async-start | bytes 65536 | tf_op jit(solution)/shard_map/all_to_all | solution.py:827
  (36 other events, 79.9 us)

commit v3 on v2

--- a/solution.py
+++ b/solution.py
@@ -768,8 +768,6 @@
     head_parts = gather_plane(head)
     (wide,) = gate([wide], small[1:2])
     wide = spread(wide, "a")
-    (tall,) = gate([tall], [wide])
-    tall = spread(tall, "a")
     small = jnp.concatenate(small, axis=0).reshape(-1, BLK)
     small = jnp.concatenate([small, swap_cores(small)], axis=0)
     small = dot_tn(turn, small).reshape(devices, slots)
@@ -778,7 +776,10 @@
     b1 = small[:, nvec : nvec + b_fc1.shape[0]].reshape(1, FF)
     (wide,) = gate([wide], head_parts[1:])
     wide_parts = gather_plane(wide)
-    head_parts = head_parts + [swap_cores(p) for p in head_parts]
+    swapped = [swap_cores(p) for p in head_parts]
+    head_parts = head_parts + swapped
+    (tall,) = gate([tall], swapped + [wide, vec])
+    tall = spread(tall, "a")
     if not direct:
         head_parts = [by_owner(head_parts, owners).reshape(-1, D // 32, 3 * D)]
     (q, k, v, h1t, wqkv, o, lse), _ = attend_call(img_lens, valid_rows, me, head_parts, inputs, turn, vec)

time: 285 us -> 281 us (0.986)
  waiting for transfers between devices: 45.7 us -> 37.2 us
    ppermute x33, waiting for transfers between devices: 36.9 us -> 30.2 us  [from_peer(): lax.ppermute(x, axes, [(i, i ^ k) for i in range(lax.axis_size(axes))])]
  transfers between devices with their start and end apart: 52 -> 52, of which waited for: 12 -> 11; matrix products, arithmetic and copies ran while one was open for 11% -> 12% of each run, Pallas kernels for 46% -> 47%
where the time goes in v3:
time: 281 us; the launch traced here: 276 us
  Pallas kernels  129 us (46%)
  starting transfers between devices  57.7 us (21%)
  waiting for transfers between devices  37.2 us (13%)
  local copies, waits for them, and re-layouts  24.9 us (9%)
  other arithmetic  23.4 us (8%)
    ppermute x33, starting transfers between devices, from_peer(): lax.ppermute(x, axes, [(i, i ^ k) for i in range(lax.axis_size(axes))])  44.6 us
    pallas_call x1, Pallas kernels, down_call(): pl.pallas_call(functools.partial(down_kernel, count), grid=(STEPS + ROWS...  37.6 us
    ppermute x33, waiting for transfers between devices, from_peer(): lax.ppermute(x, axes, [(i, i ^ k) for i in range(lax.axis_size(axes))])  30.2 us
    pallas_call x1, Pallas kernels, back_call(): pl.pallas_call(functools.partial(back_kernel, len(passed)), grid=(steps +...  29.1 us
    pallas_call x1, Pallas kernels, up_call(): pl.pallas_call(functools.partial(up_kernel, count), grid_spec=pltpu.Prefe...  29.1 us
    pallas_call x1, Pallas kernels, attend_call(): pl.pallas_call(functools.partial(attend_kernel, count, len(passed)), grid...  22.6 us
    convert_element_type x6, other arithmetic, blocks(): return (block(0), [add(block(k)).astype(bf16) for k in range(1, count)])  12.3 us
    unnamed x105, local copies, waits for them, and re-layouts  11.9 us
  transfers between devices with their start and end apart: 52, of which 11 were waited for; matrix products, arithmetic and copies ran while one was open for 12% of the time, Pallas kernels for 47%

profile of v3, /device:TPU:0, one launch (start us, length us, event | category | flops | bytes accessed | tf_op | source)
XLA Modules:
  0.0 276.4 jit_solution(13898469750869565389)
XLA Ops:
  2.0 0.9 convert.37
  3.2 5.1 %collective-permute-start.2 = (bf16[24,2432]{1,0:T(8,128)(2,1)S(1)}, bf16[24,2432]{1,0:T(8,128)(2,1)S(1)}, u32[]{:S(2)}, u32[]{:S(2)}) collective-permute-start(bf16[24,2432]{1,0:T(8,128)(2,1)S(1)} %pad_maximum_fusion.2), channel_id=1, source_target_pairs={{0,24},{8,16},{16,8},{24,0},{1,25},{9,17},{17,9},{25,1},{2,26},{10... | collective-permute-start | bytes 350216 | tf_op jit(solution)/shard_map/ppermute | solution.py:670
  9.2 1.0 convert_element_type.365
  11.3 1.3 fusion.1.refs_9_.turn_ref
  13.9 4.3 %collective-permute-done.1 = bf16[24,2432]{1,0:T(8,128)(2,1)S(1)} collective-permute-done((bf16[24,2432]{1,0:T(8,128)(2,1)S(1)}, bf16[24,2432]{1,0:T(8,128)(2,1)S(1)}, u32[]{:S(2)}, u32[]{:S(2)}) %collective-permute-start.1) | collective-permute-done | bytes 116768 | tf_op jit(solution)/shard_map/ppermute | solution.py:670
  18.2 1.6 collective-permute-start.10
  19.8 1.5 collective-permute-start.11
  21.9 1.6 collective-permute-start.3
  23.5 1.5 collective-permute-start.4
  25.6 1.8 broadcast_in_dim.4
  27.4 3.7 %all-to-all-start = ((bf16[4,5,24,768]{3,2,1,0:T(8,128)(2,1)}), bf16[4,5,24,768]{3,2,1,0:T(8,128)(2,1)S(1)}, u32[]{:S(2)}, u32[]{:S(2)}) async-start(bf16[4,5,24,768]{3,2,1,0:T(8,128)(2,1)} %broadcast_in_dim.4), calls=%async_computation | async-start | bytes 1474560 | tf_op jit(solution)/shard_map/all_to_all | solution.py:704
  31.3 3.4 %collective-permute-done.3.refs_1_ = bf16[4,24,2304]{2,1,0:T(8,128)(2,1)S(1)} collective-permute-done((bf16[4,24,2304]{2,1,0:T(8,128)(2,1)S(1)}, bf16[4,24,2304]{2,1,0:T(8,128)(2,1)S(1)}, u32[]{:S(2)}, u32[]{:S(2)}) %collective-permute-start.3) | collective-permute-done | bytes 442400 | tf_op jit(solution)/shard_map/ppermute | solution.py:670
  34.7 1.9 collective-permute-done.4.refs_2_
  36.6 6.8 %collective-permute-done.5.refs_3_ = bf16[4,24,2304]{2,1,0:T(8,128)(2,1)} collective-permute-done((bf16[4,24,2304]{2,1,0:T(8,128)(2,1)S(1)}, bf16[4,24,2304]{2,1,0:T(8,128)(2,1)}, u32[]{:S(2)}, u32[]{:S(2)}) %collective-permute-start.5) | collective-permute-done | bytes 442400 | tf_op jit(solution)/shard_map/ppermute | solution.py:670
  45.3 1.7 fusion
  47.0 1.1 reshape.211
  48.8 0.9 copy-done.1
  49.7 1.5 collective-permute-start.14
  51.2 1.2 collective-permute-start.15
  53.2 1.8 broadcast_in_dim.5
  55.0 4.1 %all-to-all-start.1 = ((bf16[4,96,768]{2,1,0:T(8,128)(2,1)}), bf16[4,96,768]{2,1,0:T(8,128)(2,1)S(1)}, u32[]{:S(2)}, u32[]{:S(2)}) async-start(bf16[4,96,768]{2,1,0:T(8,128)(2,1)} %broadcast_in_dim.5), calls=%async_computation.1 | async-start | bytes 1179648 | tf_op jit(solution)/shard_map/all_to_all | solution.py:704
  59.1 22.6 %attend.1 = (bf16[1024,768]{1,0:T(8,128)(2,1)}, bf16[1024,768]{1,0:T(8,128)(2,1)}, bf16[1024,768]{1,0:T(8,128)(2,1)}, bf16[768,1024]{1,0:T(8,128)(2,1)}, bf16[76...) custom-call(s32[1,12]{1,0:T(1,128)} %lens_ref.3, s32[1]{0:T(128)S(6)} %copy.78.valid_ref, ...), custom_call_target="tpu_custom_call" | custom-call | flops 27499999232 | bytes 75000000 | tf_op jit(solution)/shard_map/attend/pallas_call | solution.py:199
  81.8 3.7 %collective-permute-done.16.refs_3_ = bf16[4,5,24,768]{3,2,1,0:T(8,128)(2,1)S(1)} collective-permute-done((bf16[4,5,24,768]{3,2,1,0:T(8,128)(2,1)}, bf16[4,5,24,768]{3,2,1,0:T(8,128)(2,1)S(1)}, u32[]{:S(2)}, u32[]{:S(2)}) %collective-permute-start.16) | collective-permute-done | bytes 737312 | tf_op jit(solution)/shard_map/ppermute | solution.py:670
  85.5 0.9 copy-done.17
  88.3 1.5 collective-permute-start.21
  89.8 1.2 collective-permute-start.22
  91.1 2.2 collective-permute-start.23
  93.3 0.8 copy-done.43
  94.1 29.1 %mlp_up.1 = (f32[1024,768]{1,0:T(8,128)}, bf16[1024,768]{1,0:T(8,128)(2,1)}, bf16[768,1024]{1,0:T(8,128)(2,1)}, bf16[768,1024]{1,0:T(8,128)(2,1)}, bf16[1024,768...) custom-call(s32[3]{0:T(128)} %pad_add_fusion.me_ref, ...), custom_call_target="tpu_custom_call" | custom-call | flops 28600000512 | bytes 78000000 | tf_op jit(solution)/shard_map/mlp_up/pallas_call | solution.py:344
  123.3 0.8 copy-done.20
  124.4 1.1 copy-done.8
  126.6 2.5 collective-permute-done.28.refs_9_
  129.2 1.6 fusion.2
  131.6 0.8 collective-permute-start.30
  132.4 1.9 collective-permute-start.31
  135.1 0.9 copy-done.47
  136.0 37.6 %mlp_down.1 = (f32[1024,768]{1,0:T(8,128)}, f32[1024,768]{1,0:T(8,128)}, bf16[1024,768]{1,0:T(8,128)(2,1)}, bf16[384,3840]{1,0:T(8,128)(2,1)}, bf16[384,3840]{1,...) custom-call(s32[3]{0:T(128)} %pad_add_fusion.me_ref, ...), custom_call_target="tpu_custom_call", output_to_operand_aliasing={{7}: (21, {})} | custom-call | flops 38499999744 | bytes 105000000 | tf_op jit(solution)/shard_map/mlp_down/pallas_call | solution.py:465
  173.6 0.9 copy-done.11
  174.5 0.8 copy-done.12
  175.3 2.1 add_convert_fusion.9
  177.6 2.9 %collective-permute-start.37 = (bf16[96,768]{1,0:T(8,128)(2,1)S(1)}, bf16[96,768]{1,0:T(8,128)(2,1)S(1)}, u32[]{:S(2)}, u32[]{:S(2)}) collective-permute-start(bf16[96,768]{1,0:T(8,128)(2,1)S(1)} %get-tuple-element.112), channel_id=1, source_target_pairs={{0,16},{8,24},{16,0},{24,8},{1,17},{9,25},{17,1},{25,9},{2,18},{10... | collective-permute-start | bytes 442376 | tf_op jit(solution)/shard_map/ppermute | solution.py:670
  180.5 1.4 collective-permute-start.38
  181.9 2.0 add_convert_fusion
  184.9 0.8 collective-permute-start.34
  186.4 1.3 collective-permute-start.35
  187.6 29.1 %attend_back.1 = (bf16[1024,768]{1,0:T(8,128)(2,1)}, bf16[1024,768]{1,0:T(8,128)(2,1)}, bf16[1024,768]{1,0:T(8,128)(2,1)}, bf16[384,2304]{1,0:T(8,128)(2,1)}, bf...) custom-call(s32[1,12]{1,0:T(1,128)} %lens_ref.3, ...), custom_call_target="tpu_custom_call", output_to_operand_aliasing={{6}: (9, {}), {7}: (10, {})} | custom-call | flops 36300001280 | bytes 99000000 | tf_op jit(solution)/shard_map/attend_back/pallas_call | solution.py:590
  216.9 2.4 collective-permute-done.35.refs_3_
  219.3 0.9 copy-done.5
  220.1 3.0 %add_convert_fusion.8 = (bf16[24,3840]{1,0:T(8,128)(2,1)}, bf16[24,3840]{1,0:T(8,128)(2,1)}, bf16[24,3840]{1,0:T(8,128)(2,1)}) fusion(bf16[96,3840]{1,0:T(8,128)(2,1)} %copy-done.5, bf16[96,3840]{1,0:T(8,128)(2,1)} %copy-done.4, bf16[96,3840]{1,0:T(8,128)(2,1)} %copy-done.3, bf16[384,3840]{1,0:T(8,128)(2,1)} %copy-done.6, ...), kind=kLoop, calls=%fused_computation.20 | loop fusion | flops 2764800 | bytes 3317760 | tf_op jit(solution)/shard_map/convert_element_type | solution.py:736
  223.1 3.1 %collective-permute-start.47 = (bf16[24,3840]{1,0:T(8,128)(2,1)}, bf16[24,3840]{1,0:T(8,128)(2,1)}, u32[]{:S(2)}, u32[]{:S(2)}) collective-permute-start(bf16[24,3840]{1,0:T(8,128)(2,1)} %get-tuple-element.110), channel_id=1, source_target_pairs={{0,16},{8,24},{16,0},{24,8},{1,17},{9,25},{17,1},{25,9},{2,18},{10... | collective-permute-start | bytes 552968 | tf_op jit(solution)/shard_map/ppermute | solution.py:670
  226.2 1.5 add_convert_fusion.5
  228.3 1.0 collective-permute-start.41
  229.3 1.9 collective-permute-start.42
  231.2 10.7 %input_back.1 = (f32[1024,768]{1,0:T(8,128)}, f32[8,768]{1,0:T(8,128)}, bf16[384,3840]{1,0:T(8,128)(2,1)}, bf16[384,2304]{1,0:T(8,128)(2,1)}, bf16[1536,768]{1,0:T(8,128)(2,1)}) custom-call(bf16[1024,768]{1,0:T(8,128)(2,1)} %get-tuple-element.85.dq_ref, ...), custom_call_target="tpu_custom_call", output_to_operand_aliasing={{2}: (7, {}), {3}: (8, {}), {4}: (9, {})} | custom-call | flops 14300000256 | bytes 39000000 | tf_op jit(solution)/shard_map/input_back/pallas_call | solution.py:650
  241.9 1.4 collective-permute-start.48
  243.3 7.1 %collective-permute-done.42 = bf16[96,2304]{1,0:T(8,128)(2,1)S(1)} collective-permute-done((bf16[96,2304]{1,0:T(8,128)(2,1)S(1)}, bf16[96,2304]{1,0:T(8,128)(2,1)S(1)}, u32[]{:S(2)}, u32[]{:S(2)}) %collective-permute-start.42) | collective-permute-done | bytes 442400 | tf_op jit(solution)/shard_map/ppermute | solution.py:670
  250.5 2.0 add_convert_fusion.14
  253.3 1.7 convert_add_fusion.3
  255.4 1.6 collective-permute-start.44
  257.0 2.5 collective-permute-start.45
  263.2 2.6 all-to-all-start.2
  265.8 1.4 convert_add_fusion.4
  269.3 3.7 %all-to-all-done.2 = bf16[32,2,192]{2,1,0:T(2,128)(2,1)S(1)} async-done(((bf16[32,2,192]{2,1,0:T(2,128)(2,1)}), bf16[32,2,192]{2,1,0:T(2,128)(2,1)S(1)}, u32[]{:S(2)}, u32[]{:S(2)}) %all-to-all-start.2) | async-done | bytes 24608 | tf_op jit(solution)/shard_map/all_to_all | solution.py:828
  274.4 1.1 convert_add_fusion.5
  (223 shorter events, 25.5 us)
Async XLA Ops:
  0.6 9.7 %copy-start.38 = (f32[18432]{0:T(1024)S(1)}, f32[18432]{0:T(1024)}, u32[]{:S(2)}) copy-start(f32[18432]{0:T(1024)} %param.14) | copy-start | bytes 221188
  0.6 9.8 %copy-start.34 = (f32[73728]{0:T(1024)S(1)}, f32[73728]{0:T(1024)}, u32[]{:S(2)}) copy-start(f32[73728]{0:T(1024)} %param.17) | copy-start | bytes 884740
  3.2 10.6 %collective-permute-start.2 = (bf16[24,2432]{1,0:T(8,128)(2,1)S(1)}, bf16[24,2432]{1,0:T(8,128)(2,1)S(1)}, u32[]{:S(2)}, u32[]{:S(2)}) collective-permute-start(bf16[24,2432]{1,0:T(8,128)(2,1)S(1)} %pad_maximum_fusion.2), channel_id=1, source_target_pairs={{0,24},{8,16},{16,8},{24,0},{1,25},{9,17},{17,9},{25,1},{2,26},{10... | collective-permute-start | bytes 350216 | tf_op jit(solution)/shard_map/ppermute | solution.py:670
  8.4 9.8 %collective-permute-start.1 = (bf16[24,2432]{1,0:T(8,128)(2,1)S(1)}, bf16[24,2432]{1,0:T(8,128)(2,1)S(1)}, u32[]{:S(2)}, u32[]{:S(2)}) collective-permute-start(bf16[24,2432]{1,0:T(8,128)(2,1)S(1)} %pad_maximum_fusion.2), channel_id=1, source_target_pairs={{0,16},{8,24},{16,0},{24,8},{1,17},{9,25},{17,1},{25,9},{2,18},{10... | collective-permute-start | bytes 350216 | tf_op jit(solution)/shard_map/ppermute | solution.py:670
  8.4 9.8 %collective-permute-start = (bf16[24,2432]{1,0:T(8,128)(2,1)S(1)}, bf16[24,2432]{1,0:T(8,128)(2,1)S(1)}, u32[]{:S(2)}, u32[]{:S(2)}) collective-permute-start(bf16[24,2432]{1,0:T(8,128)(2,1)S(1)} %pad_maximum_fusion.2), channel_id=1, source_target_pairs={{0,8},{8,0},{16,24},{24,16},{1,9},{9,1},{17,25},{25,17},{2,10},{10... | collective-permute-start | bytes 350216 | tf_op jit(solution)/shard_map/ppermute | solution.py:670
  18.2 6.8 %collective-permute-start.10 = (bf16[4,24,128]{2,1,0:T(8,128)(2,1)S(1)}, bf16[4,24,128]{2,1,0:T(8,128)(2,1)S(1)}, u32[]{:S(2)}, u32[]{:S(2)}) collective-permute-start(bf16[4,24,128]{2,1,0:T(8,128)(2,1)S(1)} %pad_maximum_fusion.3), channel_id=1, source_target_pairs={{0,2},{2,0},{4,6},{6,4},{1,3},{3,1},{5,7},{7,5},{8,10},{10,8},{12,... | collective-permute-start | bytes 73736 | tf_op jit(solution)/shard_map/ppermute | solution.py:670
  19.8 11.4 %collective-permute-start.11 = (bf16[4,24,128]{2,1,0:T(8,128)(2,1)S(1)}, bf16[4,24,128]{2,1,0:T(8,128)(2,1)S(1)}, u32[]{:S(2)}, u32[]{:S(2)}) collective-permute-start(bf16[4,24,128]{2,1,0:T(8,128)(2,1)S(1)} %pad_maximum_fusion.3), channel_id=1, source_target_pairs={{0,4},{2,6},{4,0},{6,2},{1,5},{3,7},{5,1},{7,3},{8,12},{10,14},{12... | collective-permute-start | bytes 73736 | tf_op jit(solution)/shard_map/ppermute | solution.py:670
  21.3 22.1 %collective-permute-start.12 = (bf16[4,24,128]{2,1,0:T(8,128)(2,1)S(1)}, bf16[4,24,128]{2,1,0:T(8,128)(2,1)S(1)}, u32[]{:S(2)}, u32[]{:S(2)}) collective-permute-start(bf16[4,24,128]{2,1,0:T(8,128)(2,1)S(1)} %pad_maximum_fusion.3), channel_id=1, source_target_pairs={{0,6},{2,4},{4,2},{6,0},{1,7},{3,5},{5,3},{7,1},{8,14},{10,12},{12... | collective-permute-start | bytes 73736 | tf_op jit(solution)/shard_map/ppermute | solution.py:670
  21.9 25.1 %copy-start.28 = (bf16[4,24,2304]{2,1,0:T(8,128)(2,1)}, bf16[4,24,2304]{2,1,0:T(8,128)(2,1)S(1)}, u32[]{:S(2)}) copy-start(bf16[4,24,2304]{2,1,0:T(8,128)(2,1)S(1)} %pad_maximum_fusion.refs_0_) | copy-start | bytes 1327108
  21.9 12.8 %collective-permute-start.3 = (bf16[4,24,2304]{2,1,0:T(8,128)(2,1)S(1)}, bf16[4,24,2304]{2,1,0:T(8,128)(2,1)S(1)}, u32[]{:S(2)}, u32[]{:S(2)}) collective-permute-start(bf16[4,24,2304]{2,1,0:T(8,128)(2,1)S(1)} %pad_maximum_fusion.refs_0_), channel_id=1, source_target_pairs={{0,2},{2,0},{4,6},{6,4},{1,3},{3,1},{5,7},{7,5},{8,10},{10,8},{12,... | collective-permute-start | bytes 1327112 | tf_op jit(solution)/shard_map/ppermute | solution.py:670
  23.5 13.1 %collective-permute-start.4 = (bf16[4,24,2304]{2,1,0:T(8,128)(2,1)S(1)}, bf16[4,24,2304]{2,1,0:T(8,128)(2,1)S(1)}, u32[]{:S(2)}, u32[]{:S(2)}) collective-permute-start(bf16[4,24,2304]{2,1,0:T(8,128)(2,1)S(1)} %pad_maximum_fusion.refs_0_), channel_id=1, source_target_pairs={{0,4},{2,6},{4,0},{6,2},{1,5},{3,7},{5,1},{7,3},{8,12},{10,14},{12... | collective-permute-start | bytes 1327112 | tf_op jit(solution)/shard_map/ppermute | solution.py:670
  25.0 18.4 %collective-permute-start.5 = (bf16[4,24,2304]{2,1,0:T(8,128)(2,1)S(1)}, bf16[4,24,2304]{2,1,0:T(8,128)(2,1)}, u32[]{:S(2)}, u32[]{:S(2)}) collective-permute-start(bf16[4,24,2304]{2,1,0:T(8,128)(2,1)S(1)} %pad_maximum_fusion.refs_0_), channel_id=1, source_target_pairs={{0,6},{2,4},{4,2},{6,0},{1,7},{3,5},{5,3},{7,1},{8,14},{10,12},{12... | collective-permute-start | bytes 1327112 | tf_op jit(solution)/shard_map/ppermute | solution.py:670
  27.4 21.4 %all-to-all-start = ((bf16[4,5,24,768]{3,2,1,0:T(8,128)(2,1)}), bf16[4,5,24,768]{3,2,1,0:T(8,128)(2,1)S(1)}, u32[]{:S(2)}, u32[]{:S(2)}) async-start(bf16[4,5,24,768]{3,2,1,0:T(8,128)(2,1)} %broadcast_in_dim.4), calls=%async_computation | async-start | bytes 1474560 | tf_op jit(solution)/shard_map/all_to_all | solution.py:704
  31.2 20.0 %collective-permute-start.6 = (bf16[4,24,2304]{2,1,0:T(8,128)(2,1)S(1)}, bf16[4,24,2304]{2,1,0:T(8,128)(2,1)}, u32[]{:S(2)}, u32[]{:S(2)}) collective-permute-start(bf16[4,24,2304]{2,1,0:T(8,128)(2,1)S(1)} %pad_maximum_fusion.refs_0_), channel_id=1, source_target_pairs={{0,1},{1,0},{2,3},{3,2},{4,5},{5,4},{6,7},{7,6},{8,9},{9,8},{10,11... | collective-permute-start | bytes 1327112 | tf_op jit(solution)/shard_map/ppermute | solution.py:666
  34.7 14.1 %copy-start.29 = (bf16[4,24,2304]{2,1,0:T(8,128)(2,1)}, bf16[4,24,2304]{2,1,0:T(8,128)(2,1)S(1)}, u32[]{:S(2)}) copy-start(bf16[4,24,2304]{2,1,0:T(8,128)(2,1)S(1)} %collective-permute-done.3.refs_1_) | copy-start | bytes 1327108
  34.7 17.8 %collective-permute-start.7 = (bf16[4,24,2304]{2,1,0:T(8,128)(2,1)S(1)}, bf16[4,24,2304]{2,1,0:T(8,128)(2,1)}, u32[]{:S(2)}, u32[]{:S(2)}) collective-permute-start(bf16[4,24,2304]{2,1,0:T(8,128)(2,1)S(1)} %collective-permute-done.3.refs_1_), channel_id=1, source_target_pairs={{0,1},{1,0},{2,3},{3,2},{4,5},{5,4},{6,7},{7,6},{8,9},{9,8},{10,11... | collective-permute-start | bytes 1327112 | tf_op jit(solution)/shard_map/ppermute | solution.py:666
  36.6 12.2 %copy-start.30 = (bf16[4,24,2304]{2,1,0:T(8,128)(2,1)}, bf16[4,24,2304]{2,1,0:T(8,128)(2,1)S(1)}, u32[]{:S(2)}) copy-start(bf16[4,24,2304]{2,1,0:T(8,128)(2,1)S(1)} %collective-permute-done.4.refs_2_) | copy-start | bytes 1327108
  36.6 16.6 %collective-permute-start.8 = (bf16[4,24,2304]{2,1,0:T(8,128)(2,1)S(1)}, bf16[4,24,2304]{2,1,0:T(8,128)(2,1)}, u32[]{:S(2)}, u32[]{:S(2)}) collective-permute-start(bf16[4,24,2304]{2,1,0:T(8,128)(2,1)S(1)} %collective-permute-done.4.refs_2_), channel_id=1, source_target_pairs={{0,1},{1,0},{2,3},{3,2},{4,5},{5,4},{6,7},{7,6},{8,9},{9,8},{10,11... | collective-permute-start | bytes 1327112 | tf_op jit(solution)/shard_map/ppermute | solution.py:666
  43.4 9.8 %collective-permute-start.9 = (bf16[4,24,2304]{2,1,0:T(8,128)(2,1)}, bf16[4,24,2304]{2,1,0:T(8,128)(2,1)}, u32[]{:S(2)}, u32[]{:S(2)}) collective-permute-start(bf16[4,24,2304]{2,1,0:T(8,128)(2,1)} %collective-permute-done.5.refs_3_), channel_id=1, source_target_pairs={{0,1},{1,0},{2,3},{3,2},{4,5},{5,4},{6,7},{7,6},{8,9},{9,8},{10,11... | collective-permute-start | bytes 1327112 | tf_op jit(solution)/shard_map/ppermute | solution.py:666
  43.4 1.9 collective-permute-start.13
  49.7 32.0 %collective-permute-start.14 = (bf16[4,5,24,768]{3,2,1,0:T(8,128)(2,1)}, bf16[4,5,24,768]{3,2,1,0:T(8,128)(2,1)S(1)}, u32[]{:S(2)}, u32[]{:S(2)}) collective-permute-start(bf16[4,5,24,768]{3,2,1,0:T(8,128)(2,1)} %gate.9.refs_5_.refs_0_), channel_id=1, source_target_pairs={{0,2},{2,0},{4,6},{6,4},{1,3},{3,1},{5,7},{7,5},{8,10},{10,8},{12,... | collective-permute-start | bytes 2211848 | tf_op jit(solution)/shard_map/ppermute | solution.py:670
  51.2 30.5 %collective-permute-start.15 = (bf16[4,5,24,768]{3,2,1,0:T(8,128)(2,1)}, bf16[4,5,24,768]{3,2,1,0:T(8,128)(2,1)S(1)}, u32[]{:S(2)}, u32[]{:S(2)}) collective-permute-start(bf16[4,5,24,768]{3,2,1,0:T(8,128)(2,1)} %gate.9.refs_5_.refs_0_), channel_id=1, source_target_pairs={{0,4},{2,6},{4,0},{6,2},{1,5},{3,7},{5,1},{7,3},{8,12},{10,14},{12... | collective-permute-start | bytes 2211848 | tf_op jit(solution)/shard_map/ppermute | solution.py:670
  52.5 33.0 %collective-permute-start.16 = (bf16[4,5,24,768]{3,2,1,0:T(8,128)(2,1)}, bf16[4,5,24,768]{3,2,1,0:T(8,128)(2,1)S(1)}, u32[]{:S(2)}, u32[]{:S(2)}) collective-permute-start(bf16[4,5,24,768]{3,2,1,0:T(8,128)(2,1)} %gate.9.refs_5_.refs_0_), channel_id=1, source_target_pairs={{0,6},{2,4},{4,2},{6,0},{1,7},{3,5},{5,3},{7,1},{8,14},{10,12},{12... | collective-permute-start | bytes 2211848 | tf_op jit(solution)/shard_map/ppermute | solution.py:670
  55.0 30.5 %all-to-all-start.1 = ((bf16[4,96,768]{2,1,0:T(8,128)(2,1)}), bf16[4,96,768]{2,1,0:T(8,128)(2,1)S(1)}, u32[]{:S(2)}, u32[]{:S(2)}) async-start(bf16[4,96,768]{2,1,0:T(8,128)(2,1)} %broadcast_in_dim.5), calls=%async_computation.1 | async-start | bytes 1179648 | tf_op jit(solution)/shard_map/all_to_all | solution.py:704
  86.5 3.3 %collective-permute-start.17 = (bf16[4,5,24,768]{3,2,1,0:T(8,128)(2,1)}, bf16[4,5,24,768]{3,2,1,0:T(8,128)(2,1)S(1)}, u32[]{:S(2)}, u32[]{:S(2)}) collective-permute-start(bf16[4,5,24,768]{3,2,1,0:T(8,128)(2,1)} %get-tuple-element.59.refs_0_), channel_id=1, source_target_pairs={{0,1},{1,0},{2,3},{3,2},{4,5},{5,4},{6,7},{7,6},{8,9},{9,8},{10,11... | collective-permute-start | bytes 2211848 | tf_op jit(solution)/shard_map/ppermute | solution.py:666
  86.5 4.5 %collective-permute-start.18 = (bf16[4,5,24,768]{3,2,1,0:T(8,128)(2,1)}, bf16[4,5,24,768]{3,2,1,0:T(8,128)(2,1)S(1)}, u32[]{:S(2)}, u32[]{:S(2)}) collective-permute-start(bf16[4,5,24,768]{3,2,1,0:T(8,128)(2,1)} %get-tuple-element.60.refs_1_), channel_id=1, source_target_pairs={{0,1},{1,0},{2,3},{3,2},{4,5},{5,4},{6,7},{7,6},{8,9},{9,8},{10,11... | collective-permute-start | bytes 2211848 | tf_op jit(solution)/shard_map/ppermute | solution.py:666
  87.0 6.2 %collective-permute-start.19 = (bf16[4,5,24,768]{3,2,1,0:T(8,128)(2,1)}, bf16[4,5,24,768]{3,2,1,0:T(8,128)(2,1)S(1)}, u32[]{:S(2)}, u32[]{:S(2)}) collective-permute-start(bf16[4,5,24,768]{3,2,1,0:T(8,128)(2,1)} %get-tuple-element.61.refs_2_), channel_id=1, source_target_pairs={{0,1},{1,0},{2,3},{3,2},{4,5},{5,4},{6,7},{7,6},{8,9},{9,8},{10,11... | collective-permute-start | bytes 2211848 | tf_op jit(solution)/shard_map/ppermute | solution.py:666
  87.0 6.2 %collective-permute-start.20 = (bf16[4,5,24,768]{3,2,1,0:T(8,128)(2,1)}, bf16[4,5,24,768]{3,2,1,0:T(8,128)(2,1)}, u32[]{:S(2)}, u32[]{:S(2)}) collective-permute-start(bf16[4,5,24,768]{3,2,1,0:T(8,128)(2,1)} %get-tuple-element.62.refs_3_), channel_id=1, source_target_pairs={{0,1},{1,0},{2,3},{3,2},{4,5},{5,4},{6,7},{7,6},{8,9},{9,8},{10,11... | collective-permute-start | bytes 2211848 | tf_op jit(solution)/shard_map/ppermute | solution.py:666
  88.3 34.9 %collective-permute-start.21 = (bf16[4,96,768]{2,1,0:T(8,128)(2,1)}, bf16[4,96,768]{2,1,0:T(8,128)(2,1)S(1)}, u32[]{:S(2)}, u32[]{:S(2)}) collective-permute-start(bf16[4,96,768]{2,1,0:T(8,128)(2,1)} %get-tuple-element.72.refs_0_), channel_id=1, source_target_pairs={{0,2},{2,0},{4,6},{6,4},{1,3},{3,1},{5,7},{7,5},{8,10},{10,8},{12,... | collective-permute-start | bytes 1769480 | tf_op jit(solution)/shard_map/ppermute | solution.py:670
  89.8 33.4 %collective-permute-start.22 = (bf16[4,96,768]{2,1,0:T(8,128)(2,1)}, bf16[4,96,768]{2,1,0:T(8,128)(2,1)S(1)}, u32[]{:S(2)}, u32[]{:S(2)}) collective-permute-start(bf16[4,96,768]{2,1,0:T(8,128)(2,1)} %get-tuple-element.72.refs_0_), channel_id=1, source_target_pairs={{0,4},{2,6},{4,0},{6,2},{1,5},{3,7},{5,1},{7,3},{8,12},{10,14},{12... | collective-permute-start | bytes 1769480 | tf_op jit(solution)/shard_map/ppermute | solution.py:670
  91.1 32.2 %collective-permute-start.23 = (bf16[4,96,768]{2,1,0:T(8,128)(2,1)}, bf16[4,96,768]{2,1,0:T(8,128)(2,1)S(1)}, u32[]{:S(2)}, u32[]{:S(2)}) collective-permute-start(bf16[4,96,768]{2,1,0:T(8,128)(2,1)} %get-tuple-element.72.refs_0_), channel_id=1, source_target_pairs={{0,6},{2,4},{4,2},{6,0},{1,7},{3,5},{5,3},{7,1},{8,14},{10,12},{12... | collective-permute-start | bytes 1769480 | tf_op jit(solution)/shard_map/ppermute | solution.py:670
  124.4 4.7 %collective-permute-start.28 = (bf16[1536,768]{1,0:T(8,128)(2,1)}, bf16[1536,768]{1,0:T(8,128)(2,1)S(1)}, u32[]{:S(2)}, u32[]{:S(2)}) collective-permute-start(bf16[1536,768]{1,0:T(8,128)(2,1)} %gate.12), channel_id=1, source_target_pairs={{0,1},{1,0},{2,3},{3,2},{4,5},{5,4},{6,7},{7,6},{8,9},{9,8},{10,11... | collective-permute-start | bytes 7077896 | tf_op jit(solution)/shard_map/ppermute | solution.py:666
  125.5 6.1 %collective-permute-start.24 = (bf16[4,96,768]{2,1,0:T(8,128)(2,1)S(1)}, bf16[4,96,768]{2,1,0:T(8,128)(2,1)S(1)}, u32[]{:S(2)}, u32[]{:S(2)}) collective-permute-start(bf16[4,96,768]{2,1,0:T(8,128)(2,1)S(1)} %copy-done.8), channel_id=1, source_target_pairs={{0,1},{1,0},{2,3},{3,2},{4,5},{5,4},{6,7},{7,6},{8,9},{9,8},{10,11... | collective-permute-start | bytes 1769480 | tf_op jit(solution)/shard_map/ppermute | solution.py:666
  125.5 6.9 %collective-permute-start.25 = (bf16[4,96,768]{2,1,0:T(8,128)(2,1)}, bf16[4,96,768]{2,1,0:T(8,128)(2,1)S(1)}, u32[]{:S(2)}, u32[]{:S(2)}) collective-permute-start(bf16[4,96,768]{2,1,0:T(8,128)(2,1)} %copy-done.19), channel_id=1, source_target_pairs={{0,1},{1,0},{2,3},{3,2},{4,5},{5,4},{6,7},{7,6},{8,9},{9,8},{10,11... | collective-permute-start | bytes 1769480 | tf_op jit(solution)/shard_map/ppermute | solution.py:666
  126.0 8.3 %collective-permute-start.26 = (bf16[4,96,768]{2,1,0:T(8,128)(2,1)}, bf16[4,96,768]{2,1,0:T(8,128)(2,1)S(1)}, u32[]{:S(2)}, u32[]{:S(2)}) collective-permute-start(bf16[4,96,768]{2,1,0:T(8,128)(2,1)} %copy-done.20), channel_id=1, source_target_pairs={{0,1},{1,0},{2,3},{3,2},{4,5},{5,4},{6,7},{7,6},{8,9},{9,8},{10,11... | collective-permute-start | bytes 1769480 | tf_op jit(solution)/shard_map/ppermute | solution.py:666
  126.0 8.3 %collective-permute-start.27 = (bf16[4,96,768]{2,1,0:T(8,128)(2,1)}, bf16[4,96,768]{2,1,0:T(8,128)(2,1)S(1)}, u32[]{:S(2)}, u32[]{:S(2)}) collective-permute-start(bf16[4,96,768]{2,1,0:T(8,128)(2,1)} %copy-done.21), channel_id=1, source_target_pairs={{0,1},{1,0},{2,3},{3,2},{4,5},{5,4},{6,7},{7,6},{8,9},{9,8},{10,11... | collective-permute-start | bytes 1769480 | tf_op jit(solution)/shard_map/ppermute | solution.py:666
  130.8 42.8 %collective-permute-start.29 = (bf16[384,768]{1,0:T(8,128)(2,1)}, bf16[384,768]{1,0:T(8,128)(2,1)S(1)}, u32[]{:S(2)}, u32[]{:S(2)}) collective-permute-start(bf16[384,768]{1,0:T(8,128)(2,1)} %get-tuple-element.125), channel_id=1, source_target_pairs={{0,2},{2,0},{4,6},{6,4},{1,3},{3,1},{5,7},{7,5},{8,10},{10,8},{12,... | collective-permute-start | bytes 1769480 | tf_op jit(solution)/shard_map/ppermute | solution.py:670
  131.6 42.0 %collective-permute-start.30 = (bf16[384,768]{1,0:T(8,128)(2,1)S(1)}, bf16[384,768]{1,0:T(8,128)(2,1)S(1)}, u32[]{:S(2)}, u32[]{:S(2)}) collective-permute-start(bf16[384,768]{1,0:T(8,128)(2,1)S(1)} %get-tuple-element.124), channel_id=1, source_target_pairs={{0,4},{2,6},{4,0},{6,2},{1,5},{3,7},{5,1},{7,3},{8,12},{10,14},{12... | collective-permute-start | bytes 1769480 | tf_op jit(solution)/shard_map/ppermute | solution.py:670
  132.4 41.2 %collective-permute-start.31 = (bf16[384,768]{1,0:T(8,128)(2,1)S(1)}, bf16[384,768]{1,0:T(8,128)(2,1)S(1)}, u32[]{:S(2)}, u32[]{:S(2)}) collective-permute-start(bf16[384,768]{1,0:T(8,128)(2,1)S(1)} %get-tuple-element.123), channel_id=1, source_target_pairs={{0,6},{2,4},{4,2},{6,0},{1,7},{3,5},{5,3},{7,1},{8,14},{10,12},{12... | collective-permute-start | bytes 1769480 | tf_op jit(solution)/shard_map/ppermute | solution.py:670
  175.3 6.6 %copy-start = (bf16[384,3840]{1,0:T(8,128)(2,1)S(1)}, bf16[384,3840]{1,0:T(8,128)(2,1)}, u32[]{:S(2)}) copy-start(bf16[384,3840]{1,0:T(8,128)(2,1)} %get-tuple-element.82.refs_0_) | copy-start | bytes 8847364
  175.3 6.5 %collective-permute-start.32 = (bf16[384,3840]{1,0:T(8,128)(2,1)}, bf16[384,3840]{1,0:T(8,128)(2,1)S(1)}, u32[]{:S(2)}, u32[]{:S(2)}) collective-permute-start(bf16[384,3840]{1,0:T(8,128)(2,1)} %gate.13), channel_id=1, source_target_pairs={{0,1},{1,0},{2,3},{3,2},{4,5},{5,4},{6,7},{7,6},{8,9},{9,8},{10,11... | collective-permute-start | bytes 8847368 | tf_op jit(solution)/shard_map/ppermute | solution.py:666
  177.4 8.9 %collective-permute-start.36 = (bf16[96,768]{1,0:T(8,128)(2,1)S(1)}, bf16[96,768]{1,0:T(8,128)(2,1)S(1)}, u32[]{:S(2)}, u32[]{:S(2)}) collective-permute-start(bf16[96,768]{1,0:T(8,128)(2,1)S(1)} %get-tuple-element.113), channel_id=1, source_target_pairs={{0,8},{8,0},{16,24},{24,16},{1,9},{9,1},{17,25},{25,17},{2,10},{10... | collective-permute-start | bytes 442376 | tf_op jit(solution)/shard_map/ppermute | solution.py:670
  177.6 39.2 %collective-permute-start.37 = (bf16[96,768]{1,0:T(8,128)(2,1)S(1)}, bf16[96,768]{1,0:T(8,128)(2,1)S(1)}, u32[]{:S(2)}, u32[]{:S(2)}) collective-permute-start(bf16[96,768]{1,0:T(8,128)(2,1)S(1)} %get-tuple-element.112), channel_id=1, source_target_pairs={{0,16},{8,24},{16,0},{24,8},{1,17},{9,25},{17,1},{25,9},{2,18},{10... | collective-permute-start | bytes 442376 | tf_op jit(solution)/shard_map/ppermute | solution.py:670
  180.5 36.3 %collective-permute-start.38 = (bf16[96,768]{1,0:T(8,128)(2,1)S(1)}, bf16[96,768]{1,0:T(8,128)(2,1)S(1)}, u32[]{:S(2)}, u32[]{:S(2)}) collective-permute-start(bf16[96,768]{1,0:T(8,128)(2,1)S(1)} %get-tuple-element.111), channel_id=1, source_target_pairs={{0,24},{8,16},{16,8},{24,0},{1,25},{9,17},{17,9},{25,1},{2,26},{10... | collective-permute-start | bytes 442376 | tf_op jit(solution)/shard_map/ppermute | solution.py:670
  184.1 32.7 %collective-permute-start.33 = (bf16[96,3840]{1,0:T(8,128)(2,1)}, bf16[96,3840]{1,0:T(8,128)(2,1)S(1)}, u32[]{:S(2)}, u32[]{:S(2)}) collective-permute-start(bf16[96,3840]{1,0:T(8,128)(2,1)} %get-tuple-element.116), channel_id=1, source_target_pairs={{0,2},{2,0},{4,6},{6,4},{1,3},{3,1},{5,7},{7,5},{8,10},{10,8},{12,... | collective-permute-start | bytes 2211848 | tf_op jit(solution)/shard_map/ppermute | solution.py:670
  184.9 31.9 %collective-permute-start.34 = (bf16[96,3840]{1,0:T(8,128)(2,1)}, bf16[96,3840]{1,0:T(8,128)(2,1)S(1)}, u32[]{:S(2)}, u32[]{:S(2)}) collective-permute-start(bf16[96,3840]{1,0:T(8,128)(2,1)} %get-tuple-element.115), channel_id=1, source_target_pairs={{0,4},{2,6},{4,0},{6,2},{1,5},{3,7},{5,1},{7,3},{8,12},{10,14},{12... | collective-permute-start | bytes 2211848 | tf_op jit(solution)/shard_map/ppermute | solution.py:670
  186.4 30.4 %copy-start.22 = (bf16[96,768]{1,0:T(8,128)(2,1)}, bf16[96,768]{1,0:T(8,128)(2,1)S(1)}, u32[]{:S(2)}) copy-start(bf16[96,768]{1,0:T(8,128)(2,1)S(1)} %collective-permute-done.36.refs_4_) | copy-start | bytes 442372
  186.4 32.9 %collective-permute-start.35 = (bf16[96,3840]{1,0:T(8,128)(2,1)}, bf16[96,3840]{1,0:T(8,128)(2,1)S(1)}, u32[]{:S(2)}, u32[]{:S(2)}) collective-permute-start(bf16[96,3840]{1,0:T(8,128)(2,1)} %get-tuple-element.114), channel_id=1, source_target_pairs={{0,6},{2,4},{4,2},{6,0},{1,7},{3,5},{5,3},{7,1},{8,14},{10,12},{12... | collective-permute-start | bytes 2211848 | tf_op jit(solution)/shard_map/ppermute | solution.py:670
  220.1 6.1 %collective-permute-start.39 = (bf16[384,2304]{1,0:T(8,128)(2,1)}, bf16[384,2304]{1,0:T(8,128)(2,1)S(1)}, u32[]{:S(2)}, u32[]{:S(2)}) collective-permute-start(bf16[384,2304]{1,0:T(8,128)(2,1)} %gate.14), channel_id=1, source_target_pairs={{0,1},{1,0},{2,3},{3,2},{4,5},{5,4},{6,7},{7,6},{8,9},{9,8},{10,11... | collective-permute-start | bytes 5308424 | tf_op jit(solution)/shard_map/ppermute | solution.py:666
  223.1 29.4 %collective-permute-start.46 = (bf16[24,3840]{1,0:T(8,128)(2,1)}, bf16[24,3840]{1,0:T(8,128)(2,1)}, u32[]{:S(2)}, u32[]{:S(2)}) collective-permute-start(bf16[24,3840]{1,0:T(8,128)(2,1)} %get-tuple-element.108), channel_id=1, source_target_pairs={{0,8},{8,0},{16,24},{24,16},{1,9},{9,1},{17,25},{25,17},{2,10},{10... | collective-permute-start | bytes 552968 | tf_op jit(solution)/shard_map/ppermute | solution.py:670
  223.1 29.4 %collective-permute-start.47 = (bf16[24,3840]{1,0:T(8,128)(2,1)}, bf16[24,3840]{1,0:T(8,128)(2,1)}, u32[]{:S(2)}, u32[]{:S(2)}) collective-permute-start(bf16[24,3840]{1,0:T(8,128)(2,1)} %get-tuple-element.110), channel_id=1, source_target_pairs={{0,16},{8,24},{16,0},{24,8},{1,17},{9,25},{17,1},{25,9},{2,18},{10... | collective-permute-start | bytes 552968 | tf_op jit(solution)/shard_map/ppermute | solution.py:670
  227.7 14.2 %collective-permute-start.40 = (bf16[96,2304]{1,0:T(8,128)(2,1)}, bf16[96,2304]{1,0:T(8,128)(2,1)S(1)}, u32[]{:S(2)}, u32[]{:S(2)}) collective-permute-start(bf16[96,2304]{1,0:T(8,128)(2,1)} %get-tuple-element.120), channel_id=1, source_target_pairs={{0,2},{2,0},{4,6},{6,4},{1,3},{3,1},{5,7},{7,5},{8,10},{10,8},{12,... | collective-permute-start | bytes 1327112 | tf_op jit(solution)/shard_map/ppermute | solution.py:670
  228.3 15.0 %collective-permute-start.41 = (bf16[96,2304]{1,0:T(8,128)(2,1)}, bf16[96,2304]{1,0:T(8,128)(2,1)S(1)}, u32[]{:S(2)}, u32[]{:S(2)}) collective-permute-start(bf16[96,2304]{1,0:T(8,128)(2,1)} %get-tuple-element.122), channel_id=1, source_target_pairs={{0,4},{2,6},{4,0},{6,2},{1,5},{3,7},{5,1},{7,3},{8,12},{10,14},{12... | collective-permute-start | bytes 1327112 | tf_op jit(solution)/shard_map/ppermute | solution.py:670
  229.3 21.1 %collective-permute-start.42 = (bf16[96,2304]{1,0:T(8,128)(2,1)S(1)}, bf16[96,2304]{1,0:T(8,128)(2,1)S(1)}, u32[]{:S(2)}, u32[]{:S(2)}) collective-permute-start(bf16[96,2304]{1,0:T(8,128)(2,1)S(1)} %get-tuple-element.121), channel_id=1, source_target_pairs={{0,6},{2,4},{4,2},{6,0},{1,7},{3,5},{5,3},{7,1},{8,14},{10,12},{12... | collective-permute-start | bytes 1327112 | tf_op jit(solution)/shard_map/ppermute | solution.py:670
  231.2 10.7 %copy-start.35 = (bf16[24,3840]{1,0:T(8,128)(2,1)S(1)}, bf16[24,3840]{1,0:T(8,128)(2,1)}, u32[]{:S(2)}) copy-start(bf16[24,3840]{1,0:T(8,128)(2,1)} %get-tuple-element.109) | copy-start | bytes 552964
  241.9 10.6 %collective-permute-start.48 = (bf16[24,3840]{1,0:T(8,128)(2,1)S(1)}, bf16[24,3840]{1,0:T(8,128)(2,1)S(1)}, u32[]{:S(2)}, u32[]{:S(2)}) collective-permute-start(bf16[24,3840]{1,0:T(8,128)(2,1)S(1)} %copy-done.35), channel_id=1, source_target_pairs={{0,24},{8,16},{16,8},{24,0},{1,25},{9,17},{17,9},{25,1},{2,26},{10... | collective-permute-start | bytes 552968 | tf_op jit(solution)/shard_map/ppermute | solution.py:670
  253.2 7.8 %copy-start.40 = (f32[1,3072]{1,0:T(1,128)S(1)}, f32[1,3072]{1,0:T(1,128)}, u32[]{:S(2)}) copy-start(f32[1,3072]{1,0:T(1,128)} %get-tuple-element.106) | copy-start | bytes 36868
  253.2 12.5 %copy-start.23 = (bf16[96,768]{1,0:T(8,128)(2,1)S(1)}, bf16[96,768]{1,0:T(8,128)(2,1)}, u32[]{:S(2)}) copy-start(bf16[96,768]{1,0:T(8,128)(2,1)} %copy-done.22) | copy-start | bytes 442372
  253.2 12.5 %copy-start.25 = (bf16[96,768]{1,0:T(8,128)(2,1)S(1)}, bf16[96,768]{1,0:T(8,128)(2,1)}, u32[]{:S(2)}) copy-start(bf16[96,768]{1,0:T(8,128)(2,1)} %copy-done.24) | copy-start | bytes 442372
  253.3 12.5 %copy-start.27 = (bf16[96,768]{1,0:T(8,128)(2,1)S(1)}, bf16[96,768]{1,0:T(8,128)(2,1)}, u32[]{:S(2)}) copy-start(bf16[96,768]{1,0:T(8,128)(2,1)} %copy-done.26) | copy-start | bytes 442372
  255.0 19.4 %collective-permute-start.43 = (bf16[24,2304]{1,0:T(8,128)(2,1)S(1)}, bf16[24,2304]{1,0:T(8,128)(2,1)S(1)}, u32[]{:S(2)}, u32[]{:S(2)}) collective-permute-start(bf16[24,2304]{1,0:T(8,128)(2,1)S(1)} %copy-done.33), channel_id=1, source_target_pairs={{0,8},{8,0},{16,24},{24,16},{1,9},{9,1},{17,25},{25,17},{2,10},{10... | collective-permute-start | bytes 331784 | tf_op jit(solution)/shard_map/ppermute | solution.py:670
  255.4 18.9 %collective-permute-start.44 = (bf16[24,2304]{1,0:T(8,128)(2,1)S(1)}, bf16[24,2304]{1,0:T(8,128)(2,1)S(1)}, u32[]{:S(2)}, u32[]{:S(2)}) collective-permute-start(bf16[24,2304]{1,0:T(8,128)(2,1)S(1)} %copy-done.32), channel_id=1, source_target_pairs={{0,16},{8,24},{16,0},{24,8},{1,17},{9,25},{17,1},{25,9},{2,18},{10... | collective-permute-start | bytes 331784 | tf_op jit(solution)/shard_map/ppermute | solution.py:670
  257.0 17.4 %collective-permute-start.45 = (bf16[24,2304]{1,0:T(8,128)(2,1)S(1)}, bf16[24,2304]{1,0:T(8,128)(2,1)S(1)}, u32[]{:S(2)}, u32[]{:S(2)}) collective-permute-start(bf16[24,2304]{1,0:T(8,128)(2,1)S(1)} %copy-done.31), channel_id=1, source_target_pairs={{0,24},{8,16},{16,8},{24,0},{1,25},{9,17},{17,9},{25,1},{2,26},{10... | collective-permute-start | bytes 331784 | tf_op jit(solution)/shard_map/ppermute | solution.py:670
  263.2 9.8 %all-to-all-start.2 = ((bf16[32,2,192]{2,1,0:T(2,128)(2,1)}), bf16[32,2,192]{2,1,0:T(2,128)(2,1)S(1)}, u32[]{:S(2)}, u32[]{:S(2)}) async-start(bf16[32,2,192]{2,1,0:T(2,128)(2,1)} %reshape.227), calls=%async_computation.2 | async-start | bytes 65536 | tf_op jit(solution)/shard_map/all_to_all | solution.py:828
  (36 other events, 75.6 us)

commit v4 on v3

--- a/solution.py
+++ b/solution.py
@@ -774,6 +774,7 @@
     nvec = vectors.shape[0]
     vec = jnp.pad(small[:, :nvec].reshape(10, D), ((0, 6), (0, 0)))
     b1 = small[:, nvec : nvec + b_fc1.shape[0]].reshape(1, FF)
+    head_parts = head_parts[:1] + gate(head_parts[1:], [vec, b1])
     (wide,) = gate([wide], head_parts[1:])
     wide_parts = gather_plane(wide)
     swapped = [swap_cores(p) for p in head_parts]

time: 281 us -> 281 us (level)
    unnamed x105 -> x109, local copies, waits for them, and re-layouts: 11.9 us -> 12.7 us
  transfers between devices with their start and end apart: 52 -> 52, of which waited for: 11 -> 12; matrix products, arithmetic and copies ran while one was open for 12% -> 12% of each run, Pallas kernels for 47% -> 47%
where the time goes in v4:
time: 281 us; the launch traced here: 276 us
  Pallas kernels  129 us (46%)
  starting transfers between devices  58.3 us (21%)
  waiting for transfers between devices  35.3 us (13%)
  local copies, waits for them, and re-layouts  25.6 us (9%)
  other arithmetic  23.5 us (8%)
    ppermute x33, starting transfers between devices, from_peer(): lax.ppermute(x, axes, [(i, i ^ k) for i in range(lax.axis_size(axes))])  44.8 us
    pallas_call x1, Pallas kernels, down_call(): pl.pallas_call(functools.partial(down_kernel, count), grid=(STEPS + ROWS...  37.6 us
    pallas_call x1, Pallas kernels, back_call(): pl.pallas_call(functools.partial(back_kernel, len(passed)), grid=(steps +...  29.1 us
    pallas_call x1, Pallas kernels, up_call(): pl.pallas_call(functools.partial(up_kernel, count), grid_spec=pltpu.Prefe...  29.1 us
    ppermute x33, waiting for transfers between devices, from_peer(): lax.ppermute(x, axes, [(i, i ^ k) for i in range(lax.axis_size(axes))])  27.6 us
    pallas_call x1, Pallas kernels, attend_call(): pl.pallas_call(functools.partial(attend_kernel, count, len(passed)), grid...  22.7 us
    unnamed x109, local copies, waits for them, and re-layouts  12.7 us
    convert_element_type x6, other arithmetic, blocks(): return (block(0), [add(block(k)).astype(bf16) for k in range(1, count)])  12.3 us
  transfers between devices with their start and end apart: 52, of which 12 were waited for; matrix products, arithmetic and copies ran while one was open for 12% of the time, Pallas kernels for 47%

profile of v4, /device:TPU:0, one launch (start us, length us, event | category | flops | bytes accessed | tf_op | source)
XLA Modules:
  0.0 275.9 jit_solution(17315989548363665035)
XLA Ops:
  2.0 0.9 convert.37
  3.2 5.1 %collective-permute-start.2 = (bf16[24,2432]{1,0:T(8,128)(2,1)S(1)}, bf16[24,2432]{1,0:T(8,128)(2,1)S(1)}, u32[]{:S(2)}, u32[]{:S(2)}) collective-permute-start(bf16[24,2432]{1,0:T(8,128)(2,1)S(1)} %pad_maximum_fusion.2), channel_id=1, source_target_pairs={{0,24},{8,16},{16,8},{24,0},{1,25},{9,17},{17,9},{25,1},{2,26},{10... | collective-permute-start | bytes 350216 | tf_op jit(solution)/shard_map/ppermute | solution.py:670
  9.2 1.0 convert_element_type.365
  11.1 1.4 collective-permute-done.2
  12.4 5.7 %collective-permute-done.1 = bf16[24,2432]{1,0:T(8,128)(2,1)S(1)} collective-permute-done((bf16[24,2432]{1,0:T(8,128)(2,1)S(1)}, bf16[24,2432]{1,0:T(8,128)(2,1)S(1)}, u32[]{:S(2)}, u32[]{:S(2)}) %collective-permute-start.1) | collective-permute-done | bytes 116768 | tf_op jit(solution)/shard_map/ppermute | solution.py:670
  18.2 1.6 collective-permute-start.6
  19.8 1.5 collective-permute-start.7
  21.9 1.6 collective-permute-start.3
  23.5 1.5 collective-permute-start.4
  25.6 1.8 broadcast_in_dim.4
  27.4 3.7 %all-to-all-start = ((bf16[4,5,24,768]{3,2,1,0:T(8,128)(2,1)}), bf16[4,5,24,768]{3,2,1,0:T(8,128)(2,1)S(1)}, u32[]{:S(2)}, u32[]{:S(2)}) async-start(bf16[4,5,24,768]{3,2,1,0:T(8,128)(2,1)} %broadcast_in_dim.4), calls=%async_computation | async-start | bytes 1474560 | tf_op jit(solution)/shard_map/all_to_all | solution.py:704
  32.6 1.7 fusion.1
  34.3 1.1 reshape.211
  36.9 6.4 %collective-permute-done.5.refs_2_ = bf16[4,24,2304]{2,1,0:T(8,128)(2,1)S(1)} collective-permute-done((bf16[4,24,2304]{2,1,0:T(8,128)(2,1)S(1)}, bf16[4,24,2304]{2,1,0:T(8,128)(2,1)S(1)}, u32[]{:S(2)}, u32[]{:S(2)}) %collective-permute-start.5) | collective-permute-done | bytes 442400 | tf_op jit(solution)/shard_map/ppermute | solution.py:670
  46.7 1.3 fusion.refs_9_.turn_ref
  48.1 0.9 copy-done.1
  49.0 1.4 collective-permute-start.14
  50.4 1.3 collective-permute-start.15
  51.7 0.8 collective-permute-start.16
  52.5 1.8 broadcast_in_dim.5
  54.3 4.0 %all-to-all-start.1 = ((bf16[4,96,768]{2,1,0:T(8,128)(2,1)}), bf16[4,96,768]{2,1,0:T(8,128)(2,1)S(1)}, u32[]{:S(2)}, u32[]{:S(2)}) async-start(bf16[4,96,768]{2,1,0:T(8,128)(2,1)} %broadcast_in_dim.5), calls=%async_computation.1 | async-start | bytes 1179648 | tf_op jit(solution)/shard_map/all_to_all | solution.py:704
  58.3 22.7 %attend.1 = (bf16[1024,768]{1,0:T(8,128)(2,1)}, bf16[1024,768]{1,0:T(8,128)(2,1)}, bf16[1024,768]{1,0:T(8,128)(2,1)}, bf16[768,1024]{1,0:T(8,128)(2,1)}, bf16[76...) custom-call(s32[1,12]{1,0:T(1,128)} %lens_ref.3, s32[1]{0:T(128)S(6)} %copy.84.valid_ref, ...), custom_call_target="tpu_custom_call" | custom-call | flops 27499999232 | bytes 75000000 | tf_op jit(solution)/shard_map/attend/pallas_call | solution.py:199
  81.1 3.9 %collective-permute-done.16.refs_3_ = bf16[4,5,24,768]{3,2,1,0:T(8,128)(2,1)S(1)} collective-permute-done((bf16[4,5,24,768]{3,2,1,0:T(8,128)(2,1)}, bf16[4,5,24,768]{3,2,1,0:T(8,128)(2,1)S(1)}, u32[]{:S(2)}, u32[]{:S(2)}) %collective-permute-start.16) | collective-permute-done | bytes 737312 | tf_op jit(solution)/shard_map/ppermute | solution.py:670
  85.0 0.9 copy-done.20
  87.1 1.5 collective-permute-start.21
  88.6 1.4 collective-permute-start.22
  90.6 2.2 collective-permute-start.23
  92.8 0.8 copy-done.45
  93.7 29.1 %mlp_up.1 = (f32[1024,768]{1,0:T(8,128)}, bf16[1024,768]{1,0:T(8,128)(2,1)}, bf16[768,1024]{1,0:T(8,128)(2,1)}, bf16[768,1024]{1,0:T(8,128)(2,1)}, bf16[1024,768...) custom-call(s32[3]{0:T(128)} %pad_add_fusion.me_ref, ...), custom_call_target="tpu_custom_call" | custom-call | flops 28600000512 | bytes 78000000 | tf_op jit(solution)/shard_map/mlp_up/pallas_call | solution.py:344
  122.8 0.8 copy-done.23
  123.9 1.1 copy-done.8
  126.2 2.5 collective-permute-done.28.refs_9_
  128.7 1.6 fusion.2
  131.0 0.9 collective-permute-start.30
  131.9 1.9 collective-permute-start.31
  134.6 0.9 copy-done.49
  135.5 37.6 %mlp_down.1 = (f32[1024,768]{1,0:T(8,128)}, f32[1024,768]{1,0:T(8,128)}, bf16[1024,768]{1,0:T(8,128)(2,1)}, bf16[384,3840]{1,0:T(8,128)(2,1)}, bf16[384,3840]{1,...) custom-call(s32[3]{0:T(128)} %pad_add_fusion.me_ref, ...), custom_call_target="tpu_custom_call", output_to_operand_aliasing={{7}: (21, {})} | custom-call | flops 38499999744 | bytes 105000000 | tf_op jit(solution)/shard_map/mlp_down/pallas_call | solution.py:465
  173.1 0.8 copy-done.11
  173.9 0.8 copy-done.12
  174.8 2.1 add_convert_fusion.9
  177.0 2.9 %collective-permute-start.37 = (bf16[96,768]{1,0:T(8,128)(2,1)S(1)}, bf16[96,768]{1,0:T(8,128)(2,1)S(1)}, u32[]{:S(2)}, u32[]{:S(2)}) collective-permute-start(bf16[96,768]{1,0:T(8,128)(2,1)S(1)} %get-tuple-element.118), channel_id=1, source_target_pairs={{0,16},{8,24},{16,0},{24,8},{1,17},{9,25},{17,1},{25,9},{2,18},{10... | collective-permute-start | bytes 442376 | tf_op jit(solution)/shard_map/ppermute | solution.py:670
  180.0 1.3 collective-permute-start.38
  181.3 2.0 add_convert_fusion
  184.3 0.9 collective-permute-start.34
  185.8 1.3 collective-permute-start.35
  187.0 29.1 %attend_back.1 = (bf16[1024,768]{1,0:T(8,128)(2,1)}, bf16[1024,768]{1,0:T(8,128)(2,1)}, bf16[1024,768]{1,0:T(8,128)(2,1)}, bf16[384,2304]{1,0:T(8,128)(2,1)}, bf...) custom-call(s32[1,12]{1,0:T(1,128)} %lens_ref.3, ...), custom_call_target="tpu_custom_call", output_to_operand_aliasing={{6}: (9, {}), {7}: (10, {})} | custom-call | flops 36300001280 | bytes 99000000 | tf_op jit(solution)/shard_map/attend_back/pallas_call | solution.py:590
  216.3 2.4 collective-permute-done.35.refs_3_
  218.7 0.9 copy-done.5
  219.5 3.0 %add_convert_fusion.8 = (bf16[24,3840]{1,0:T(8,128)(2,1)}, bf16[24,3840]{1,0:T(8,128)(2,1)}, bf16[24,3840]{1,0:T(8,128)(2,1)}) fusion(bf16[96,3840]{1,0:T(8,128)(2,1)} %copy-done.5, bf16[96,3840]{1,0:T(8,128)(2,1)} %copy-done.4, bf16[96,3840]{1,0:T(8,128)(2,1)} %copy-done.3, bf16[384,3840]{1,0:T(8,128)(2,1)} %copy-done.6, ...), kind=kLoop, calls=%fused_computation.20 | loop fusion | flops 2764800 | bytes 3317760 | tf_op jit(solution)/shard_map/convert_element_type | solution.py:736
  222.6 3.1 %collective-permute-start.47 = (bf16[24,3840]{1,0:T(8,128)(2,1)}, bf16[24,3840]{1,0:T(8,128)(2,1)}, u32[]{:S(2)}, u32[]{:S(2)}) collective-permute-start(bf16[24,3840]{1,0:T(8,128)(2,1)} %get-tuple-element.116), channel_id=1, source_target_pairs={{0,16},{8,24},{16,0},{24,8},{1,17},{9,25},{17,1},{25,9},{2,18},{10... | collective-permute-start | bytes 552968 | tf_op jit(solution)/shard_map/ppermute | solution.py:670
  225.6 1.5 add_convert_fusion.5
  227.8 1.0 collective-permute-start.41
  228.8 1.9 collective-permute-start.42
  230.7 10.7 %input_back.1 = (f32[1024,768]{1,0:T(8,128)}, f32[8,768]{1,0:T(8,128)}, bf16[384,3840]{1,0:T(8,128)(2,1)}, bf16[384,2304]{1,0:T(8,128)(2,1)}, bf16[1536,768]{1,0:T(8,128)(2,1)}) custom-call(bf16[1024,768]{1,0:T(8,128)(2,1)} %get-tuple-element.91.dq_ref, ...), custom_call_target="tpu_custom_call", output_to_operand_aliasing={{2}: (7, {}), {3}: (8, {}), {4}: (9, {})} | custom-call | flops 14300000256 | bytes 39000000 | tf_op jit(solution)/shard_map/input_back/pallas_call | solution.py:650
  241.4 1.4 collective-permute-start.48
  242.8 7.1 %collective-permute-done.42 = bf16[96,2304]{1,0:T(8,128)(2,1)S(1)} collective-permute-done((bf16[96,2304]{1,0:T(8,128)(2,1)S(1)}, bf16[96,2304]{1,0:T(8,128)(2,1)S(1)}, u32[]{:S(2)}, u32[]{:S(2)}) %collective-permute-start.42) | collective-permute-done | bytes 442400 | tf_op jit(solution)/shard_map/ppermute | solution.py:670
  249.9 2.0 add_convert_fusion.14
  252.7 1.7 convert_add_fusion.3
  254.9 1.6 collective-permute-start.44
  256.5 2.5 collective-permute-start.45
  262.7 2.6 all-to-all-start.2
  265.3 1.4 convert_add_fusion.4
  268.8 3.7 %all-to-all-done.2 = bf16[32,2,192]{2,1,0:T(2,128)(2,1)S(1)} async-done(((bf16[32,2,192]{2,1,0:T(2,128)(2,1)}), bf16[32,2,192]{2,1,0:T(2,128)(2,1)S(1)}, u32[]{:S(2)}, u32[]{:S(2)}) %all-to-all-start.2) | async-done | bytes 24608 | tf_op jit(solution)/shard_map/all_to_all | solution.py:829
  273.8 1.1 convert_add_fusion.5
  (228 shorter events, 26.8 us)
Async XLA Ops:
  0.6 9.7 %copy-start.40 = (f32[18432]{0:T(1024)S(1)}, f32[18432]{0:T(1024)}, u32[]{:S(2)}) copy-start(f32[18432]{0:T(1024)} %param.14) | copy-start | bytes 221188
  3.2 9.2 %collective-permute-start.2 = (bf16[24,2432]{1,0:T(8,128)(2,1)S(1)}, bf16[24,2432]{1,0:T(8,128)(2,1)S(1)}, u32[]{:S(2)}, u32[]{:S(2)}) collective-permute-start(bf16[24,2432]{1,0:T(8,128)(2,1)S(1)} %pad_maximum_fusion.2), channel_id=1, source_target_pairs={{0,24},{8,16},{16,8},{24,0},{1,25},{9,17},{17,9},{25,1},{2,26},{10... | collective-permute-start | bytes 350216 | tf_op jit(solution)/shard_map/ppermute | solution.py:670
  8.3 9.8 %collective-permute-start.1 = (bf16[24,2432]{1,0:T(8,128)(2,1)S(1)}, bf16[24,2432]{1,0:T(8,128)(2,1)S(1)}, u32[]{:S(2)}, u32[]{:S(2)}) collective-permute-start(bf16[24,2432]{1,0:T(8,128)(2,1)S(1)} %pad_maximum_fusion.2), channel_id=1, source_target_pairs={{0,16},{8,24},{16,0},{24,8},{1,17},{9,25},{17,1},{25,9},{2,18},{10... | collective-permute-start | bytes 350216 | tf_op jit(solution)/shard_map/ppermute | solution.py:670
  8.3 9.8 %collective-permute-start = (bf16[24,2432]{1,0:T(8,128)(2,1)S(1)}, bf16[24,2432]{1,0:T(8,128)(2,1)S(1)}, u32[]{:S(2)}, u32[]{:S(2)}) collective-permute-start(bf16[24,2432]{1,0:T(8,128)(2,1)S(1)} %pad_maximum_fusion.2), channel_id=1, source_target_pairs={{0,8},{8,0},{16,24},{24,16},{1,9},{9,1},{17,25},{25,17},{2,10},{10... | collective-permute-start | bytes 350216 | tf_op jit(solution)/shard_map/ppermute | solution.py:670
  18.2 6.8 %collective-permute-start.6 = (bf16[4,24,128]{2,1,0:T(8,128)(2,1)S(1)}, bf16[4,24,128]{2,1,0:T(8,128)(2,1)S(1)}, u32[]{:S(2)}, u32[]{:S(2)}) collective-permute-start(bf16[4,24,128]{2,1,0:T(8,128)(2,1)S(1)} %pad_maximum_fusion.3), channel_id=1, source_target_pairs={{0,2},{2,0},{4,6},{6,4},{1,3},{3,1},{5,7},{7,5},{8,10},{10,8},{12,... | collective-permute-start | bytes 73736 | tf_op jit(solution)/shard_map/ppermute | solution.py:670
  19.8 11.4 %collective-permute-start.7 = (bf16[4,24,128]{2,1,0:T(8,128)(2,1)S(1)}, bf16[4,24,128]{2,1,0:T(8,128)(2,1)S(1)}, u32[]{:S(2)}, u32[]{:S(2)}) collective-permute-start(bf16[4,24,128]{2,1,0:T(8,128)(2,1)S(1)} %pad_maximum_fusion.3), channel_id=1, source_target_pairs={{0,4},{2,6},{4,0},{6,2},{1,5},{3,7},{5,1},{7,3},{8,12},{10,14},{12... | collective-permute-start | bytes 73736 | tf_op jit(solution)/shard_map/ppermute | solution.py:670
  21.3 9.9 %collective-permute-start.8 = (bf16[4,24,128]{2,1,0:T(8,128)(2,1)S(1)}, bf16[4,24,128]{2,1,0:T(8,128)(2,1)S(1)}, u32[]{:S(2)}, u32[]{:S(2)}) collective-permute-start(bf16[4,24,128]{2,1,0:T(8,128)(2,1)S(1)} %pad_maximum_fusion.3), channel_id=1, source_target_pairs={{0,6},{2,4},{4,2},{6,0},{1,7},{3,5},{5,3},{7,1},{8,14},{10,12},{12... | collective-permute-start | bytes 73736 | tf_op jit(solution)/shard_map/ppermute | solution.py:670
  21.9 12.4 %copy-start.31 = (bf16[4,24,2304]{2,1,0:T(8,128)(2,1)}, bf16[4,24,2304]{2,1,0:T(8,128)(2,1)S(1)}, u32[]{:S(2)}) copy-start(bf16[4,24,2304]{2,1,0:T(8,128)(2,1)S(1)} %pad_maximum_fusion.refs_0_) | copy-start | bytes 1327108
  21.9 15.0 %collective-permute-start.3 = (bf16[4,24,2304]{2,1,0:T(8,128)(2,1)S(1)}, bf16[4,24,2304]{2,1,0:T(8,128)(2,1)S(1)}, u32[]{:S(2)}, u32[]{:S(2)}) collective-permute-start(bf16[4,24,2304]{2,1,0:T(8,128)(2,1)S(1)} %pad_maximum_fusion.refs_0_), channel_id=1, source_target_pairs={{0,2},{2,0},{4,6},{6,4},{1,3},{3,1},{5,7},{7,5},{8,10},{10,8},{12,... | collective-permute-start | bytes 1327112 | tf_op jit(solution)/shard_map/ppermute | solution.py:670
  23.5 13.4 %collective-permute-start.4 = (bf16[4,24,2304]{2,1,0:T(8,128)(2,1)S(1)}, bf16[4,24,2304]{2,1,0:T(8,128)(2,1)S(1)}, u32[]{:S(2)}, u32[]{:S(2)}) collective-permute-start(bf16[4,24,2304]{2,1,0:T(8,128)(2,1)S(1)} %pad_maximum_fusion.refs_0_), channel_id=1, source_target_pairs={{0,4},{2,6},{4,0},{6,2},{1,5},{3,7},{5,1},{7,3},{8,12},{10,14},{12... | collective-permute-start | bytes 1327112 | tf_op jit(solution)/shard_map/ppermute | solution.py:670
  25.0 18.3 %collective-permute-start.5 = (bf16[4,24,2304]{2,1,0:T(8,128)(2,1)S(1)}, bf16[4,24,2304]{2,1,0:T(8,128)(2,1)S(1)}, u32[]{:S(2)}, u32[]{:S(2)}) collective-permute-start(bf16[4,24,2304]{2,1,0:T(8,128)(2,1)S(1)} %pad_maximum_fusion.refs_0_), channel_id=1, source_target_pairs={{0,6},{2,4},{4,2},{6,0},{1,7},{3,5},{5,3},{7,1},{8,14},{10,12},{12... | collective-permute-start | bytes 1327112 | tf_op jit(solution)/shard_map/ppermute | solution.py:670
  27.4 20.7 %all-to-all-start = ((bf16[4,5,24,768]{3,2,1,0:T(8,128)(2,1)}), bf16[4,5,24,768]{3,2,1,0:T(8,128)(2,1)S(1)}, u32[]{:S(2)}, u32[]{:S(2)}) async-start(bf16[4,5,24,768]{3,2,1,0:T(8,128)(2,1)} %broadcast_in_dim.4), calls=%async_computation | async-start | bytes 1474560 | tf_op jit(solution)/shard_map/all_to_all | solution.py:704
  31.2 1.4 collective-permute-start.9
  31.4 19.0 %collective-permute-start.10 = (bf16[4,24,2304]{2,1,0:T(8,128)(2,1)S(1)}, bf16[4,24,2304]{2,1,0:T(8,128)(2,1)S(1)}, u32[]{:S(2)}, u32[]{:S(2)}) collective-permute-start(bf16[4,24,2304]{2,1,0:T(8,128)(2,1)S(1)} %pad_maximum_fusion.refs_0_), channel_id=1, source_target_pairs={{0,1},{1,0},{2,3},{3,2},{4,5},{5,4},{6,7},{7,6},{8,9},{9,8},{10,11... | collective-permute-start | bytes 1327112 | tf_op jit(solution)/shard_map/ppermute | solution.py:666
  35.4 9.1 %copy-start.36 = (f32[73728]{0:T(1024)S(1)}, f32[73728]{0:T(1024)}, u32[]{:S(2)}) copy-start(f32[73728]{0:T(1024)} %param.17) | copy-start | bytes 884740
  36.8 6.4 %copy-start.15 = (bf16[4,24,2304]{2,1,0:T(8,128)(2,1)}, bf16[4,24,2304]{2,1,0:T(8,128)(2,1)S(1)}, u32[]{:S(2)}) copy-start(bf16[4,24,2304]{2,1,0:T(8,128)(2,1)S(1)} %collective-permute-done.3.refs_0_) | copy-start | bytes 1327108
  36.8 6.4 %copy-start.16 = (bf16[4,24,2304]{2,1,0:T(8,128)(2,1)}, bf16[4,24,2304]{2,1,0:T(8,128)(2,1)S(1)}, u32[]{:S(2)}) copy-start(bf16[4,24,2304]{2,1,0:T(8,128)(2,1)S(1)} %collective-permute-done.4.refs_1_) | copy-start | bytes 1327108
  44.1 7.7 %collective-permute-start.11 = (bf16[4,24,2304]{2,1,0:T(8,128)(2,1)}, bf16[4,24,2304]{2,1,0:T(8,128)(2,1)}, u32[]{:S(2)}, u32[]{:S(2)}) collective-permute-start(bf16[4,24,2304]{2,1,0:T(8,128)(2,1)} %get-tuple-element.61.refs_1_), channel_id=1, source_target_pairs={{0,1},{1,0},{2,3},{3,2},{4,5},{5,4},{6,7},{7,6},{8,9},{9,8},{10,11... | collective-permute-start | bytes 1327112 | tf_op jit(solution)/shard_map/ppermute | solution.py:666
  44.1 8.5 %collective-permute-start.12 = (bf16[4,24,2304]{2,1,0:T(8,128)(2,1)}, bf16[4,24,2304]{2,1,0:T(8,128)(2,1)}, u32[]{:S(2)}, u32[]{:S(2)}) collective-permute-start(bf16[4,24,2304]{2,1,0:T(8,128)(2,1)} %get-tuple-element.62.refs_2_), channel_id=1, source_target_pairs={{0,1},{1,0},{2,3},{3,2},{4,5},{5,4},{6,7},{7,6},{8,9},{9,8},{10,11... | collective-permute-start | bytes 1327112 | tf_op jit(solution)/shard_map/ppermute | solution.py:666
  44.6 8.0 %collective-permute-start.13 = (bf16[4,24,2304]{2,1,0:T(8,128)(2,1)}, bf16[4,24,2304]{2,1,0:T(8,128)(2,1)}, u32[]{:S(2)}, u32[]{:S(2)}) collective-permute-start(bf16[4,24,2304]{2,1,0:T(8,128)(2,1)} %get-tuple-element.63.refs_3_), channel_id=1, source_target_pairs={{0,1},{1,0},{2,3},{3,2},{4,5},{5,4},{6,7},{7,6},{8,9},{9,8},{10,11... | collective-permute-start | bytes 1327112 | tf_op jit(solution)/shard_map/ppermute | solution.py:666
  49.0 32.0 %collective-permute-start.14 = (bf16[4,5,24,768]{3,2,1,0:T(8,128)(2,1)}, bf16[4,5,24,768]{3,2,1,0:T(8,128)(2,1)S(1)}, u32[]{:S(2)}, u32[]{:S(2)}) collective-permute-start(bf16[4,5,24,768]{3,2,1,0:T(8,128)(2,1)} %gate.11.refs_5_.refs_0_), channel_id=1, source_target_pairs={{0,2},{2,0},{4,6},{6,4},{1,3},{3,1},{5,7},{7,5},{8,10},{10,8},{12,... | collective-permute-start | bytes 2211848 | tf_op jit(solution)/shard_map/ppermute | solution.py:670
  50.4 30.7 %collective-permute-start.15 = (bf16[4,5,24,768]{3,2,1,0:T(8,128)(2,1)}, bf16[4,5,24,768]{3,2,1,0:T(8,128)(2,1)S(1)}, u32[]{:S(2)}, u32[]{:S(2)}) collective-permute-start(bf16[4,5,24,768]{3,2,1,0:T(8,128)(2,1)} %gate.11.refs_5_.refs_0_), channel_id=1, source_target_pairs={{0,4},{2,6},{4,0},{6,2},{1,5},{3,7},{5,1},{7,3},{8,12},{10,14},{12... | collective-permute-start | bytes 2211848 | tf_op jit(solution)/shard_map/ppermute | solution.py:670
  51.7 33.3 %collective-permute-start.16 = (bf16[4,5,24,768]{3,2,1,0:T(8,128)(2,1)}, bf16[4,5,24,768]{3,2,1,0:T(8,128)(2,1)S(1)}, u32[]{:S(2)}, u32[]{:S(2)}) collective-permute-start(bf16[4,5,24,768]{3,2,1,0:T(8,128)(2,1)} %gate.11.refs_5_.refs_0_), channel_id=1, source_target_pairs={{0,6},{2,4},{4,2},{6,0},{1,7},{3,5},{5,3},{7,1},{8,14},{10,12},{12... | collective-permute-start | bytes 2211848 | tf_op jit(solution)/shard_map/ppermute | solution.py:670
  54.3 30.7 %all-to-all-start.1 = ((bf16[4,96,768]{2,1,0:T(8,128)(2,1)}), bf16[4,96,768]{2,1,0:T(8,128)(2,1)S(1)}, u32[]{:S(2)}, u32[]{:S(2)}) async-start(bf16[4,96,768]{2,1,0:T(8,128)(2,1)} %broadcast_in_dim.5), calls=%async_computation.1 | async-start | bytes 1179648 | tf_op jit(solution)/shard_map/all_to_all | solution.py:704
  86.1 2.5 collective-permute-start.17
  86.1 4.5 %collective-permute-start.18 = (bf16[4,5,24,768]{3,2,1,0:T(8,128)(2,1)}, bf16[4,5,24,768]{3,2,1,0:T(8,128)(2,1)S(1)}, u32[]{:S(2)}, u32[]{:S(2)}) collective-permute-start(bf16[4,5,24,768]{3,2,1,0:T(8,128)(2,1)} %get-tuple-element.66.refs_1_), channel_id=1, source_target_pairs={{0,1},{1,0},{2,3},{3,2},{4,5},{5,4},{6,7},{7,6},{8,9},{9,8},{10,11... | collective-permute-start | bytes 2211848 | tf_op jit(solution)/shard_map/ppermute | solution.py:666
  86.6 6.2 %collective-permute-start.19 = (bf16[4,5,24,768]{3,2,1,0:T(8,128)(2,1)}, bf16[4,5,24,768]{3,2,1,0:T(8,128)(2,1)S(1)}, u32[]{:S(2)}, u32[]{:S(2)}) collective-permute-start(bf16[4,5,24,768]{3,2,1,0:T(8,128)(2,1)} %get-tuple-element.67.refs_2_), channel_id=1, source_target_pairs={{0,1},{1,0},{2,3},{3,2},{4,5},{5,4},{6,7},{7,6},{8,9},{9,8},{10,11... | collective-permute-start | bytes 2211848 | tf_op jit(solution)/shard_map/ppermute | solution.py:666
  86.6 6.2 %collective-permute-start.20 = (bf16[4,5,24,768]{3,2,1,0:T(8,128)(2,1)}, bf16[4,5,24,768]{3,2,1,0:T(8,128)(2,1)}, u32[]{:S(2)}, u32[]{:S(2)}) collective-permute-start(bf16[4,5,24,768]{3,2,1,0:T(8,128)(2,1)} %get-tuple-element.68.refs_3_), channel_id=1, source_target_pairs={{0,1},{1,0},{2,3},{3,2},{4,5},{5,4},{6,7},{7,6},{8,9},{9,8},{10,11... | collective-permute-start | bytes 2211848 | tf_op jit(solution)/shard_map/ppermute | solution.py:666
  87.1 35.7 %collective-permute-start.21 = (bf16[4,96,768]{2,1,0:T(8,128)(2,1)}, bf16[4,96,768]{2,1,0:T(8,128)(2,1)S(1)}, u32[]{:S(2)}, u32[]{:S(2)}) collective-permute-start(bf16[4,96,768]{2,1,0:T(8,128)(2,1)} %get-tuple-element.78.refs_0_), channel_id=1, source_target_pairs={{0,2},{2,0},{4,6},{6,4},{1,3},{3,1},{5,7},{7,5},{8,10},{10,8},{12,... | collective-permute-start | bytes 1769480 | tf_op jit(solution)/shard_map/ppermute | solution.py:670
  88.6 34.2 %collective-permute-start.22 = (bf16[4,96,768]{2,1,0:T(8,128)(2,1)}, bf16[4,96,768]{2,1,0:T(8,128)(2,1)S(1)}, u32[]{:S(2)}, u32[]{:S(2)}) collective-permute-start(bf16[4,96,768]{2,1,0:T(8,128)(2,1)} %get-tuple-element.78.refs_0_), channel_id=1, source_target_pairs={{0,4},{2,6},{4,0},{6,2},{1,5},{3,7},{5,1},{7,3},{8,12},{10,14},{12... | collective-permute-start | bytes 1769480 | tf_op jit(solution)/shard_map/ppermute | solution.py:670
  90.6 32.2 %collective-permute-start.23 = (bf16[4,96,768]{2,1,0:T(8,128)(2,1)}, bf16[4,96,768]{2,1,0:T(8,128)(2,1)S(1)}, u32[]{:S(2)}, u32[]{:S(2)}) collective-permute-start(bf16[4,96,768]{2,1,0:T(8,128)(2,1)} %get-tuple-element.78.refs_0_), channel_id=1, source_target_pairs={{0,6},{2,4},{4,2},{6,0},{1,7},{3,5},{5,3},{7,1},{8,14},{10,12},{12... | collective-permute-start | bytes 1769480 | tf_op jit(solution)/shard_map/ppermute | solution.py:670
  123.9 4.7 %collective-permute-start.28 = (bf16[1536,768]{1,0:T(8,128)(2,1)}, bf16[1536,768]{1,0:T(8,128)(2,1)S(1)}, u32[]{:S(2)}, u32[]{:S(2)}) collective-permute-start(bf16[1536,768]{1,0:T(8,128)(2,1)} %gate.14), channel_id=1, source_target_pairs={{0,1},{1,0},{2,3},{3,2},{4,5},{5,4},{6,7},{7,6},{8,9},{9,8},{10,11... | collective-permute-start | bytes 7077896 | tf_op jit(solution)/shard_map/ppermute | solution.py:666
  125.0 6.0 %collective-permute-start.24 = (bf16[4,96,768]{2,1,0:T(8,128)(2,1)S(1)}, bf16[4,96,768]{2,1,0:T(8,128)(2,1)S(1)}, u32[]{:S(2)}, u32[]{:S(2)}) collective-permute-start(bf16[4,96,768]{2,1,0:T(8,128)(2,1)S(1)} %copy-done.8), channel_id=1, source_target_pairs={{0,1},{1,0},{2,3},{3,2},{4,5},{5,4},{6,7},{7,6},{8,9},{9,8},{10,11... | collective-permute-start | bytes 1769480 | tf_op jit(solution)/shard_map/ppermute | solution.py:666
  125.0 6.9 %collective-permute-start.25 = (bf16[4,96,768]{2,1,0:T(8,128)(2,1)}, bf16[4,96,768]{2,1,0:T(8,128)(2,1)S(1)}, u32[]{:S(2)}, u32[]{:S(2)}) collective-permute-start(bf16[4,96,768]{2,1,0:T(8,128)(2,1)} %copy-done.22), channel_id=1, source_target_pairs={{0,1},{1,0},{2,3},{3,2},{4,5},{5,4},{6,7},{7,6},{8,9},{9,8},{10,11... | collective-permute-start | bytes 1769480 | tf_op jit(solution)/shard_map/ppermute | solution.py:666
  125.5 8.3 %collective-permute-start.26 = (bf16[4,96,768]{2,1,0:T(8,128)(2,1)}, bf16[4,96,768]{2,1,0:T(8,128)(2,1)S(1)}, u32[]{:S(2)}, u32[]{:S(2)}) collective-permute-start(bf16[4,96,768]{2,1,0:T(8,128)(2,1)} %copy-done.23), channel_id=1, source_target_pairs={{0,1},{1,0},{2,3},{3,2},{4,5},{5,4},{6,7},{7,6},{8,9},{9,8},{10,11... | collective-permute-start | bytes 1769480 | tf_op jit(solution)/shard_map/ppermute | solution.py:666
  125.5 8.3 %collective-permute-start.27 = (bf16[4,96,768]{2,1,0:T(8,128)(2,1)}, bf16[4,96,768]{2,1,0:T(8,128)(2,1)S(1)}, u32[]{:S(2)}, u32[]{:S(2)}) collective-permute-start(bf16[4,96,768]{2,1,0:T(8,128)(2,1)} %copy-done.24), channel_id=1, source_target_pairs={{0,1},{1,0},{2,3},{3,2},{4,5},{5,4},{6,7},{7,6},{8,9},{9,8},{10,11... | collective-permute-start | bytes 1769480 | tf_op jit(solution)/shard_map/ppermute | solution.py:666
  130.3 42.8 %collective-permute-start.29 = (bf16[384,768]{1,0:T(8,128)(2,1)}, bf16[384,768]{1,0:T(8,128)(2,1)S(1)}, u32[]{:S(2)}, u32[]{:S(2)}) collective-permute-start(bf16[384,768]{1,0:T(8,128)(2,1)} %get-tuple-element.131), channel_id=1, source_target_pairs={{0,2},{2,0},{4,6},{6,4},{1,3},{3,1},{5,7},{7,5},{8,10},{10,8},{12,... | collective-permute-start | bytes 1769480 | tf_op jit(solution)/shard_map/ppermute | solution.py:670
  131.0 42.0 %collective-permute-start.30 = (bf16[384,768]{1,0:T(8,128)(2,1)S(1)}, bf16[384,768]{1,0:T(8,128)(2,1)S(1)}, u32[]{:S(2)}, u32[]{:S(2)}) collective-permute-start(bf16[384,768]{1,0:T(8,128)(2,1)S(1)} %get-tuple-element.130), channel_id=1, source_target_pairs={{0,4},{2,6},{4,0},{6,2},{1,5},{3,7},{5,1},{7,3},{8,12},{10,14},{12... | collective-permute-start | bytes 1769480 | tf_op jit(solution)/shard_map/ppermute | solution.py:670
  131.9 41.2 %collective-permute-start.31 = (bf16[384,768]{1,0:T(8,128)(2,1)S(1)}, bf16[384,768]{1,0:T(8,128)(2,1)S(1)}, u32[]{:S(2)}, u32[]{:S(2)}) collective-permute-start(bf16[384,768]{1,0:T(8,128)(2,1)S(1)} %get-tuple-element.129), channel_id=1, source_target_pairs={{0,6},{2,4},{4,2},{6,0},{1,7},{3,5},{5,3},{7,1},{8,14},{10,12},{12... | collective-permute-start | bytes 1769480 | tf_op jit(solution)/shard_map/ppermute | solution.py:670
  174.8 6.6 %copy-start = (bf16[384,3840]{1,0:T(8,128)(2,1)S(1)}, bf16[384,3840]{1,0:T(8,128)(2,1)}, u32[]{:S(2)}) copy-start(bf16[384,3840]{1,0:T(8,128)(2,1)} %get-tuple-element.88.refs_0_) | copy-start | bytes 8847364
  174.8 6.5 %collective-permute-start.32 = (bf16[384,3840]{1,0:T(8,128)(2,1)}, bf16[384,3840]{1,0:T(8,128)(2,1)S(1)}, u32[]{:S(2)}, u32[]{:S(2)}) collective-permute-start(bf16[384,3840]{1,0:T(8,128)(2,1)} %gate.15), channel_id=1, source_target_pairs={{0,1},{1,0},{2,3},{3,2},{4,5},{5,4},{6,7},{7,6},{8,9},{9,8},{10,11... | collective-permute-start | bytes 8847368 | tf_op jit(solution)/shard_map/ppermute | solution.py:666
  176.8 8.9 %collective-permute-start.36 = (bf16[96,768]{1,0:T(8,128)(2,1)S(1)}, bf16[96,768]{1,0:T(8,128)(2,1)S(1)}, u32[]{:S(2)}, u32[]{:S(2)}) collective-permute-start(bf16[96,768]{1,0:T(8,128)(2,1)S(1)} %get-tuple-element.119), channel_id=1, source_target_pairs={{0,8},{8,0},{16,24},{24,16},{1,9},{9,1},{17,25},{25,17},{2,10},{10... | collective-permute-start | bytes 442376 | tf_op jit(solution)/shard_map/ppermute | solution.py:670
  177.0 39.2 %collective-permute-start.37 = (bf16[96,768]{1,0:T(8,128)(2,1)S(1)}, bf16[96,768]{1,0:T(8,128)(2,1)S(1)}, u32[]{:S(2)}, u32[]{:S(2)}) collective-permute-start(bf16[96,768]{1,0:T(8,128)(2,1)S(1)} %get-tuple-element.118), channel_id=1, source_target_pairs={{0,16},{8,24},{16,0},{24,8},{1,17},{9,25},{17,1},{25,9},{2,18},{10... | collective-permute-start | bytes 442376 | tf_op jit(solution)/shard_map/ppermute | solution.py:670
  180.0 36.3 %collective-permute-start.38 = (bf16[96,768]{1,0:T(8,128)(2,1)S(1)}, bf16[96,768]{1,0:T(8,128)(2,1)S(1)}, u32[]{:S(2)}, u32[]{:S(2)}) collective-permute-start(bf16[96,768]{1,0:T(8,128)(2,1)S(1)} %get-tuple-element.117), channel_id=1, source_target_pairs={{0,24},{8,16},{16,8},{24,0},{1,25},{9,17},{17,9},{25,1},{2,26},{10... | collective-permute-start | bytes 442376 | tf_op jit(solution)/shard_map/ppermute | solution.py:670
  183.6 32.7 %collective-permute-start.33 = (bf16[96,3840]{1,0:T(8,128)(2,1)}, bf16[96,3840]{1,0:T(8,128)(2,1)S(1)}, u32[]{:S(2)}, u32[]{:S(2)}) collective-permute-start(bf16[96,3840]{1,0:T(8,128)(2,1)} %get-tuple-element.122), channel_id=1, source_target_pairs={{0,2},{2,0},{4,6},{6,4},{1,3},{3,1},{5,7},{7,5},{8,10},{10,8},{12,... | collective-permute-start | bytes 2211848 | tf_op jit(solution)/shard_map/ppermute | solution.py:670
  184.3 31.9 %collective-permute-start.34 = (bf16[96,3840]{1,0:T(8,128)(2,1)}, bf16[96,3840]{1,0:T(8,128)(2,1)S(1)}, u32[]{:S(2)}, u32[]{:S(2)}) collective-permute-start(bf16[96,3840]{1,0:T(8,128)(2,1)} %get-tuple-element.121), channel_id=1, source_target_pairs={{0,4},{2,6},{4,0},{6,2},{1,5},{3,7},{5,1},{7,3},{8,12},{10,14},{12... | collective-permute-start | bytes 2211848 | tf_op jit(solution)/shard_map/ppermute | solution.py:670
  185.8 30.4 %copy-start.25 = (bf16[96,768]{1,0:T(8,128)(2,1)}, bf16[96,768]{1,0:T(8,128)(2,1)S(1)}, u32[]{:S(2)}) copy-start(bf16[96,768]{1,0:T(8,128)(2,1)S(1)} %collective-permute-done.36.refs_4_) | copy-start | bytes 442372
  185.8 32.9 %collective-permute-start.35 = (bf16[96,3840]{1,0:T(8,128)(2,1)}, bf16[96,3840]{1,0:T(8,128)(2,1)S(1)}, u32[]{:S(2)}, u32[]{:S(2)}) collective-permute-start(bf16[96,3840]{1,0:T(8,128)(2,1)} %get-tuple-element.120), channel_id=1, source_target_pairs={{0,6},{2,4},{4,2},{6,0},{1,7},{3,5},{5,3},{7,1},{8,14},{10,12},{12... | collective-permute-start | bytes 2211848 | tf_op jit(solution)/shard_map/ppermute | solution.py:670
  219.5 6.1 %collective-permute-start.39 = (bf16[384,2304]{1,0:T(8,128)(2,1)}, bf16[384,2304]{1,0:T(8,128)(2,1)S(1)}, u32[]{:S(2)}, u32[]{:S(2)}) collective-permute-start(bf16[384,2304]{1,0:T(8,128)(2,1)} %gate.16), channel_id=1, source_target_pairs={{0,1},{1,0},{2,3},{3,2},{4,5},{5,4},{6,7},{7,6},{8,9},{9,8},{10,11... | collective-permute-start | bytes 5308424 | tf_op jit(solution)/shard_map/ppermute | solution.py:666
  222.5 29.4 %collective-permute-start.46 = (bf16[24,3840]{1,0:T(8,128)(2,1)}, bf16[24,3840]{1,0:T(8,128)(2,1)}, u32[]{:S(2)}, u32[]{:S(2)}) collective-permute-start(bf16[24,3840]{1,0:T(8,128)(2,1)} %get-tuple-element.114), channel_id=1, source_target_pairs={{0,8},{8,0},{16,24},{24,16},{1,9},{9,1},{17,25},{25,17},{2,10},{10... | collective-permute-start | bytes 552968 | tf_op jit(solution)/shard_map/ppermute | solution.py:670
  222.6 29.4 %collective-permute-start.47 = (bf16[24,3840]{1,0:T(8,128)(2,1)}, bf16[24,3840]{1,0:T(8,128)(2,1)}, u32[]{:S(2)}, u32[]{:S(2)}) collective-permute-start(bf16[24,3840]{1,0:T(8,128)(2,1)} %get-tuple-element.116), channel_id=1, source_target_pairs={{0,16},{8,24},{16,0},{24,8},{1,17},{9,25},{17,1},{25,9},{2,18},{10... | collective-permute-start | bytes 552968 | tf_op jit(solution)/shard_map/ppermute | solution.py:670
  227.2 14.2 %collective-permute-start.40 = (bf16[96,2304]{1,0:T(8,128)(2,1)}, bf16[96,2304]{1,0:T(8,128)(2,1)S(1)}, u32[]{:S(2)}, u32[]{:S(2)}) collective-permute-start(bf16[96,2304]{1,0:T(8,128)(2,1)} %get-tuple-element.126), channel_id=1, source_target_pairs={{0,2},{2,0},{4,6},{6,4},{1,3},{3,1},{5,7},{7,5},{8,10},{10,8},{12,... | collective-permute-start | bytes 1327112 | tf_op jit(solution)/shard_map/ppermute | solution.py:670
  227.8 15.0 %collective-permute-start.41 = (bf16[96,2304]{1,0:T(8,128)(2,1)}, bf16[96,2304]{1,0:T(8,128)(2,1)S(1)}, u32[]{:S(2)}, u32[]{:S(2)}) collective-permute-start(bf16[96,2304]{1,0:T(8,128)(2,1)} %get-tuple-element.128), channel_id=1, source_target_pairs={{0,4},{2,6},{4,0},{6,2},{1,5},{3,7},{5,1},{7,3},{8,12},{10,14},{12... | collective-permute-start | bytes 1327112 | tf_op jit(solution)/shard_map/ppermute | solution.py:670
  228.8 21.1 %collective-permute-start.42 = (bf16[96,2304]{1,0:T(8,128)(2,1)S(1)}, bf16[96,2304]{1,0:T(8,128)(2,1)S(1)}, u32[]{:S(2)}, u32[]{:S(2)}) collective-permute-start(bf16[96,2304]{1,0:T(8,128)(2,1)S(1)} %get-tuple-element.127), channel_id=1, source_target_pairs={{0,6},{2,4},{4,2},{6,0},{1,7},{3,5},{5,3},{7,1},{8,14},{10,12},{12... | collective-permute-start | bytes 1327112 | tf_op jit(solution)/shard_map/ppermute | solution.py:670
  230.7 10.7 %copy-start.37 = (bf16[24,3840]{1,0:T(8,128)(2,1)S(1)}, bf16[24,3840]{1,0:T(8,128)(2,1)}, u32[]{:S(2)}) copy-start(bf16[24,3840]{1,0:T(8,128)(2,1)} %get-tuple-element.115) | copy-start | bytes 552964
  241.4 10.6 %collective-permute-start.48 = (bf16[24,3840]{1,0:T(8,128)(2,1)S(1)}, bf16[24,3840]{1,0:T(8,128)(2,1)S(1)}, u32[]{:S(2)}, u32[]{:S(2)}) collective-permute-start(bf16[24,3840]{1,0:T(8,128)(2,1)S(1)} %copy-done.37), channel_id=1, source_target_pairs={{0,24},{8,16},{16,8},{24,0},{1,25},{9,17},{17,9},{25,1},{2,26},{10... | collective-permute-start | bytes 552968 | tf_op jit(solution)/shard_map/ppermute | solution.py:670
  252.7 7.8 %copy-start.42 = (f32[1,3072]{1,0:T(1,128)S(1)}, f32[1,3072]{1,0:T(1,128)}, u32[]{:S(2)}) copy-start(f32[1,3072]{1,0:T(1,128)} %get-tuple-element.112) | copy-start | bytes 36868
  252.7 12.5 %copy-start.26 = (bf16[96,768]{1,0:T(8,128)(2,1)S(1)}, bf16[96,768]{1,0:T(8,128)(2,1)}, u32[]{:S(2)}) copy-start(bf16[96,768]{1,0:T(8,128)(2,1)} %copy-done.25) | copy-start | bytes 442372
  252.7 12.5 %copy-start.28 = (bf16[96,768]{1,0:T(8,128)(2,1)S(1)}, bf16[96,768]{1,0:T(8,128)(2,1)}, u32[]{:S(2)}) copy-start(bf16[96,768]{1,0:T(8,128)(2,1)} %copy-done.27) | copy-start | bytes 442372
  252.7 12.5 %copy-start.30 = (bf16[96,768]{1,0:T(8,128)(2,1)S(1)}, bf16[96,768]{1,0:T(8,128)(2,1)}, u32[]{:S(2)}) copy-start(bf16[96,768]{1,0:T(8,128)(2,1)} %copy-done.29) | copy-start | bytes 442372
  254.5 19.4 %collective-permute-start.43 = (bf16[24,2304]{1,0:T(8,128)(2,1)S(1)}, bf16[24,2304]{1,0:T(8,128)(2,1)S(1)}, u32[]{:S(2)}, u32[]{:S(2)}) collective-permute-start(bf16[24,2304]{1,0:T(8,128)(2,1)S(1)} %copy-done.35), channel_id=1, source_target_pairs={{0,8},{8,0},{16,24},{24,16},{1,9},{9,1},{17,25},{25,17},{2,10},{10... | collective-permute-start | bytes 331784 | tf_op jit(solution)/shard_map/ppermute | solution.py:670
  254.9 18.9 %collective-permute-start.44 = (bf16[24,2304]{1,0:T(8,128)(2,1)S(1)}, bf16[24,2304]{1,0:T(8,128)(2,1)S(1)}, u32[]{:S(2)}, u32[]{:S(2)}) collective-permute-start(bf16[24,2304]{1,0:T(8,128)(2,1)S(1)} %copy-done.34), channel_id=1, source_target_pairs={{0,16},{8,24},{16,0},{24,8},{1,17},{9,25},{17,1},{25,9},{2,18},{10... | collective-permute-start | bytes 331784 | tf_op jit(solution)/shard_map/ppermute | solution.py:670
  256.5 17.4 %collective-permute-start.45 = (bf16[24,2304]{1,0:T(8,128)(2,1)S(1)}, bf16[24,2304]{1,0:T(8,128)(2,1)S(1)}, u32[]{:S(2)}, u32[]{:S(2)}) collective-permute-start(bf16[24,2304]{1,0:T(8,128)(2,1)S(1)} %copy-done.33), channel_id=1, source_target_pairs={{0,24},{8,16},{16,8},{24,0},{1,25},{9,17},{17,9},{25,1},{2,26},{10... | collective-permute-start | bytes 331784 | tf_op jit(solution)/shard_map/ppermute | solution.py:670
  262.7 9.8 %all-to-all-start.2 = ((bf16[32,2,192]{2,1,0:T(2,128)(2,1)}), bf16[32,2,192]{2,1,0:T(2,128)(2,1)S(1)}, u32[]{:S(2)}, u32[]{:S(2)}) async-start(bf16[32,2,192]{2,1,0:T(2,128)(2,1)} %reshape.227), calls=%async_computation.2 | async-start | bytes 65536 | tf_op jit(solution)/shard_map/all_to_all | solution.py:829
  (38 other events, 79.7 us)
